TPU v7x, 512 devices: a whole 4x8x8 slice. The times are simulated.
512 devices in a mesh: mem: 8 (over y_hi, x), lon: 64 (over z, y_lo, core).
Axes of the slice: x: 4, y: 8 (y_hi: 2, y_lo: 4; y = y_hi * 4 + y_lo), z: 8, core: 2. Of those that a mesh axis runs over, the one named last changes fastest.
Arguments:
- control: bfloat16 [16, 64, 512, 512], P('mem', None, 'lon'), may hold values from -6 to 6
- perturb: bfloat16 [16, 64, 512, 512], P('mem', None, 'lon'), may hold values from -1.5 to 1.5
- member_group: int32 [16], P('mem'), may hold values from 0 to 3, as said below
- group_weight: float32 [4], replicated, may hold values from 0.25 to 4
- step_counts: int32 [64], replicated, may hold values from 1 to 4, as said below
- lat_inverse: bfloat16 [512, 512], replicated, may hold values from -0.25 to 0.25
- vert_inverse: float32 [64, 64], replicated, may hold values from -0.75 to 0.75
- innovation: bfloat16 [64, 512, 512], P(None, 'lon'), may hold values from -6 to 6
- precision: bfloat16 [64, 512, 512], P(None, 'lon'), may hold values from 2 to 20
Outputs:
- gradient: bfloat16 [16, 64, 512, 512], P('mem', None, 'lon')
Inputs may be any that keep to these rules, and one draw needn't show every extreme that they name: `step_counts`: some level takes 4 steps and some level takes 1. `member_group`: some member belongs to group 0 and some member to group 4 - 1.
All inputs are finite; a program needn't handle non-finite values.
Results may differ from a plain program's by a relative error of at most 0.013.
Values may be sent and summed in bfloat16 or wider, within the bound.
No kernel may reach another device: no remote copies, remote signals or barrier semaphores. Data moves between devices by JAX's collectives and lax.ppermute only.
A program may use at most 64 MiB of HBM per device.

v0:
```python
import jax
import jax.numpy as jnp
from jax import lax
from jax.sharding import PartitionSpec as P

KMAX = 4


diffusion_number = 0.5


def with_halo(array, sides, width):
    for axis, dim in sides:
        devices, length = (lax.axis_size(axis), array.shape[dim])
        up = [(i, (i + 1) % devices) for i in range(devices)]
        down = [(j, i) for i, j in up]
        last = lax.slice_in_dim(array, length - width, length, axis=dim)
        leading = lax.slice_in_dim(array, 0, width, axis=dim)
        before = lax.ppermute(last, axis, up)
        after = lax.ppermute(leading, axis, down)
        array = jnp.concatenate([before, array, after], axis=dim)
    return array


def diffuse(values, step_counts):
    for sweep in range(KMAX):
        active = (step_counts > sweep)[None, :, None, None]
        padded = with_halo(values, (("lon", 2),), 1)
        second = padded[:, :, :-2] + padded[:, :, 2:] - 2.0 * values
        values = values + jnp.where(active, diffusion_number * second, jnp.float32(0.0))
    return values


def shards(
    control,
    perturb,
    member_group,
    group_weight,
    step_counts,
    lat_inverse,
    vert_inverse,
    innovation,
    precision,
):
    groups_iota = jnp.arange(group_weight.shape[0], dtype=jnp.int32)
    matches = member_group[:, None] == groups_iota[None, :]
    member_weight = jnp.sum(jnp.where(matches, group_weight[None, :], jnp.float32(0.0)), axis=1)
    weight_cells = member_weight[:, None, None, None]
    spread = diffuse(control.astype(jnp.float32), step_counts).astype(jnp.bfloat16)
    latmix = jnp.dot(spread, lat_inverse, preferred_element_type=jnp.float32)
    local_part = jnp.einsum("kl,mlxy->mkxy", vert_inverse, latmix, precision=lax.Precision.HIGHEST)
    partial_sum = jnp.sum(weight_cells * perturb.astype(jnp.float32) * local_part, axis=0)
    summed = lax.psum(partial_sum, "mem")
    misfit = (precision.astype(jnp.float32) * (summed - innovation.astype(jnp.float32))).astype(
        jnp.bfloat16
    )
    adjoint = weight_cells * perturb.astype(jnp.float32) * misfit.astype(jnp.float32)[None]
    vertback = jnp.einsum(
        "kl,mkxy->mlxy", vert_inverse, adjoint, precision=lax.Precision.HIGHEST
    ).astype(jnp.bfloat16)
    latback = lax.dot_general(
        vertback, lat_inverse, (((3,), (1,)), ((), ())), preferred_element_type=jnp.float32
    )
    return (control.astype(jnp.float32) + diffuse(latback, step_counts)).astype(jnp.bfloat16)


def solution(mesh):
    return jax.shard_map(
        shards,
        mesh=mesh,
        in_specs=(
            P("mem", None, "lon", None),
            P("mem", None, "lon", None),
            P("mem"),
            P(),
            P(),
            P(),
            P(),
            P(None, "lon", None),
            P(None, "lon", None),
        ),
        out_specs=P("mem", None, "lon", None),
        check_vma=False,
    )
```

profile of v0, /device:TPU:217, one launch (start us, length us, event | category | flops | bytes accessed | tf_op | source)
XLA Modules:
  0.0 273.1 jit_solution(9440211486016695168)
XLA Ops:
  6.5 2.2 fusion.72
  8.7 5.4 %collective-permute-start = (f32[2,64,1,512]{3,2,1,0:T(1,128)S(1)}, f32[2,64,1,512]{3,2,1,0:T(1,128)S(1)}, u32[]{:S(2)}, u32[]{:S(2)}) collective-permute-start(f32[2,64,1,512]{3,2,1,0:T(1,128)S(1)} %get-tuple-element.19), channel_id=1, source_target_pairs={{0,1},{1,2},{2,3},{3,4},{4,5},{5,6},{6,7},{7,8},{8,9},{9,10},{10,1... | collective-permute-start | bytes 786440 | tf_op jit(solution)/shard_map/ppermute | solution.py:19
  19.4 6.4 %collective-permute-done.1 = f32[2,64,1,512]{3,2,1,0:T(1,128)S(1)} collective-permute-done((f32[2,64,1,512]{3,2,1,0:T(1,128)S(1)}, f32[2,64,1,512]{3,2,1,0:T(1,128)S(1)}, u32[]{:S(2)}, u32[]{:S(2)}) %collective-permute-start.1) | collective-permute-done | bytes 262176 | tf_op jit(solution)/shard_map/ppermute | solution.py:20
  29.2 2.4 collective-permute-start.3
  32.5 8.3 %collective-permute-done.3 = f32[2,64,1,512]{3,2,1,0:T(1,128)S(1)} collective-permute-done((f32[2,64,1,512]{3,2,1,0:T(1,128)S(1)}, f32[2,64,1,512]{3,2,1,0:T(1,128)S(1)}, u32[]{:S(2)}, u32[]{:S(2)}) %collective-permute-start.3) | collective-permute-done | bytes 262176 | tf_op jit(solution)/shard_map/ppermute | solution.py:20
  44.2 2.4 collective-permute-start.5
  47.5 8.3 %collective-permute-done.5 = f32[2,64,1,512]{3,2,1,0:T(1,128)S(1)} collective-permute-done((f32[2,64,1,512]{3,2,1,0:T(1,128)S(1)}, f32[2,64,1,512]{3,2,1,0:T(1,128)S(1)}, u32[]{:S(2)}, u32[]{:S(2)}) %collective-permute-start.5) | collective-permute-done | bytes 262176 | tf_op jit(solution)/shard_map/ppermute | solution.py:20
  59.2 2.6 collective-permute-start.7
  62.6 8.3 %collective-permute-done.7 = f32[2,64,1,512]{3,2,1,0:T(1,128)S(1)} collective-permute-done((f32[2,64,1,512]{3,2,1,0:T(1,128)S(1)}, f32[2,64,1,512]{3,2,1,0:T(1,128)S(1)}, u32[]{:S(2)}, u32[]{:S(2)}) %collective-permute-start.7) | collective-permute-done | bytes 262176 | tf_op jit(solution)/shard_map/ppermute | solution.py:20
  72.2 3.3 %fusion.46 = f32[2,8,512,64]{2,3,1,0:T(8,128)S(1)} fusion(f32[2,64,8,512]{3,2,1,0:T(8,128)S(1)} %fusion.52, f32[64,64]{1,0:T(8,128)S(1)} %copy-done.5), kind=kOutput, calls=%fused_computation.64 | convolution fusion | flops 402653184 | bytes 4210688 | tf_op jit(solution)/shard_map/kl,mlxy->mkxy/dot_general | solution.py:51
  75.5 2.3 fusion.43
  77.9 110.1 %all-reduce.2.cloned.1.call-done = f32[64,8,512]{2,1,0:T(8,128)} async-done(((f32[64,8,512]{2,1,0:T(8,128)}), f32[64,8,512]{2,1,0:T(8,128)}) %all-reduce.2.cloned.1.call-update) | async-done | bytes 1048592 | tf_op jit(solution)/shard_map/psum | solution.py:53
  189.9 3.3 %fusion.44 = bf16[2,8,512,64]{2,3,1,0:T(8,128)(2,1)S(1)} fusion(f32[2,64,8,512]{3,2,1,0:T(8,128)S(1)} %fusion.48, f32[64,64]{1,0:T(8,128)S(1)} %copy-done.5), kind=kOutput, calls=%fused_computation.62 | convolution fusion | flops 402653184 | bytes 3162112 | tf_op jit(solution)/shard_map/kl,mkxy->mlxy/dot_general | solution.py:58
  194.3 12.9 %collective-permute-start.8 = (f32[2,64,1,512]{3,2,1,0:T(1,128)S(1)}, f32[2,64,1,512]{3,2,1,0:T(1,128)S(1)}, u32[]{:S(2)}, u32[]{:S(2)}) collective-permute-start(f32[2,64,1,512]{3,2,1,0:T(1,128)S(1)} %get-tuple-element.11), channel_id=1, source_target_pairs={{0,1},{1,2},{2,3},{3,4},{4,5},{5,6},{6,7},{7,8},{8,9},{9,10},{10,1... | collective-permute-start | bytes 786440 | tf_op jit(solution)/shard_map/ppermute | solution.py:19
  207.1 2.1 collective-permute-start.9
  209.3 2.1 collective-permute-done.8
  211.4 7.4 %collective-permute-done.9 = f32[2,64,1,512]{3,2,1,0:T(1,128)S(1)} collective-permute-done((f32[2,64,1,512]{3,2,1,0:T(1,128)S(1)}, f32[2,64,1,512]{3,2,1,0:T(1,128)S(1)}, u32[]{:S(2)}, u32[]{:S(2)}) %collective-permute-start.9) | collective-permute-done | bytes 262176 | tf_op jit(solution)/shard_map/ppermute | solution.py:20
  222.1 2.4 collective-permute-start.11
  225.5 8.3 %collective-permute-done.11 = f32[2,64,1,512]{3,2,1,0:T(1,128)S(1)} collective-permute-done((f32[2,64,1,512]{3,2,1,0:T(1,128)S(1)}, f32[2,64,1,512]{3,2,1,0:T(1,128)S(1)}, u32[]{:S(2)}, u32[]{:S(2)}) %collective-permute-start.11) | collective-permute-done | bytes 262176 | tf_op jit(solution)/shard_map/ppermute | solution.py:20
  237.1 2.5 collective-permute-start.13
  240.5 8.5 %collective-permute-done.13 = f32[2,64,1,512]{3,2,1,0:T(1,128)S(1)} collective-permute-done((f32[2,64,1,512]{3,2,1,0:T(1,128)S(1)}, f32[2,64,1,512]{3,2,1,0:T(1,128)S(1)}, u32[]{:S(2)}, u32[]{:S(2)}) %collective-permute-start.13) | collective-permute-done | bytes 262176 | tf_op jit(solution)/shard_map/ppermute | solution.py:20
  252.4 2.4 collective-permute-start.15
  255.7 8.3 %collective-permute-done.15 = f32[2,64,1,512]{3,2,1,0:T(1,128)S(1)} collective-permute-done((f32[2,64,1,512]{3,2,1,0:T(1,128)S(1)}, f32[2,64,1,512]{3,2,1,0:T(1,128)S(1)}, u32[]{:S(2)}, u32[]{:S(2)}) %collective-permute-start.15) | collective-permute-done | bytes 262176 | tf_op jit(solution)/shard_map/ppermute | solution.py:20
  264.0 2.3 fusion.6
  (54 shorter events, 34.9 us)
Async XLA Ops:
  6.5 64.3 %copy-start = (bf16[512,512]{1,0:T(8,128)(2,1)S(1)}, bf16[512,512]{1,0:T(8,128)(2,1)}, u32[]{:S(2)}) copy-start(bf16[512,512]{1,0:T(8,128)(2,1)} %param.14) | copy-start | bytes 1572868
  6.5 11.1 %copy-start.6 = (s32[64]{0:T(128)S(1)}, s32[64]{0:T(128)}, u32[]{:S(2)}) copy-start(s32[64]{0:T(128)} %param.13) | copy-start | bytes 772
  6.5 181.5 %all-reduce.2.cloned.1.call-start = ((), (), s32[]{:S(2)}) async-start(), calls=%async_computation | async-start | bytes 2097152 | tf_op jit(solution)/shard_map/psum | solution.py:53
  8.7 10.6 %collective-permute-start = (f32[2,64,1,512]{3,2,1,0:T(1,128)S(1)}, f32[2,64,1,512]{3,2,1,0:T(1,128)S(1)}, u32[]{:S(2)}, u32[]{:S(2)}) collective-permute-start(f32[2,64,1,512]{3,2,1,0:T(1,128)S(1)} %get-tuple-element.19), channel_id=1, source_target_pairs={{0,1},{1,2},{2,3},{3,4},{4,5},{5,6},{6,7},{7,8},{8,9},{9,10},{10,1... | collective-permute-start | bytes 786440 | tf_op jit(solution)/shard_map/ppermute | solution.py:19
  14.2 11.6 %collective-permute-start.1 = (f32[2,64,1,512]{3,2,1,0:T(1,128)S(1)}, f32[2,64,1,512]{3,2,1,0:T(1,128)S(1)}, u32[]{:S(2)}, u32[]{:S(2)}) collective-permute-start(f32[2,64,1,512]{3,2,1,0:T(1,128)S(1)} %get-tuple-element.20), channel_id=1, source_target_pairs={{1,0},{2,1},{3,2},{4,3},{5,4},{6,5},{7,6},{8,7},{9,8},{10,9},{11,1... | collective-permute-start | bytes 786440 | tf_op jit(solution)/shard_map/ppermute | solution.py:20
  27.2 5.3 %collective-permute-start.2 = (f32[2,64,1,512]{3,2,1,0:T(1,128)S(1)}, f32[2,64,1,512]{3,2,1,0:T(1,128)S(1)}, u32[]{:S(2)}, u32[]{:S(2)}) collective-permute-start(f32[2,64,1,512]{3,2,1,0:T(1,128)S(1)} %get-tuple-element.17), channel_id=1, source_target_pairs={{0,1},{1,2},{2,3},{3,4},{4,5},{5,6},{6,7},{7,8},{8,9},{9,10},{10,1... | collective-permute-start | bytes 786440 | tf_op jit(solution)/shard_map/ppermute | solution.py:19
  29.2 11.6 %collective-permute-start.3 = (f32[2,64,1,512]{3,2,1,0:T(1,128)S(1)}, f32[2,64,1,512]{3,2,1,0:T(1,128)S(1)}, u32[]{:S(2)}, u32[]{:S(2)}) collective-permute-start(f32[2,64,1,512]{3,2,1,0:T(1,128)S(1)} %get-tuple-element.18), channel_id=1, source_target_pairs={{1,0},{2,1},{3,2},{4,3},{5,4},{6,5},{7,6},{8,7},{9,8},{10,9},{11,1... | collective-permute-start | bytes 786440 | tf_op jit(solution)/shard_map/ppermute | solution.py:20
  42.2 5.3 %collective-permute-start.4 = (f32[2,64,1,512]{3,2,1,0:T(1,128)S(1)}, f32[2,64,1,512]{3,2,1,0:T(1,128)S(1)}, u32[]{:S(2)}, u32[]{:S(2)}) collective-permute-start(f32[2,64,1,512]{3,2,1,0:T(1,128)S(1)} %get-tuple-element.15), channel_id=1, source_target_pairs={{0,1},{1,2},{2,3},{3,4},{4,5},{5,6},{6,7},{7,8},{8,9},{9,10},{10,1... | collective-permute-start | bytes 786440 | tf_op jit(solution)/shard_map/ppermute | solution.py:19
  44.2 11.7 %collective-permute-start.5 = (f32[2,64,1,512]{3,2,1,0:T(1,128)S(1)}, f32[2,64,1,512]{3,2,1,0:T(1,128)S(1)}, u32[]{:S(2)}, u32[]{:S(2)}) collective-permute-start(f32[2,64,1,512]{3,2,1,0:T(1,128)S(1)} %get-tuple-element.16), channel_id=1, source_target_pairs={{1,0},{2,1},{3,2},{4,3},{5,4},{6,5},{7,6},{8,7},{9,8},{10,9},{11,1... | collective-permute-start | bytes 786440 | tf_op jit(solution)/shard_map/ppermute | solution.py:20
  55.8 6.0 %copy-start.7 = (f32[4]{0:T(128)S(1)}, f32[4]{0:T(128)}, u32[]{:S(2)}) copy-start(f32[4]{0:T(128)} %param.12) | copy-start | bytes 52
  55.8 6.0 %copy-start.8 = (s32[2]{0:T(128)S(1)}, s32[2]{0:T(128)}, u32[]{:S(2)}) copy-start(s32[2]{0:T(128)} %param.11) | copy-start | bytes 28
  57.3 5.3 %collective-permute-start.6 = (f32[2,64,1,512]{3,2,1,0:T(1,128)S(1)}, f32[2,64,1,512]{3,2,1,0:T(1,128)S(1)}, u32[]{:S(2)}, u32[]{:S(2)}) collective-permute-start(f32[2,64,1,512]{3,2,1,0:T(1,128)S(1)} %get-tuple-element.13), channel_id=1, source_target_pairs={{0,1},{1,2},{2,3},{3,4},{4,5},{5,6},{6,7},{7,8},{8,9},{9,10},{10,1... | collective-permute-start | bytes 786440 | tf_op jit(solution)/shard_map/ppermute | solution.py:19
  59.2 11.6 %collective-permute-start.7 = (f32[2,64,1,512]{3,2,1,0:T(1,128)S(1)}, f32[2,64,1,512]{3,2,1,0:T(1,128)S(1)}, u32[]{:S(2)}, u32[]{:S(2)}) collective-permute-start(f32[2,64,1,512]{3,2,1,0:T(1,128)S(1)} %get-tuple-element.14), channel_id=1, source_target_pairs={{1,0},{2,1},{3,2},{4,3},{5,4},{6,5},{7,6},{8,7},{9,8},{10,9},{11,1... | collective-permute-start | bytes 786440 | tf_op jit(solution)/shard_map/ppermute | solution.py:20
  75.5 112.5 %copy-start.3 = (bf16[64,8,512]{2,1,0:T(8,128)(2,1)S(1)}, bf16[64,8,512]{2,1,0:T(8,128)(2,1)}, u32[]{:S(2)}) copy-start(bf16[64,8,512]{2,1,0:T(8,128)(2,1)} %param.16) | copy-start | bytes 1572868
  75.5 112.5 %copy-start.4 = (bf16[64,8,512]{2,1,0:T(8,128)(2,1)S(1)}, bf16[64,8,512]{2,1,0:T(8,128)(2,1)}, u32[]{:S(2)}) copy-start(bf16[64,8,512]{2,1,0:T(8,128)(2,1)} %param.17) | copy-start | bytes 1572868
  194.3 17.1 %collective-permute-start.8 = (f32[2,64,1,512]{3,2,1,0:T(1,128)S(1)}, f32[2,64,1,512]{3,2,1,0:T(1,128)S(1)}, u32[]{:S(2)}, u32[]{:S(2)}) collective-permute-start(f32[2,64,1,512]{3,2,1,0:T(1,128)S(1)} %get-tuple-element.11), channel_id=1, source_target_pairs={{0,1},{1,2},{2,3},{3,4},{4,5},{5,6},{6,7},{7,8},{8,9},{9,10},{10,1... | collective-permute-start | bytes 786440 | tf_op jit(solution)/shard_map/ppermute | solution.py:19
  207.1 11.6 %collective-permute-start.9 = (f32[2,64,1,512]{3,2,1,0:T(1,128)S(1)}, f32[2,64,1,512]{3,2,1,0:T(1,128)S(1)}, u32[]{:S(2)}, u32[]{:S(2)}) collective-permute-start(f32[2,64,1,512]{3,2,1,0:T(1,128)S(1)} %get-tuple-element.12), channel_id=1, source_target_pairs={{1,0},{2,1},{3,2},{4,3},{5,4},{6,5},{7,6},{8,7},{9,8},{10,9},{11,1... | collective-permute-start | bytes 786440 | tf_op jit(solution)/shard_map/ppermute | solution.py:20
  220.2 5.3 %collective-permute-start.10 = (f32[2,64,1,512]{3,2,1,0:T(1,128)S(1)}, f32[2,64,1,512]{3,2,1,0:T(1,128)S(1)}, u32[]{:S(2)}, u32[]{:S(2)}) collective-permute-start(f32[2,64,1,512]{3,2,1,0:T(1,128)S(1)} %get-tuple-element.9), channel_id=1, source_target_pairs={{0,1},{1,2},{2,3},{3,4},{4,5},{5,6},{6,7},{7,8},{8,9},{9,10},{10,1... | collective-permute-start | bytes 786440 | tf_op jit(solution)/shard_map/ppermute | solution.py:19
  222.1 11.6 %collective-permute-start.11 = (f32[2,64,1,512]{3,2,1,0:T(1,128)S(1)}, f32[2,64,1,512]{3,2,1,0:T(1,128)S(1)}, u32[]{:S(2)}, u32[]{:S(2)}) collective-permute-start(f32[2,64,1,512]{3,2,1,0:T(1,128)S(1)} %get-tuple-element.10), channel_id=1, source_target_pairs={{1,0},{2,1},{3,2},{4,3},{5,4},{6,5},{7,6},{8,7},{9,8},{10,9},{11,1... | collective-permute-start | bytes 786440 | tf_op jit(solution)/shard_map/ppermute | solution.py:20
  235.2 5.3 %collective-permute-start.12 = (f32[2,64,1,512]{3,2,1,0:T(1,128)S(1)}, f32[2,64,1,512]{3,2,1,0:T(1,128)S(1)}, u32[]{:S(2)}, u32[]{:S(2)}) collective-permute-start(f32[2,64,1,512]{3,2,1,0:T(1,128)S(1)} %get-tuple-element.7), channel_id=1, source_target_pairs={{0,1},{1,2},{2,3},{3,4},{4,5},{5,6},{6,7},{7,8},{8,9},{9,10},{10,1... | collective-permute-start | bytes 786440 | tf_op jit(solution)/shard_map/ppermute | solution.py:19
  237.1 26.9 %copy-start.1 = (bf16[2,64,8,512]{3,2,1,0:T(8,128)(2,1)S(1)}, bf16[2,64,8,512]{3,2,1,0:T(8,128)(2,1)}, u32[]{:S(2)}) copy-start(bf16[2,64,8,512]{3,2,1,0:T(8,128)(2,1)} %param.9) | copy-start | bytes 3145732
  237.1 11.8 %collective-permute-start.13 = (f32[2,64,1,512]{3,2,1,0:T(1,128)S(1)}, f32[2,64,1,512]{3,2,1,0:T(1,128)S(1)}, u32[]{:S(2)}, u32[]{:S(2)}) collective-permute-start(f32[2,64,1,512]{3,2,1,0:T(1,128)S(1)} %get-tuple-element.8), channel_id=1, source_target_pairs={{1,0},{2,1},{3,2},{4,3},{5,4},{6,5},{7,6},{8,7},{9,8},{10,9},{11,1... | collective-permute-start | bytes 786440 | tf_op jit(solution)/shard_map/ppermute | solution.py:20
  250.4 5.3 %collective-permute-start.14 = (f32[2,64,1,512]{3,2,1,0:T(1,128)S(1)}, f32[2,64,1,512]{3,2,1,0:T(1,128)S(1)}, u32[]{:S(2)}, u32[]{:S(2)}) collective-permute-start(f32[2,64,1,512]{3,2,1,0:T(1,128)S(1)} %get-tuple-element.5), channel_id=1, source_target_pairs={{0,1},{1,2},{2,3},{3,4},{4,5},{5,6},{6,7},{7,8},{8,9},{9,10},{10,1... | collective-permute-start | bytes 786440 | tf_op jit(solution)/shard_map/ppermute | solution.py:19
  252.4 11.6 %collective-permute-start.15 = (f32[2,64,1,512]{3,2,1,0:T(1,128)S(1)}, f32[2,64,1,512]{3,2,1,0:T(1,128)S(1)}, u32[]{:S(2)}, u32[]{:S(2)}) collective-permute-start(f32[2,64,1,512]{3,2,1,0:T(1,128)S(1)} %get-tuple-element.6), channel_id=1, source_target_pairs={{1,0},{2,1},{3,2},{4,3},{5,4},{6,5},{7,6},{8,7},{9,8},{10,9},{11,1... | collective-permute-start | bytes 786440 | tf_op jit(solution)/shard_map/ppermute | solution.py:20
  (2 other events, 4.7 us)
Sparse Core Ops, SparseCore 0:
  78.0 109.9 all-reduce.1
where the time goes:
time: 274 us; the launch traced here: 273 us
  waiting for transfers between devices  183 us (67%)
  starting transfers between devices  48.6 us (18%)
  other arithmetic  15 us (5%)
  between operations  13.7 us (5%)
  matrix products  8.73 us (3%)
  local copies, waits for them, and re-layouts  4.46 us (2%)
    psum x1, waiting for transfers between devices, shards(): summed = lax.psum(partial_sum, 'mem')  110 us
    ppermute x8, waiting for transfers between devices, with_halo(): after = lax.ppermute(leading, axis, down)  63.6 us
    ppermute x8, starting transfers between devices, with_halo(): before = lax.ppermute(last, axis, up)  29.8 us
    ppermute x8, starting transfers between devices, with_halo(): after = lax.ppermute(leading, axis, down)  18.8 us
    ppermute x8, waiting for transfers between devices, with_halo(): before = lax.ppermute(last, axis, up)  8.84 us
    add x6, other arithmetic, diffuse(): values + jnp.where(active, diffusion_number * second, jnp.float32(0.0))  6.81 us
  transfers between devices with their start and end apart: 17, of which 17 were waited for; matrix products, arithmetic and copies ran while one was open for 1% of the time, Pallas kernels for 0%

commit v1 on v0

v1 whole, which is shorter than its diff:
```python
import functools

import jax
import jax.numpy as jnp
from jax import lax
from jax.experimental import pallas as pl
from jax.experimental.pallas import tpu as pltpu
from jax.sharding import PartitionSpec as P

LEV = 64
ROWS = 8
LAT = 512
KMAX = 4
HALO = 4
MEMBERS = 2
XS = 4
OWN = LEV * ROWS
SIDE = LEV * HALO

BF = jnp.bfloat16
F32 = jnp.float32
VMEM = pl.BlockSpec(memory_space=pltpu.VMEM)
SMEM = pl.BlockSpec(memory_space=pltpu.SMEM)

BAND = {
    1: {1: 0.5},
    2: {0: 0.5, 2: 0.25},
    3: {1: 0.375, 3: 0.125},
    4: {0: 0.375, 2: 0.25, 4: 0.0625},
}


def call(kernel, out, operands, specs, flops, moved):
    return pl.pallas_call(
        kernel,
        out_shape=out,
        in_specs=specs,
        out_specs=jax.tree.map(lambda _: VMEM, out),
        compiler_params=pltpu.CompilerParams(vmem_limit_bytes=40 * 2**20),
        cost_estimate=pl.CostEstimate(flops=flops, bytes_accessed=moved, transcendentals=0),
    )(*operands)


def halves(x):
    columns = x.shape[1]
    x = x.reshape(LEV // 2, 2, ROWS, columns)
    even, odd = x[:, 0], x[:, 1]
    low = lax.broadcasted_iota(jnp.int32, even.shape, 1) < HALO
    top = jnp.where(low, even, pltpu.roll(odd, HALO, 1))
    bottom = jnp.where(low, pltpu.roll(even, HALO, 1), odd)
    return top.reshape(SIDE, columns), bottom.reshape(SIDE, columns)


def pack_kernel(x_ref, top_ref, bottom_ref):
    for m in range(x_ref.shape[0]):
        top, bottom = halves(x_ref[m].astype(F32))
        top_ref[m] = top.astype(BF)
        bottom_ref[m] = bottom.astype(BF)


def pack(x):
    members = x.shape[0]
    half = jax.ShapeDtypeStruct((members, SIDE, LAT), BF)
    return call(pack_kernel, (half, half), (x,), [VMEM], 0, 4 * members * OWN * LAT)


def weights(n, distance):
    total = jnp.zeros(distance.shape, F32)
    for sweeps, band in BAND.items():
        row = jnp.zeros(distance.shape, F32)
        for d, c in band.items():
            row = jnp.where(jnp.abs(distance) == d, jnp.float32(c), row)
        total = jnp.where(n == sweeps, row, total)
    return total


def spread_lanes(width, per):
    level = lax.broadcasted_iota(jnp.int32, (LEV, width), 0)
    lane = lax.broadcasted_iota(jnp.int32, (LEV, width), 1)
    return jnp.where(level == lane // per, F32(1.0), F32(0.0)).astype(BF)


def side_distance():
    row = lax.broadcasted_iota(jnp.int32, (ROWS, 2 * SIDE), 0)
    lane = lax.broadcasted_iota(jnp.int32, (ROWS, 2 * SIDE), 1)
    place = jnp.where(lane < SIDE, lane % HALO - HALO, lane % HALO + ROWS)
    return place - row


def own_distance():
    row = lax.broadcasted_iota(jnp.int32, (ROWS, OWN), 0)
    lane = lax.broadcasted_iota(jnp.int32, (ROWS, OWN), 1)
    return lane % ROWS - row


def first_kernel(
    group_ref, weight_ref, steps_ref, steps_row_ref, vert_ref, lat_ref, control_ref, perturb_ref,
    side_ref, back_own_ref, back_side_ref, partial_ref, table,
):
    vert = vert_ref[...].astype(BF)
    steps_row = steps_row_ref[...].astype(F32).astype(BF)
    lanes_own = spread_lanes(OWN, ROWS)
    lanes_half = spread_lanes(SIDE, HALO)
    lanes_side = jnp.concatenate([lanes_half, lanes_half], axis=1)

    def expand(matrix, lanes, dims=(((1,), (0,)), ((), ()))):
        return lax.dot_general(matrix, lanes, dims, preferred_element_type=F32)

    def forward(lanes, distance):
        n = expand(steps_row, lanes)
        wide = expand(vert, lanes)
        band = weights(n, distance)
        return (wide[:, None, :] * band[None]).reshape(OWN, OWN).astype(BF)

    side_ref[...] = forward(lanes_side, side_distance())
    own = forward(lanes_own, own_distance())

    first_dim = (((0,), (0,)), ((), ()))
    for lanes, distance, out_ref in (
        (lanes_own, own_distance(), back_own_ref),
        (lanes_side, side_distance(), back_side_ref),
    ):
        wide = expand(vert, lanes, first_dim)
        for n in range(1, KMAX + 1):
            table[n - 1] = weights(n, distance)
        for l in range(0, LEV, 2):
            pair = [wide[l + i : l + i + 1] * table[steps_ref[l + i] - 1] for i in range(2)]
            out_ref[pl.ds(l * ROWS, 2 * ROWS), :] = jnp.concatenate(pair, axis=0).astype(BF)

    total = jnp.zeros((OWN, LAT), F32)
    for m in range(MEMBERS):
        mixed = jnp.dot(own, control_ref[m], preferred_element_type=F32).astype(BF)
        local = jnp.dot(mixed, lat_ref[...], preferred_element_type=F32)
        weight = weight_ref[group_ref[m]]
        total = total + (weight * perturb_ref[m].astype(F32)) * local
    partial_ref[...] = total


def forward_kernel(
    group_ref, weight_ref, side_ref, lat_ref, left_ref, right_ref, perturb_ref, partial_ref, out_ref
):
    total = partial_ref[...]
    for m in range(MEMBERS):
        mixed = jnp.dot(side_ref[:, :SIDE], left_ref[m], preferred_element_type=F32)
        mixed += jnp.dot(side_ref[:, SIDE:], right_ref[m], preferred_element_type=F32)
        local = jnp.dot(mixed.astype(BF), lat_ref[...], preferred_element_type=F32)
        weight = weight_ref[group_ref[m]]
        total = total + (weight * perturb_ref[m].astype(F32)) * local
    out_ref[...] = total.astype(BF)


LAST = (((1,), (1,)), ((), ()))


def back_own_kernel(
    group_ref, weight_ref, back_own_ref, lat_ref, misfit_ref, perturb_ref, control_ref, out_ref
):
    misfit = misfit_ref[...].astype(F32)
    for m in range(MEMBERS):
        weight = weight_ref[group_ref[m]]
        back = ((weight * perturb_ref[m].astype(F32)) * misfit).astype(BF)
        mixed = jnp.dot(back_own_ref[...], back, preferred_element_type=F32).astype(BF)
        latback = lax.dot_general(mixed, lat_ref[...], LAST, preferred_element_type=F32)
        out_ref[m] = control_ref[m].astype(F32) + latback


def back_side_kernel(
    group_ref, weight_ref, back_side_ref, lat_ref, left_ref, right_ref, p_left_ref, p_right_ref,
    base_ref, out_ref,
):
    left = left_ref[...].astype(F32)
    right = right_ref[...].astype(F32)
    for m in range(MEMBERS):
        weight = weight_ref[group_ref[m]]
        from_left = ((weight * p_left_ref[m].astype(F32)) * left).astype(BF)
        from_right = ((weight * p_right_ref[m].astype(F32)) * right).astype(BF)
        mixed = jnp.dot(back_side_ref[:, :SIDE], from_left, preferred_element_type=F32)
        mixed += jnp.dot(back_side_ref[:, SIDE:], from_right, preferred_element_type=F32)
        latback = lax.dot_general(mixed.astype(BF), lat_ref[...], LAST, preferred_element_type=F32)
        out_ref[m] = (base_ref[m] + latback).astype(BF)


def shards(
    control,
    perturb,
    member_group,
    group_weight,
    step_counts,
    lat_inverse,
    vert_inverse,
    innovation,
    precision,
):
    lons = lax.axis_size("lon")
    up = [(i, (i + 1) % lons) for i in range(lons)]
    down = [(j, i) for i, j in up]
    mems = lax.axis_size("mem")
    along_x = [list(range(i, i + XS)) for i in range(0, mems, XS)]
    across_y = [(i, (i + XS) % mems) for i in range(mems)]
    x = lax.axis_index("mem") % XS

    def halo(top, bottom):
        return lax.ppermute(bottom, "lon", up), lax.ppermute(top, "lon", down)

    control = control.reshape(MEMBERS, OWN, LAT)
    perturb = perturb.reshape(MEMBERS, OWN, LAT)
    c_left, c_right = halo(*pack(control))
    p_left, p_right = halo(*pack(perturb))

    square = OWN * LAT
    matmul = 2 * OWN * LAT * LAT
    side, back_own, back_side, partial = call(
        first_kernel_with_table,
        (
            jax.ShapeDtypeStruct((OWN, 2 * SIDE), BF),
            jax.ShapeDtypeStruct((OWN, OWN), BF),
            jax.ShapeDtypeStruct((OWN, 2 * SIDE), BF),
            jax.ShapeDtypeStruct((OWN, LAT), F32),
        ),
        (member_group, group_weight, step_counts, step_counts.reshape(1, LEV), vert_inverse,
         lat_inverse, control, perturb),
        [SMEM, SMEM, SMEM] + [VMEM] * 5,
        4 * matmul, 20 * square,
    )
    partial = call(
        forward_kernel,
        jax.ShapeDtypeStruct((OWN, LAT), BF),
        (member_group, group_weight, side, lat_inverse, c_left, c_right, perturb, partial),
        [SMEM, SMEM] + [VMEM] * 6,
        4 * matmul, 18 * square,
    )

    quarter = OWN // XS
    parts = lax.all_to_all(
        partial.reshape(XS, quarter, LAT), "mem", 0, 0, axis_index_groups=along_x
    )
    some = jnp.sum(parts.astype(F32), axis=0).astype(BF)
    other = lax.ppermute(some, "mem", across_y)
    increment = some.astype(F32) + other.astype(F32)
    innov = lax.dynamic_slice_in_dim(innovation.reshape(OWN, LAT), x * quarter, quarter, 0)
    prec = lax.dynamic_slice_in_dim(precision.reshape(OWN, LAT), x * quarter, quarter, 0)
    misfit = (prec.astype(F32) * (increment - innov.astype(F32))).astype(BF)
    misfit = lax.all_to_all(
        jnp.broadcast_to(misfit, (XS, quarter, LAT)), "mem", 0, 0, axis_index_groups=along_x
    ).reshape(OWN, LAT)

    top, bottom = pack(misfit[None])
    m_left, m_right = halo(top[0], bottom[0])
    base = call(
        back_own_kernel,
        jax.ShapeDtypeStruct((MEMBERS, OWN, LAT), F32),
        (member_group, group_weight, back_own, lat_inverse, misfit, perturb, control),
        [SMEM, SMEM] + [VMEM] * 5,
        4 * matmul, 18 * square,
    )
    out = call(
        back_side_kernel,
        jax.ShapeDtypeStruct((MEMBERS, OWN, LAT), BF),
        (member_group, group_weight, back_side, lat_inverse, m_left, m_right, p_left, p_right, base),
        [SMEM, SMEM] + [VMEM] * 7,
        4 * matmul, 20 * square,
    )
    return out.reshape(MEMBERS, LEV, ROWS, LAT)


def first_kernel_with_table(*refs):
    pl.run_scoped(
        functools.partial(first_kernel, *refs), pltpu.VMEM((KMAX, ROWS, OWN), F32)
    )


def solution(mesh):
    return jax.shard_map(
        shards,
        mesh=mesh,
        in_specs=(
            P("mem", None, "lon", None),
            P("mem", None, "lon", None),
            P("mem"),
            P(),
            P(),
            P(),
            P(),
            P(None, "lon", None),
            P(None, "lon", None),
        ),
        out_specs=P("mem", None, "lon", None),
        check_vma=False,
    )
```

time: 274 us -> 87.8 us (0.32)
  the two profiles are of different devices: /device:TPU:217 before, /device:TPU:2 now
where the time goes in v1:
time: 87.8 us; the launch traced here: 87.1 us
  starting transfers between devices  44.3 us (50%)
  Pallas kernels  11.4 us (13%)
  blocking collectives  11.3 us (13%)
  local copies, waits for them, and re-layouts  10.9 us (12%)
  waiting for transfers between devices  7.76 us (9%)
  other arithmetic  1.14 us (1%)
    ppermute x6, starting transfers between devices, halo(): return (lax.ppermute(bottom, 'lon', up), lax.ppermute(top, 'lon', down))  34.3 us
    pallas_call x7, Pallas kernels, call(): pl.pallas_call(kernel, out_shape=out, in_specs=specs, out_specs=jax.tree....  11.4 us
    all_to_all x1, blocking collectives, shards(): lax.all_to_all(partial.reshape(XS, quarter, LAT), 'mem', 0, 0, axis_index...  11.3 us
    unnamed x34, local copies, waits for them, and re-layouts  10.1 us
    ppermute x1, waiting for transfers between devices, shards(): other = lax.ppermute(some, 'mem', across_y)  5.75 us
    ppermute x1, starting transfers between devices, shards(): other = lax.ppermute(some, 'mem', across_y)  5.16 us
    all_to_all x1, starting transfers between devices, shards(): lax.all_to_all(jnp.broadcast_to(misfit, (XS, quarter, LAT)), 'mem', 0, 0,...  4.9 us
    ppermute x6, waiting for transfers between devices, halo(): return (lax.ppermute(bottom, 'lon', up), lax.ppermute(top, 'lon', down))  2.01 us
  transfers between devices with their start and end apart: 8, of which 2 were waited for; matrix products, arithmetic and copies ran while one was open for 0% of the time, Pallas kernels for 6%

profile of v1, /device:TPU:2, one launch (start us, length us, event | category | flops | bytes accessed | tf_op | source)
XLA Modules:
  0.0 87.1 jit_solution(11623624004255764972)
XLA Ops:
  0.0 1.2 %copy-done.4 = bf16[2,64,8,512]{3,2,1,0:T(8,128)(2,1)S(1)} copy-done((bf16[2,64,8,512]{3,2,1,0:T(8,128)(2,1)S(1)}, bf16[2,64,8,512]{3,2,1,0:T(8,128)(2,1)}, u32[]{:S(2)}) %copy-start.4) | copy-done | bytes 1048600
  1.6 1.9 %collective-permute-start = (bf16[2,256,512]{2,1,0:T(8,128)(2,1)S(1)}, bf16[2,256,512]{2,1,0:T(8,128)(2,1)S(1)}, u32[]{:S(2)}, u32[]{:S(2)}) collective-permute-start(bf16[2,256,512]{2,1,0:T(8,128)(2,1)S(1)} %get-tuple-element.17), channel_id=1, source_target_pairs={{0,1},{1,2},{2,3},{3,4},{4,5},{5,6},{6,7},{7,8},{8,9},{9,10},{10,1... | collective-permute-start | bytes 1572872 | tf_op jit(solution)/shard_map/ppermute | solution.py:203
  3.5 13.4 %collective-permute-start.1 = (bf16[2,256,512]{2,1,0:T(8,128)(2,1)S(1)}, bf16[2,256,512]{2,1,0:T(8,128)(2,1)S(1)}, u32[]{:S(2)}, u32[]{:S(2)}) collective-permute-start(bf16[2,256,512]{2,1,0:T(8,128)(2,1)S(1)} %get-tuple-element.18), channel_id=1, source_target_pairs={{1,0},{2,1},{3,2},{4,3},{5,4},{6,5},{7,6},{8,7},{9,8},{10,9},{11,1... | collective-permute-start | bytes 1572872 | tf_op jit(solution)/shard_map/ppermute | solution.py:203
  16.9 1.2 %copy-done = bf16[2,64,8,512]{3,2,1,0:T(8,128)(2,1)S(1)} copy-done((bf16[2,64,8,512]{3,2,1,0:T(8,128)(2,1)S(1)}, bf16[2,64,8,512]{3,2,1,0:T(8,128)(2,1)}, u32[]{:S(2)}) %copy-start) | copy-done | bytes 1048600
  18.1 1.0 %copy-done.2 = bf16[512,512]{1,0:T(8,128)(2,1)S(1)} copy-done((bf16[512,512]{1,0:T(8,128)(2,1)S(1)}, bf16[512,512]{1,0:T(8,128)(2,1)}, u32[]{:S(2)}) %copy-start.2) | copy-done | bytes 524312
  19.2 1.2 %copy-done.5 = bf16[2,64,8,512]{3,2,1,0:T(8,128)(2,1)S(1)} copy-done((bf16[2,64,8,512]{3,2,1,0:T(8,128)(2,1)S(1)}, bf16[2,64,8,512]{3,2,1,0:T(8,128)(2,1)}, u32[]{:S(2)}) %copy-start.5) | copy-done | bytes 1048600
  23.1 2.3 %shard_map.91 = (bf16[512,512]{1,0:T(8,128)(2,1)S(1)}, bf16[512,512]{1,0:T(8,128)(2,1)S(1)}, bf16[512,512]{1,0:T(8,128)(2,1)S(1)}, f32[512,512]{1,0:T(8,128)S(1)}) custom-call(s32[2]{0:T(128)S(1)} %copy-done.11, f32[4]{0:T(128)S(1)} %copy-done.13, s32[64]{0:T(128)S(1)} %copy-done.16, s32[1,64]{1,0:T(1,128)S(1)} %bitcast.23, f32[64,64]{1,0:T(8,128)S(1)} %copy-done.15, ...), custom_call_target="tpu_custom_call" | custom-call | flops 1073741824 | bytes 5242880 | tf_op jit(solution)/shard_map/pallas_call | solution.py:34
  26.3 0.8 copy-done.9
  27.1 1.9 %shard_map.93 = bf16[512,512]{1,0:T(8,128)(2,1)S(1)} custom-call(s32[2]{0:T(128)S(1)} %copy-done.11, f32[4]{0:T(128)S(1)} %copy-done.13, bf16[512,512]{1,0:T(8,128)(2,1)S(1)} %get-tuple-element.16.side_ref, bf16[512,512]{1,0:T(8,128)(2,1)S(1)} %copy-done.2, bf16[2,256,512]{2,1,0:T(8,128)(2,1)S(1)} %collective-permute-done.left_ref, ...), custom_call_target="tpu_custom_call" | custom-call | flops 1073741824 | bytes 4718592 | tf_op jit(solution)/shard_map/pallas_call | solution.py:34
  29.0 11.3 %all_to_all.10 = bf16[4,128,512]{2,1,0:T(8,128)(2,1)S(1)} all-to-all(bf16[4,128,512]{2,1,0:T(8,128)(2,1)S(1)} %bitcast.20), channel_id=1, replica_groups={{0,64,128,192},{256,320,384,448},{1,65,129,193},{257,321,385,449},{2,66..., dimensions={0} | all-to-all | bytes 1048576 | tf_op jit(solution)/shard_map/all_to_all | solution.py:234
  40.4 5.2 %collective-permute-start.2 = (bf16[128,512]{1,0:T(8,128)(2,1)S(1)}, bf16[128,512]{1,0:T(8,128)(2,1)S(1)}, u32[]{:S(2)}, u32[]{:S(2)}) collective-permute-start(bf16[128,512]{1,0:T(8,128)(2,1)S(1)} %reduce_sum.12), channel_id=1, source_target_pairs={{0,256},{64,320},{128,384},{192,448},{256,0},{320,64},{384,128},{4... | collective-permute-start | bytes 393224 | tf_op jit(solution)/shard_map/ppermute | solution.py:238
  45.6 5.8 %collective-permute-done.2 = bf16[128,512]{1,0:T(8,128)(2,1)S(1)} collective-permute-done((bf16[128,512]{1,0:T(8,128)(2,1)S(1)}, bf16[128,512]{1,0:T(8,128)(2,1)S(1)}, u32[]{:S(2)}, u32[]{:S(2)}) %collective-permute-start.2) | collective-permute-done | bytes 131104 | tf_op jit(solution)/shard_map/ppermute | solution.py:238
  51.3 1.1 %multiply_convert_fusion = bf16[128,512]{1,0:T(8,128)(2,1)S(1)} fusion(bf16[128,512]{1,0:T(8,128)(2,1)S(1)} %collective-permute-done.2, bf16[128,512]{1,0:T(8,128)(2,1)S(1)} %reduce_sum.12, bf16[512,512]{1,0:T(8,128)(2,1)} %bitcast.24, s32[]{:T(128)S(6)} %select_n.12, bf16[512,512]{1,0:T(8,128)(2,1)} %bitcast.25), kind=kLoop, calls=%fused_computation | loop fusion | flops 524288 | bytes 655364 | tf_op jit(solution)/shard_map/convert_element_type | solution.py:242
  52.4 0.8 broadcast_in_dim.3
  53.2 4.9 %all-to-all-start.1 = ((bf16[4,128,512]{2,1,0:T(8,128)(2,1)}), bf16[4,128,512]{2,1,0:T(8,128)(2,1)S(1)}, u32[]{:S(2)}, u32[]{:S(2)}) async-start(bf16[4,128,512]{2,1,0:T(8,128)(2,1)} %broadcast_in_dim.3), calls=%async_computation.1 | async-start | bytes 1048576 | tf_op jit(solution)/shard_map/all_to_all | solution.py:243
  58.1 1.3 %shard_map.95 = (bf16[2,256,512]{2,1,0:T(8,128)(2,1)}, bf16[2,256,512]{2,1,0:T(8,128)(2,1)}) custom-call(bf16[2,512,512]{2,1,0:T(8,128)(2,1)S(1)} %bitcast.13), custom_call_target="tpu_custom_call" | custom-call | bytes 2097152 | tf_op jit(solution)/shard_map/pallas_call | solution.py:34
  59.4 1.9 %collective-permute-start.5 = (bf16[2,256,512]{2,1,0:T(8,128)(2,1)}, bf16[2,256,512]{2,1,0:T(8,128)(2,1)}, u32[]{:S(2)}, u32[]{:S(2)}) collective-permute-start(bf16[2,256,512]{2,1,0:T(8,128)(2,1)} %get-tuple-element.22), channel_id=1, source_target_pairs={{0,1},{1,2},{2,3},{3,4},{4,5},{5,6},{6,7},{7,8},{8,9},{9,10},{10,1... | collective-permute-start | bytes 1572872 | tf_op jit(solution)/shard_map/ppermute | solution.py:203
  61.3 7.6 %collective-permute-start.6 = (bf16[2,256,512]{2,1,0:T(8,128)(2,1)}, bf16[2,256,512]{2,1,0:T(8,128)(2,1)}, u32[]{:S(2)}, u32[]{:S(2)}) collective-permute-start(bf16[2,256,512]{2,1,0:T(8,128)(2,1)} %get-tuple-element.23), channel_id=1, source_target_pairs={{1,0},{2,1},{3,2},{4,3},{5,4},{6,5},{7,6},{8,7},{9,8},{10,9},{11,1... | collective-permute-start | bytes 1572872 | tf_op jit(solution)/shard_map/ppermute | solution.py:203
  69.1 1.9 %collective-permute-start.3 = (bf16[256,512]{1,0:T(8,128)(2,1)S(1)}, bf16[256,512]{1,0:T(8,128)(2,1)S(1)}, u32[]{:S(2)}, u32[]{:S(2)}) collective-permute-start(bf16[256,512]{1,0:T(8,128)(2,1)S(1)} %bitcast.22), channel_id=1, source_target_pairs={{0,1},{1,2},{2,3},{3,4},{4,5},{5,6},{6,7},{7,8},{8,9},{9,10},{10,1... | collective-permute-start | bytes 786440 | tf_op jit(solution)/shard_map/ppermute | solution.py:203
  71.0 7.5 %collective-permute-start.4 = (bf16[256,512]{1,0:T(8,128)(2,1)S(1)}, bf16[256,512]{1,0:T(8,128)(2,1)S(1)}, u32[]{:S(2)}, u32[]{:S(2)}) collective-permute-start(bf16[256,512]{1,0:T(8,128)(2,1)S(1)} %bitcast.21), channel_id=1, source_target_pairs={{1,0},{2,1},{3,2},{4,3},{5,4},{6,5},{7,6},{8,7},{9,8},{10,9},{11,1... | collective-permute-start | bytes 786440 | tf_op jit(solution)/shard_map/ppermute | solution.py:203
  78.6 1.0 %copy-done.10 = bf16[512,512]{1,0:T(8,128)(2,1)S(1)} copy-done((bf16[512,512]{1,0:T(8,128)(2,1)S(1)}, bf16[512,512]{1,0:T(8,128)(2,1)}, u32[]{:S(2)}) %copy-start.10) | copy-done | bytes 524312
  79.6 1.9 %shard_map.96.base_ref = f32[2,512,512]{2,1,0:T(8,128)S(1)} custom-call(s32[2]{0:T(128)S(1)} %copy-done.12, f32[4]{0:T(128)S(1)} %copy-done.14, bf16[512,512]{1,0:T(8,128)(2,1)S(1)} %copy-done.10, bf16[512,512]{1,0:T(8,128)(2,1)S(1)} %copy-done.3, bf16[512,512]{1,0:T(8,128)(2,1)S(1)} %bitcast.16, bf16[2,512,512]{2,1,0:T(8,128)(2,1)S(1)} %bitcast.14, ...), custom_call_target="tpu_custom_call" | custom-call | flops 1073741824 | bytes 4718592 | tf_op jit(solution)/shard_map/pallas_call | solution.py:34
  81.5 2.0 %collective-permute-done.3.left_ref = bf16[256,512]{1,0:T(8,128)(2,1)S(1)} collective-permute-done((bf16[256,512]{1,0:T(8,128)(2,1)S(1)}, bf16[256,512]{1,0:T(8,128)(2,1)S(1)}, u32[]{:S(2)}, u32[]{:S(2)}) %collective-permute-start.3) | collective-permute-done | bytes 262176 | tf_op jit(solution)/shard_map/ppermute | solution.py:203
  83.5 3.5 %shard_map.97 = bf16[2,512,512]{2,1,0:T(8,128)(2,1)} custom-call(s32[2]{0:T(128)S(1)} %copy-done.12, f32[4]{0:T(128)S(1)} %copy-done.14, bf16[512,512]{1,0:T(8,128)(2,1)S(1)} %copy-done.8, bf16[512,512]{1,0:T(8,128)(2,1)S(1)} %copy-done.3, bf16[256,512]{1,0:T(8,128)(2,1)S(1)} %collective-permute-done.3.left_ref, ...), custom_call_target="tpu_custom_call" | custom-call | flops 1073741824 | bytes 5242880 | tf_op jit(solution)/shard_map/pallas_call | solution.py:34
  (37 shorter events, 4.1 us)
Async XLA Ops:
  0.0 1.2 %copy-start.4 = (bf16[2,64,8,512]{3,2,1,0:T(8,128)(2,1)S(1)}, bf16[2,64,8,512]{3,2,1,0:T(8,128)(2,1)}, u32[]{:S(2)}) copy-start(bf16[2,64,8,512]{3,2,1,0:T(8,128)(2,1)} %param.9) | copy-start | bytes 3145732
  1.2 25.8 %copy-start.1 = (bf16[2,64,8,512]{3,2,1,0:T(8,128)(2,1)S(1)}, bf16[2,64,8,512]{3,2,1,0:T(8,128)(2,1)}, u32[]{:S(2)}) copy-start(bf16[2,64,8,512]{3,2,1,0:T(8,128)(2,1)} %param.10) | copy-start | bytes 3145732
  1.6 25.5 %collective-permute-start = (bf16[2,256,512]{2,1,0:T(8,128)(2,1)S(1)}, bf16[2,256,512]{2,1,0:T(8,128)(2,1)S(1)}, u32[]{:S(2)}, u32[]{:S(2)}) collective-permute-start(bf16[2,256,512]{2,1,0:T(8,128)(2,1)S(1)} %get-tuple-element.17), channel_id=1, source_target_pairs={{0,1},{1,2},{2,3},{3,4},{4,5},{5,6},{6,7},{7,8},{8,9},{9,10},{10,1... | collective-permute-start | bytes 1572872 | tf_op jit(solution)/shard_map/ppermute | solution.py:203
  3.5 23.6 %collective-permute-start.1 = (bf16[2,256,512]{2,1,0:T(8,128)(2,1)S(1)}, bf16[2,256,512]{2,1,0:T(8,128)(2,1)S(1)}, u32[]{:S(2)}, u32[]{:S(2)}) collective-permute-start(bf16[2,256,512]{2,1,0:T(8,128)(2,1)S(1)} %get-tuple-element.18), channel_id=1, source_target_pairs={{1,0},{2,1},{3,2},{4,3},{5,4},{6,5},{7,6},{8,7},{9,8},{10,9},{11,1... | collective-permute-start | bytes 1572872 | tf_op jit(solution)/shard_map/ppermute | solution.py:203
  16.9 1.2 %copy-start = (bf16[2,64,8,512]{3,2,1,0:T(8,128)(2,1)S(1)}, bf16[2,64,8,512]{3,2,1,0:T(8,128)(2,1)}, u32[]{:S(2)}) copy-start(bf16[2,64,8,512]{3,2,1,0:T(8,128)(2,1)} %param.10) | copy-start | bytes 3145732
  18.1 1.0 %copy-start.2 = (bf16[512,512]{1,0:T(8,128)(2,1)S(1)}, bf16[512,512]{1,0:T(8,128)(2,1)}, u32[]{:S(2)}) copy-start(bf16[512,512]{1,0:T(8,128)(2,1)} %lat_ref.5) | copy-start | bytes 1572868
  19.2 1.2 %copy-start.5 = (bf16[2,64,8,512]{3,2,1,0:T(8,128)(2,1)S(1)}, bf16[2,64,8,512]{3,2,1,0:T(8,128)(2,1)}, u32[]{:S(2)}) copy-start(bf16[2,64,8,512]{3,2,1,0:T(8,128)(2,1)} %param.9) | copy-start | bytes 3145732
  20.4 0.7 copy-start.11
  21.1 0.7 copy-start.13
  21.7 0.8 copy-start.15
  25.5 0.8 copy-start.7
  26.3 0.8 copy-start.9
  40.3 38.2 %copy-start.3 = (bf16[512,512]{1,0:T(8,128)(2,1)S(1)}, bf16[512,512]{1,0:T(8,128)(2,1)}, u32[]{:S(2)}) copy-start(bf16[512,512]{1,0:T(8,128)(2,1)} %lat_ref.5) | copy-start | bytes 1572868
  40.4 38.2 %copy-start.6 = (bf16[2,64,8,512]{3,2,1,0:T(8,128)(2,1)S(1)}, bf16[2,64,8,512]{3,2,1,0:T(8,128)(2,1)}, u32[]{:S(2)}) copy-start(bf16[2,64,8,512]{3,2,1,0:T(8,128)(2,1)} %param.9) | copy-start | bytes 3145732
  40.4 38.2 %copy-start.12 = (s32[2]{0:T(128)S(1)}, s32[2]{0:T(128)}, u32[]{:S(2)}) copy-start(s32[2]{0:T(128)} %group_ref.5) | copy-start | bytes 28
  40.4 38.2 %copy-start.14 = (f32[4]{0:T(128)S(1)}, f32[4]{0:T(128)}, u32[]{:S(2)}) copy-start(f32[4]{0:T(128)} %weight_ref.5) | copy-start | bytes 52
  40.4 10.9 %collective-permute-start.2 = (bf16[128,512]{1,0:T(8,128)(2,1)S(1)}, bf16[128,512]{1,0:T(8,128)(2,1)S(1)}, u32[]{:S(2)}, u32[]{:S(2)}) collective-permute-start(bf16[128,512]{1,0:T(8,128)(2,1)S(1)} %reduce_sum.12), channel_id=1, source_target_pairs={{0,256},{64,320},{128,384},{192,448},{256,0},{320,64},{384,128},{4... | collective-permute-start | bytes 393224 | tf_op jit(solution)/shard_map/ppermute | solution.py:238
  53.2 15.6 %all-to-all-start.1 = ((bf16[4,128,512]{2,1,0:T(8,128)(2,1)}), bf16[4,128,512]{2,1,0:T(8,128)(2,1)S(1)}, u32[]{:S(2)}, u32[]{:S(2)}) async-start(bf16[4,128,512]{2,1,0:T(8,128)(2,1)} %broadcast_in_dim.3), calls=%async_computation.1 | async-start | bytes 1048576 | tf_op jit(solution)/shard_map/all_to_all | solution.py:243
  59.4 22.1 %collective-permute-start.5 = (bf16[2,256,512]{2,1,0:T(8,128)(2,1)}, bf16[2,256,512]{2,1,0:T(8,128)(2,1)}, u32[]{:S(2)}, u32[]{:S(2)}) collective-permute-start(bf16[2,256,512]{2,1,0:T(8,128)(2,1)} %get-tuple-element.22), channel_id=1, source_target_pairs={{0,1},{1,2},{2,3},{3,4},{4,5},{5,6},{6,7},{7,8},{8,9},{9,10},{10,1... | collective-permute-start | bytes 1572872 | tf_op jit(solution)/shard_map/ppermute | solution.py:203
  61.3 20.2 %collective-permute-start.6 = (bf16[2,256,512]{2,1,0:T(8,128)(2,1)}, bf16[2,256,512]{2,1,0:T(8,128)(2,1)}, u32[]{:S(2)}, u32[]{:S(2)}) collective-permute-start(bf16[2,256,512]{2,1,0:T(8,128)(2,1)} %get-tuple-element.23), channel_id=1, source_target_pairs={{1,0},{2,1},{3,2},{4,3},{5,4},{6,5},{7,6},{8,7},{9,8},{10,9},{11,1... | collective-permute-start | bytes 1572872 | tf_op jit(solution)/shard_map/ppermute | solution.py:203
  69.1 14.5 %collective-permute-start.3 = (bf16[256,512]{1,0:T(8,128)(2,1)S(1)}, bf16[256,512]{1,0:T(8,128)(2,1)S(1)}, u32[]{:S(2)}, u32[]{:S(2)}) collective-permute-start(bf16[256,512]{1,0:T(8,128)(2,1)S(1)} %bitcast.22), channel_id=1, source_target_pairs={{0,1},{1,2},{2,3},{3,4},{4,5},{5,6},{6,7},{7,8},{8,9},{9,10},{10,1... | collective-permute-start | bytes 786440 | tf_op jit(solution)/shard_map/ppermute | solution.py:203
  71.0 12.5 %collective-permute-start.4 = (bf16[256,512]{1,0:T(8,128)(2,1)S(1)}, bf16[256,512]{1,0:T(8,128)(2,1)S(1)}, u32[]{:S(2)}, u32[]{:S(2)}) collective-permute-start(bf16[256,512]{1,0:T(8,128)(2,1)S(1)} %bitcast.21), channel_id=1, source_target_pairs={{1,0},{2,1},{3,2},{4,3},{5,4},{6,5},{7,6},{8,7},{9,8},{10,9},{11,1... | collective-permute-start | bytes 786440 | tf_op jit(solution)/shard_map/ppermute | solution.py:203
  78.6 1.0 %copy-start.10 = (bf16[512,512]{1,0:T(8,128)(2,1)S(1)}, bf16[512,512]{1,0:T(8,128)(2,1)}, u32[]{:S(2)}) copy-start(bf16[512,512]{1,0:T(8,128)(2,1)} %copy-done.9) | copy-start | bytes 1572868
  79.6 3.9 %copy-start.8 = (bf16[512,512]{1,0:T(8,128)(2,1)S(1)}, bf16[512,512]{1,0:T(8,128)(2,1)}, u32[]{:S(2)}) copy-start(bf16[512,512]{1,0:T(8,128)(2,1)} %copy-done.7) | copy-start | bytes 1572868
  (1 other events, 0.7 us)

commit v2 on v1

v2 whole, which is shorter than its diff:
```python
import jax
import jax.numpy as jnp
from jax import lax
from jax.experimental import pallas as pl
from jax.experimental.pallas import tpu as pltpu
from jax.sharding import PartitionSpec as P

LEV = 64
ROWS = 8
LAT = 512
KMAX = 4
HALO = 4
MEMBERS = 2
XS = 4
PACK_PARTS = 4
OWN = LEV * ROWS
SIDE = LEV * HALO

VMEM_LIMIT = 16 * 2**20

BF = jnp.bfloat16
F32 = jnp.float32
VMEM = pl.BlockSpec(memory_space=pltpu.VMEM)
HBM = pl.BlockSpec(memory_space=pltpu.HBM)

BAND = {
    1: {1: 0.5},
    2: {0: 0.5, 2: 0.25},
    3: {1: 0.375, 3: 0.125},
    4: {0: 0.375, 2: 0.25, 4: 0.0625},
}


def in_hbm(x):
    return pltpu.with_memory_space_constraint(x, pltpu.HBM)


def call(kernel, out, operands, specs, flops, moved, scratch=()):
    return pl.pallas_call(
        kernel,
        out_shape=out,
        in_specs=specs,
        out_specs=jax.tree.map(lambda _: VMEM, out),
        scratch_shapes=scratch,
        compiler_params=pltpu.CompilerParams(vmem_limit_bytes=VMEM_LIMIT),
        cost_estimate=pl.CostEstimate(flops=flops, bytes_accessed=moved, transcendentals=0),
    )(*(in_hbm(x) if spec is HBM else x for x, spec in zip(operands, specs)))


def halves(x):
    rows, columns = x.shape
    x = x.reshape(rows // (2 * ROWS), 2, ROWS, columns)
    even, odd = x[:, 0], x[:, 1]
    low = lax.broadcasted_iota(jnp.int32, even.shape, 1) < HALO
    top = jnp.where(low, even, pltpu.roll(odd, HALO, 1))
    bottom = jnp.where(low, pltpu.roll(even, HALO, 1), odd)
    return top.reshape(rows // 2, columns), bottom.reshape(rows // 2, columns)


def odd_place():
    return lax.rem(lax.axis_index("lon"), 2) == 1


def pack_into(odd, x, outer_ref, inner_ref, at):
    top, bottom = halves(x.astype(F32))
    outer_ref[at] = jnp.where(odd, bottom, top).astype(BF)
    inner_ref[at] = jnp.where(odd, top, bottom).astype(BF)


def pack_kernel(x_ref, outer_ref, inner_ref, x, sems):
    odd = odd_place()
    part = OWN // PACK_PARTS
    copies = []
    for i in range(MEMBERS * PACK_PARTS):
        rows = (i // PACK_PARTS, pl.ds(i % PACK_PARTS * part, part))
        copies.append(pltpu.make_async_copy(x_ref.at[rows], x.at[rows], sems.at[i]))
        copies[-1].start()
    for i, copy in enumerate(copies):
        copy.wait()
        m, p = i // PACK_PARTS, i % PACK_PARTS
        pack_into(odd, x[m, pl.ds(p * part, part)], outer_ref, inner_ref, (m, pl.ds(p * part // 2, part // 2)))


def half_like(members):
    return jax.ShapeDtypeStruct((members, SIDE, LAT), BF)


def weights(n, distance):
    total = jnp.zeros(distance.shape, F32)
    for sweeps, band in BAND.items():
        row = jnp.zeros(distance.shape, F32)
        for d, c in band.items():
            row = jnp.where(jnp.abs(distance) == d, jnp.float32(c), row)
        total = jnp.where(n == sweeps, row, total)
    return total


def spread_lanes(width, per):
    level = lax.broadcasted_iota(jnp.int32, (LEV, width), 0)
    lane = lax.broadcasted_iota(jnp.int32, (LEV, width), 1)
    return jnp.where(level == lane // per, F32(1.0), F32(0.0)).astype(BF)


def side_distance(odd):
    row = lax.broadcasted_iota(jnp.int32, (ROWS, 2 * SIDE), 0)
    lane = lax.broadcasted_iota(jnp.int32, (ROWS, 2 * SIDE), 1)
    left = (lane < SIDE) != odd
    place = jnp.where(left, lane % HALO - HALO, lane % HALO + ROWS)
    return place - row


def own_distance():
    row = lax.broadcasted_iota(jnp.int32, (ROWS, OWN), 0)
    lane = lax.broadcasted_iota(jnp.int32, (ROWS, OWN), 1)
    return lane % ROWS - row


def first_kernel(
    group_hbm, weight_hbm, steps_hbm, steps_row_hbm, vert_hbm, lat_hbm, control_hbm, perturb_hbm,
    precision_hbm, innovation_hbm,
    side_ref, back_own_ref, back_side_ref, partial_ref, p_outer_ref, p_inner_ref,
    lat_ref, control_ref, weighted_ref, scale_ref, precision_ref, innovation_ref,
    table, group_ref, weight_ref, steps_ref, steps_row_ref, vert_ref, perturb_ref, sems,
):
    odd = odd_place()
    quarter = precision_ref.shape[0]
    start = pl.multiple_of(lax.rem(lax.axis_index("mem"), XS) * quarter, quarter)
    moves = [
        (vert_hbm, vert_ref),
        (steps_row_hbm, steps_row_ref),
        (steps_hbm, steps_ref),
        (group_hbm, group_ref),
        (weight_hbm, weight_ref),
        (control_hbm, control_ref),
        (lat_hbm, lat_ref),
        (perturb_hbm, perturb_ref),
        (precision_hbm.at[pl.ds(start, quarter)], precision_ref),
        (innovation_hbm.at[pl.ds(start, quarter)], innovation_ref),
    ]
    copies = [pltpu.make_async_copy(a, b, sems.at[i]) for i, (a, b) in enumerate(moves)]
    for copy in copies:
        copy.start()
    for copy in copies[:5]:
        copy.wait()

    vert = vert_ref[...].astype(BF)
    steps_row = steps_row_ref[...].astype(F32).astype(BF)
    lanes_own = spread_lanes(OWN, ROWS)
    lanes_half = spread_lanes(SIDE, HALO)
    lanes_side = jnp.concatenate([lanes_half, lanes_half], axis=1)

    def expand(matrix, lanes, dims=(((1,), (0,)), ((), ()))):
        return lax.dot_general(matrix, lanes, dims, preferred_element_type=F32)

    def forward(lanes, distance):
        n = expand(steps_row, lanes)
        wide = expand(vert, lanes)
        band = weights(n, distance)
        return (wide[:, None, :] * band[None]).reshape(OWN, OWN).astype(BF)

    side_ref[...] = forward(lanes_side, side_distance(odd))
    own = forward(lanes_own, own_distance())

    first_dim = (((0,), (0,)), ((), ()))
    for lanes, distance, out_ref in (
        (lanes_own, own_distance(), back_own_ref),
        (lanes_side, side_distance(odd), back_side_ref),
    ):
        wide = expand(vert, lanes, first_dim)
        for n in range(1, KMAX + 1):
            table[n - 1] = weights(n, distance)
        for l in range(0, LEV, 2):
            pair = [wide[l + i : l + i + 1] * table[steps_ref[l + i] - 1] for i in range(2)]
            out_ref[pl.ds(l * ROWS, 2 * ROWS), :] = jnp.concatenate(pair, axis=0).astype(BF)

    for copy in copies[5:]:
        copy.wait()
    total = jnp.zeros((OWN, LAT), F32)
    for m in range(MEMBERS):
        pack_into(odd, perturb_ref[m], p_outer_ref, p_inner_ref, m)
        weight = weight_ref[group_ref[m]]
        scale_ref[m] = jnp.full((ROWS, LAT), weight)
        weighted = weight * perturb_ref[m].astype(F32)
        weighted_ref[m] = weighted
        mixed = jnp.dot(own, control_ref[m], preferred_element_type=F32).astype(BF)
        total += weighted * jnp.dot(mixed, lat_ref[...], preferred_element_type=F32)
    partial_ref[...] = total


def forward_kernel(side_ref, lat_ref, outer_ref, inner_ref, weighted_ref, partial_ref, out_ref):
    total = partial_ref[...]
    for m in range(MEMBERS):
        mixed = jnp.dot(side_ref[:, :SIDE], outer_ref[m], preferred_element_type=F32)
        mixed += jnp.dot(side_ref[:, SIDE:], inner_ref[m], preferred_element_type=F32)
        local = jnp.dot(mixed.astype(BF), lat_ref[...], preferred_element_type=F32)
        total += weighted_ref[m] * local
    out_ref[...] = total.astype(BF)


def misfit_kernel(some_ref, other_ref, precision_ref, innovation_ref, out_ref):
    increment = some_ref[...].astype(F32) + other_ref[...].astype(F32)
    departure = increment - innovation_ref[...].astype(F32)
    misfit = (precision_ref[...].astype(F32) * departure).astype(BF)
    for j in range(XS):
        out_ref[j] = misfit


def edge_kernel(misfit_ref, outer_ref, inner_ref):
    pack_into(odd_place(), misfit_ref[...], outer_ref, inner_ref, ...)


def sum_kernel(parts_ref, out_ref):
    out_ref[...] = jnp.sum(parts_ref[...].astype(F32), axis=0).astype(BF)


LAST = (((1,), (1,)), ((), ()))


def back_own_kernel(back_own_ref, lat_ref, misfit_ref, weighted_ref, control_ref, out_ref):
    misfit = misfit_ref[...].astype(F32)
    for m in range(MEMBERS):
        back = (weighted_ref[m] * misfit).astype(BF)
        mixed = jnp.dot(back_own_ref[...], back, preferred_element_type=F32).astype(BF)
        latback = lax.dot_general(mixed, lat_ref[...], LAST, preferred_element_type=F32)
        out_ref[m] = control_ref[m].astype(F32) + latback


def back_side_kernel(
    back_side_ref, lat_ref, outer_ref, inner_ref, p_outer_ref, p_inner_ref, scale_ref, base_ref,
    out_hbm, out, sems,
):
    def back(m, p_ref, misfit_ref):
        p = p_ref[m].astype(F32).reshape(SIDE // ROWS, ROWS, LAT)
        weighted = (scale_ref[m][None] * p).reshape(SIDE, LAT)
        return (weighted * misfit_ref[...].astype(F32)).astype(BF)

    half = OWN // 2
    copies = []
    for m in range(MEMBERS):
        from_outer = back(m, p_outer_ref, outer_ref)
        from_inner = back(m, p_inner_ref, inner_ref)
        for h in range(2):
            rows = pl.ds(h * half, half)
            mixed = jnp.dot(back_side_ref[rows, :SIDE], from_outer, preferred_element_type=F32)
            mixed += jnp.dot(back_side_ref[rows, SIDE:], from_inner, preferred_element_type=F32)
            latback = lax.dot_general(
                mixed.astype(BF), lat_ref[...], LAST, preferred_element_type=F32
            )
            out[m, rows, :] = (base_ref[m, rows, :] + latback).astype(BF)
            copy = pltpu.make_async_copy(
                out.at[m, rows], out_hbm.at[m, rows], sems.at[2 * m + h]
            )
            copy.start()
            copies.append(copy)
    for copy in copies:
        copy.wait()


def shards(
    control,
    perturb,
    member_group,
    group_weight,
    step_counts,
    lat_inverse,
    vert_inverse,
    innovation,
    precision,
):
    lons = lax.axis_size("lon")
    within = [(i, i + 1 - 2 * (i % 2)) for i in range(lons)]
    beyond = [(i, (i - 1 + 2 * (i % 2)) % lons) for i in range(lons)]
    mems = lax.axis_size("mem")
    along_x = [list(range(i, i + XS)) for i in range(0, mems, XS)]
    across_y = [(i, (i + XS) % mems) for i in range(mems)]

    def halo(outer, inner):
        from_inner = lax.ppermute(inner, "lon", within)
        return lax.ppermute(outer, "lon", beyond), from_inner

    control = control.reshape(MEMBERS, OWN, LAT)
    perturb = perturb.reshape(MEMBERS, OWN, LAT)
    square = OWN * LAT
    matmul = 2 * OWN * LAT * LAT
    quarter = OWN // XS

    c_outer, c_inner = halo(
        *call(
            pack_kernel, (half_like(MEMBERS),) * 2, (control,), [HBM], 0, 8 * square,
            (pltpu.VMEM((MEMBERS, OWN, LAT), BF), pltpu.SemaphoreType.DMA((MEMBERS * PACK_PARTS,))),
        )
    )
    (
        side, back_own, back_side, partial, p_outer, p_inner, lat, control, weighted, scale, prec,
        innov,
    ) = call(
        first_kernel,
        (
            jax.ShapeDtypeStruct((OWN, 2 * SIDE), BF),
            jax.ShapeDtypeStruct((OWN, OWN), BF),
            jax.ShapeDtypeStruct((OWN, 2 * SIDE), BF),
            jax.ShapeDtypeStruct((OWN, LAT), F32),
            half_like(MEMBERS),
            half_like(MEMBERS),
            jax.ShapeDtypeStruct(lat_inverse.shape, BF),
            jax.ShapeDtypeStruct(control.shape, BF),
            jax.ShapeDtypeStruct(perturb.shape, F32),
            jax.ShapeDtypeStruct((MEMBERS, ROWS, LAT), F32),
            jax.ShapeDtypeStruct((quarter, LAT), BF),
            jax.ShapeDtypeStruct((quarter, LAT), BF),
        ),
        (member_group, group_weight, step_counts, step_counts.reshape(1, LEV), vert_inverse,
         lat_inverse, control, perturb, precision.reshape(OWN, LAT), innovation.reshape(OWN, LAT)),
        [HBM] * 10,
        4 * matmul, 20 * square,
        (
            pltpu.VMEM((KMAX, ROWS, OWN), F32),
            pltpu.SMEM(member_group.shape, jnp.int32),
            pltpu.SMEM(group_weight.shape, F32),
            pltpu.SMEM(step_counts.shape, jnp.int32),
            pltpu.VMEM((1, LEV), jnp.int32),
            pltpu.VMEM(vert_inverse.shape, F32),
            pltpu.VMEM(perturb.shape, BF),
            pltpu.SemaphoreType.DMA((10,)),
        ),
    )
    p_outer, p_inner = halo(p_outer, p_inner)
    partial = call(
        forward_kernel,
        jax.ShapeDtypeStruct((OWN, LAT), BF),
        (side, lat, c_outer, c_inner, weighted, partial),
        [VMEM] * 6,
        4 * matmul, 18 * square,
    )

    parts = lax.all_to_all(
        partial.reshape(XS, quarter, LAT), "mem", 0, 0, axis_index_groups=along_x
    )
    some = call(
        sum_kernel, jax.ShapeDtypeStruct((quarter, LAT), BF), (parts,), [VMEM], 0, 2 * square
    )
    some, p_outer, p_inner = lax.optimization_barrier((some, p_outer, p_inner))
    other = lax.ppermute(some, "mem", across_y)
    misfit = call(
        misfit_kernel,
        jax.ShapeDtypeStruct((XS, quarter, LAT), BF),
        (some, other, prec, innov),
        [VMEM] * 4,
        0, 2 * square,
    )
    misfit = lax.all_to_all(misfit, "mem", 0, 0, axis_index_groups=along_x).reshape(OWN, LAT)

    edge = jax.ShapeDtypeStruct((SIDE, LAT), BF)
    m_outer, m_inner = halo(*call(edge_kernel, (edge, edge), (misfit,), [VMEM], 0, 4 * square))
    base = call(
        back_own_kernel,
        jax.ShapeDtypeStruct((MEMBERS, OWN, LAT), F32),
        (back_own, lat, misfit, weighted, control),
        [VMEM] * 5,
        4 * matmul, 18 * square,
    )
    out = pl.pallas_call(
        back_side_kernel,
        out_shape=jax.ShapeDtypeStruct((MEMBERS, OWN, LAT), BF),
        in_specs=[VMEM] * 8,
        out_specs=HBM,
        scratch_shapes=(
            pltpu.VMEM((MEMBERS, OWN, LAT), BF),
            pltpu.SemaphoreType.DMA((2 * MEMBERS,)),
        ),
        compiler_params=pltpu.CompilerParams(vmem_limit_bytes=VMEM_LIMIT),
        cost_estimate=pl.CostEstimate(
            flops=4 * matmul, bytes_accessed=20 * square, transcendentals=0
        ),
    )(back_side, lat, m_outer, m_inner, p_outer, p_inner, scale, base)
    return out.reshape(MEMBERS, LEV, ROWS, LAT)


def solution(mesh):
    return jax.shard_map(
        shards,
        mesh=mesh,
        in_specs=(
            P("mem", None, "lon", None),
            P("mem", None, "lon", None),
            P("mem"),
            P(),
            P(),
            P(),
            P(),
            P(None, "lon", None),
            P(None, "lon", None),
        ),
        out_specs=P("mem", None, "lon", None),
        check_vma=False,
    )
```

time: 87.8 us -> 77.4 us (0.88)
  starting transfers between devices: 44.3 us -> 31.1 us
  blocking collectives: 11.3 us -> 22.3 us
  local copies, waits for them, and re-layouts: 10.9 us -> 0 us
  waiting for transfers between devices: 7.76 us -> 13.2 us
  other arithmetic: 1.14 us -> 0 us
  Pallas kernels: 11.4 us -> 10.3 us
    all_to_all x0 -> x1, blocking collectives: none -> 10.5 us  [shards(): lax.all_to_all(misfit, 'mem', 0, 0, axis_index_groups=along_x)]
    unnamed x34 -> x0, local copies, waits for them, and re-layouts: 10.1 us -> none
    ppermute x6, starting transfers between devices: 34.3 us -> 25.3 us  [the longest x3 19.2 us: halo(): return (lax.ppermute(outer, 'lon', beyond), from_inner)]
    ppermute x6, waiting for transfers between devices: 2.01 us -> 8.27 us  [the longest x3 8.26 us: halo(): return (lax.ppermute(outer, 'lon', beyond), from_inner)]
    all_to_all x1 -> x0, starting transfers between devices: 4.9 us -> none  [shards(): lax.all_to_all(jnp.broadcast_to(misfit, (XS, quarter, LAT)), 'mem', 0, 0,...]
    pallas_call x7, Pallas kernels: 11.4 us -> 7.89 us  [call(): pl.pallas_call(kernel, out_shape=out, in_specs=specs, out_specs=jax.tree....]
    pallas_call x0 -> x1, Pallas kernels: none -> 2.37 us  [shards(): pl.pallas_call(back_side_kernel, out_shape=jax.ShapeDtypeStruct((MEMBERS,...]
    convert_element_type x1 -> x0, other arithmetic: 1.06 us -> none  [shards(): misfit = (prec.astype(F32) * (increment - innov.astype(F32))).astype(BF)]
  transfers between devices with their start and end apart: 8 -> 7, of which waited for: 2 -> 3; matrix products, arithmetic and copies ran while one was open for 0% -> 0% of each run, Pallas kernels for 6% -> 8%
where the time goes in v2:
time: 77.4 us; the launch traced here: 77 us
  starting transfers between devices  31.1 us (40%)
  blocking collectives  22.3 us (29%)
  waiting for transfers between devices  13.2 us (17%)
  Pallas kernels  10.3 us (13%)
    ppermute x3, starting transfers between devices, halo(): return (lax.ppermute(outer, 'lon', beyond), from_inner)  19.2 us
    all_to_all x1, blocking collectives, shards(): lax.all_to_all(partial.reshape(XS, quarter, LAT), 'mem', 0, 0, axis_index...  11.8 us
    all_to_all x1, blocking collectives, shards(): lax.all_to_all(misfit, 'mem', 0, 0, axis_index_groups=along_x)  10.5 us
    ppermute x3, waiting for transfers between devices, halo(): return (lax.ppermute(outer, 'lon', beyond), from_inner)  8.26 us
    pallas_call x7, Pallas kernels, call(): pl.pallas_call(kernel, out_shape=out, in_specs=specs, out_specs=jax.tree....  7.89 us
    ppermute x3, starting transfers between devices, halo(): from_inner = lax.ppermute(inner, 'lon', within)  6.13 us
    ppermute x1, starting transfers between devices, shards(): other = lax.ppermute(some, 'mem', across_y)  5.81 us
    ppermute x1, waiting for transfers between devices, shards(): other = lax.ppermute(some, 'mem', across_y)  4.95 us
  transfers between devices with their start and end apart: 7, of which 3 were waited for; matrix products, arithmetic and copies ran while one was open for 0% of the time, Pallas kernels for 8%

profile of v2, /device:TPU:2, one launch (start us, length us, event | category | flops | bytes accessed | tf_op | source)
XLA Modules:
  0.0 77.0 jit_solution(6846456590838355998)
XLA Ops:
  0.0 1.4 %shard_map.92 = (bf16[2,256,512]{2,1,0:T(8,128)(2,1)S(1)}, bf16[2,256,512]{2,1,0:T(8,128)(2,1)S(1)}) custom-call(bf16[2,512,512]{2,1,0:T(8,128)(2,1)} %bitcast.11), custom_call_target="tpu_custom_call" | custom-call | bytes 2097152 | tf_op jit(solution)/shard_map/pallas_call | solution.py:39
  1.4 13.4 %collective-permute-start = (bf16[2,256,512]{2,1,0:T(8,128)(2,1)S(1)}, bf16[2,256,512]{2,1,0:T(8,128)(2,1)S(1)}, u32[]{:S(2)}, u32[]{:S(2)}) collective-permute-start(bf16[2,256,512]{2,1,0:T(8,128)(2,1)S(1)} %get-tuple-element.27), channel_id=1, source_target_pairs={{0,63},{1,2},{2,1},{3,4},{4,3},{5,6},{6,5},{7,8},{8,7},{9,10},{10,... | collective-permute-start | bytes 1572872 | tf_op jit(solution)/shard_map/ppermute | solution.py:279
  14.8 1.9 %collective-permute-start.1 = (bf16[2,256,512]{2,1,0:T(8,128)(2,1)S(1)}, bf16[2,256,512]{2,1,0:T(8,128)(2,1)S(1)}, u32[]{:S(2)}, u32[]{:S(2)}) collective-permute-start(bf16[2,256,512]{2,1,0:T(8,128)(2,1)S(1)} %get-tuple-element.28), channel_id=1, source_target_pairs={{0,1},{1,0},{2,3},{3,2},{4,5},{5,4},{6,7},{7,6},{8,9},{9,8},{10,11... | collective-permute-start | bytes 1572872 | tf_op jit(solution)/shard_map/ppermute | solution.py:278
  16.8 3.6 %shard_map.91 = (bf16[512,512]{1,0:T(8,128)(2,1)S(1)}, bf16[512,512]{1,0:T(8,128)(2,1)S(1)}, bf16[512,512]{1,0:T(8,128)(2,1)S(1)}, f32[512,512]{1,0:T(8,128)S(1)...) custom-call(s32[2]{0:T(128)} %group_hbm.1, ...), custom_call_target="tpu_custom_call" | custom-call | flops 1073741824 | bytes 5242880 | tf_op jit(solution)/shard_map/pallas_call | solution.py:39
  20.4 2.6 %collective-permute-start.2 = (bf16[2,256,512]{2,1,0:T(8,128)(2,1)S(1)}, bf16[2,256,512]{2,1,0:T(8,128)(2,1)S(1)}, u32[]{:S(2)}, u32[]{:S(2)}) collective-permute-start(bf16[2,256,512]{2,1,0:T(8,128)(2,1)S(1)} %get-tuple-element.31), channel_id=1, source_target_pairs={{0,63},{1,2},{2,1},{3,4},{4,3},{5,6},{6,5},{7,8},{8,7},{9,10},{10,... | collective-permute-start | bytes 1572872 | tf_op jit(solution)/shard_map/ppermute | solution.py:279
  23.0 1.9 %collective-permute-start.3 = (bf16[2,256,512]{2,1,0:T(8,128)(2,1)S(1)}, bf16[2,256,512]{2,1,0:T(8,128)(2,1)S(1)}, u32[]{:S(2)}, u32[]{:S(2)}) collective-permute-start(bf16[2,256,512]{2,1,0:T(8,128)(2,1)S(1)} %get-tuple-element.32), channel_id=1, source_target_pairs={{0,1},{1,0},{2,3},{3,2},{4,5},{5,4},{6,7},{7,6},{8,9},{9,8},{10,11... | collective-permute-start | bytes 1572872 | tf_op jit(solution)/shard_map/ppermute | solution.py:278
  24.9 1.6 %collective-permute-done.outer_ref = bf16[2,256,512]{2,1,0:T(8,128)(2,1)S(1)} collective-permute-done((bf16[2,256,512]{2,1,0:T(8,128)(2,1)S(1)}, bf16[2,256,512]{2,1,0:T(8,128)(2,1)S(1)}, u32[]{:S(2)}, u32[]{:S(2)}) %collective-permute-start) | collective-permute-done | bytes 524320 | tf_op jit(solution)/shard_map/ppermute | solution.py:279
  26.5 0.0 collective-permute-done.1.inner_ref
  26.5 1.3 %shard_map.93 = bf16[512,512]{1,0:T(8,128)(2,1)S(1)} custom-call(bf16[512,512]{1,0:T(8,128)(2,1)S(1)} %get-tuple-element.26.side_ref, bf16[512,512]{1,0:T(8,128)(2,1)S(1)} %get-tuple-element.25.lat_ref, bf16[2,256,512]{2,1,0:T(8,128)(2,1)S(1)} %collective-permute-done.outer_ref, bf16[2,256,512]{2,1,0:T(8,128)(2,1)S(1)} %collective-permute-done.1.inner_ref, ...), custom_call_target="tpu_custom_call" | custom-call | flops 1073741824 | bytes 4718592 | tf_op jit(solution)/shard_map/pallas_call | solution.py:39
  27.8 11.8 %all_to_all.10.parts_ref = bf16[4,128,512]{2,1,0:T(8,128)(2,1)S(1)} all-to-all(bf16[4,128,512]{2,1,0:T(8,128)(2,1)S(1)} %bitcast.10), channel_id=1, replica_groups={{0,64,128,192},{256,320,384,448},{1,65,129,193},{257,321,385,449},{2,66..., dimensions={0} | all-to-all | bytes 1048576 | tf_op jit(solution)/shard_map/all_to_all | solution.py:336
  39.5 0.1 shard_map.94.some_ref
  39.6 0.0 collective-permute-done.2.p_outer_ref
  39.6 0.0 collective-permute-done.3.p_inner_ref
  39.6 5.8 %collective-permute-start.4 = (bf16[128,512]{1,0:T(8,128)(2,1)S(1)}, bf16[128,512]{1,0:T(8,128)(2,1)S(1)}, u32[]{:S(2)}, u32[]{:S(2)}) collective-permute-start(bf16[128,512]{1,0:T(8,128)(2,1)S(1)} %shard_map.94.some_ref), channel_id=1, source_target_pairs={{0,256},{64,320},{128,384},{192,448},{256,0},{320,64},{384,128},{4... | collective-permute-start | bytes 393224 | tf_op jit(solution)/shard_map/ppermute | solution.py:343
  45.5 4.9 %collective-permute-done.4.other_ref = bf16[128,512]{1,0:T(8,128)(2,1)S(1)} collective-permute-done((bf16[128,512]{1,0:T(8,128)(2,1)S(1)}, bf16[128,512]{1,0:T(8,128)(2,1)S(1)}, u32[]{:S(2)}, u32[]{:S(2)}) %collective-permute-start.4) | collective-permute-done | bytes 131104 | tf_op jit(solution)/shard_map/ppermute | solution.py:343
  50.4 0.1 shard_map.95
  50.5 10.5 %all_to_all.11 = bf16[4,128,512]{2,1,0:T(8,128)(2,1)S(1)} all-to-all(bf16[4,128,512]{2,1,0:T(8,128)(2,1)S(1)} %shard_map.95), channel_id=1, replica_groups={{0,64,128,192},{256,320,384,448},{1,65,129,193},{257,321,385,449},{2,66..., dimensions={0} | all-to-all | bytes 1048576 | tf_op jit(solution)/shard_map/all_to_all | solution.py:351
  61.0 0.2 shard_map.96
  61.1 3.2 %collective-permute-start.5 = (bf16[256,512]{1,0:T(8,128)(2,1)S(1)}, bf16[256,512]{1,0:T(8,128)(2,1)S(1)}, u32[]{:S(2)}, u32[]{:S(2)}) collective-permute-start(bf16[256,512]{1,0:T(8,128)(2,1)S(1)} %get-tuple-element.36), channel_id=1, source_target_pairs={{0,63},{1,2},{2,1},{3,4},{4,3},{5,6},{6,5},{7,8},{8,7},{9,10},{10,... | collective-permute-start | bytes 786440 | tf_op jit(solution)/shard_map/ppermute | solution.py:279
  64.3 2.3 %collective-permute-start.6 = (bf16[256,512]{1,0:T(8,128)(2,1)S(1)}, bf16[256,512]{1,0:T(8,128)(2,1)S(1)}, u32[]{:S(2)}, u32[]{:S(2)}) collective-permute-start(bf16[256,512]{1,0:T(8,128)(2,1)S(1)} %get-tuple-element.37), channel_id=1, source_target_pairs={{0,1},{1,0},{2,3},{3,2},{4,5},{5,4},{6,7},{7,6},{8,9},{9,8},{10,11... | collective-permute-start | bytes 786440 | tf_op jit(solution)/shard_map/ppermute | solution.py:278
  66.6 1.3 %shard_map.97.base_ref = f32[2,512,512]{2,1,0:T(8,128)S(1)} custom-call(bf16[512,512]{1,0:T(8,128)(2,1)S(1)} %get-tuple-element.41.back_own_ref, bf16[512,512]{1,0:T(8,128)(2,1)S(1)} %get-tuple-element.25.lat_ref, bf16[512,512]{1,0:T(8,128)(2,1)S(1)} %bitcast.9, f32[2,512,512]{2,1,0:T(8,128)S(1)} %get-tuple-element.29.weighted_ref, ...), custom_call_target="tpu_custom_call" | custom-call | flops 1073741824 | bytes 4718592 | tf_op jit(solution)/shard_map/pallas_call | solution.py:39
  67.9 6.7 %collective-permute-done.5.outer_ref = bf16[256,512]{1,0:T(8,128)(2,1)S(1)} collective-permute-done((bf16[256,512]{1,0:T(8,128)(2,1)S(1)}, bf16[256,512]{1,0:T(8,128)(2,1)S(1)}, u32[]{:S(2)}, u32[]{:S(2)}) %collective-permute-start.5) | collective-permute-done | bytes 262176 | tf_op jit(solution)/shard_map/ppermute | solution.py:279
  74.6 0.0 collective-permute-done.6.inner_ref
  74.6 2.4 %shard_map.98 = bf16[2,512,512]{2,1,0:T(8,128)(2,1)} custom-call(bf16[512,512]{1,0:T(8,128)(2,1)S(1)} %get-tuple-element.24.back_side_ref, bf16[512,512]{1,0:T(8,128)(2,1)S(1)} %get-tuple-element.25.lat_ref, bf16[256,512]{1,0:T(8,128)(2,1)S(1)} %collective-permute-done.5.outer_ref, bf16[256,512]{1,0:T(8,128)(2,1)S(1)} %collective-permute-done.6.inner_ref, ...), custom_call_target="tpu_custom_call" | custom-call | flops 1073741824 | bytes 5242880 | tf_op jit(solution)/shard_map/pallas_call | solution.py:362
Async XLA Ops:
  1.4 25.1 %collective-permute-start = (bf16[2,256,512]{2,1,0:T(8,128)(2,1)S(1)}, bf16[2,256,512]{2,1,0:T(8,128)(2,1)S(1)}, u32[]{:S(2)}, u32[]{:S(2)}) collective-permute-start(bf16[2,256,512]{2,1,0:T(8,128)(2,1)S(1)} %get-tuple-element.27), channel_id=1, source_target_pairs={{0,63},{1,2},{2,1},{3,4},{4,3},{5,6},{6,5},{7,8},{8,7},{9,10},{10,... | collective-permute-start | bytes 1572872 | tf_op jit(solution)/shard_map/ppermute | solution.py:279
  14.8 11.6 %collective-permute-start.1 = (bf16[2,256,512]{2,1,0:T(8,128)(2,1)S(1)}, bf16[2,256,512]{2,1,0:T(8,128)(2,1)S(1)}, u32[]{:S(2)}, u32[]{:S(2)}) collective-permute-start(bf16[2,256,512]{2,1,0:T(8,128)(2,1)S(1)} %get-tuple-element.28), channel_id=1, source_target_pairs={{0,1},{1,0},{2,3},{3,2},{4,5},{5,4},{6,7},{7,6},{8,9},{9,8},{10,11... | collective-permute-start | bytes 1572872 | tf_op jit(solution)/shard_map/ppermute | solution.py:278
  20.4 19.2 %collective-permute-start.2 = (bf16[2,256,512]{2,1,0:T(8,128)(2,1)S(1)}, bf16[2,256,512]{2,1,0:T(8,128)(2,1)S(1)}, u32[]{:S(2)}, u32[]{:S(2)}) collective-permute-start(bf16[2,256,512]{2,1,0:T(8,128)(2,1)S(1)} %get-tuple-element.31), channel_id=1, source_target_pairs={{0,63},{1,2},{2,1},{3,4},{4,3},{5,6},{6,5},{7,8},{8,7},{9,10},{10,... | collective-permute-start | bytes 1572872 | tf_op jit(solution)/shard_map/ppermute | solution.py:279
  23.0 16.6 %collective-permute-start.3 = (bf16[2,256,512]{2,1,0:T(8,128)(2,1)S(1)}, bf16[2,256,512]{2,1,0:T(8,128)(2,1)S(1)}, u32[]{:S(2)}, u32[]{:S(2)}) collective-permute-start(bf16[2,256,512]{2,1,0:T(8,128)(2,1)S(1)} %get-tuple-element.32), channel_id=1, source_target_pairs={{0,1},{1,0},{2,3},{3,2},{4,5},{5,4},{6,7},{7,6},{8,9},{9,8},{10,11... | collective-permute-start | bytes 1572872 | tf_op jit(solution)/shard_map/ppermute | solution.py:278
  39.6 10.8 %collective-permute-start.4 = (bf16[128,512]{1,0:T(8,128)(2,1)S(1)}, bf16[128,512]{1,0:T(8,128)(2,1)S(1)}, u32[]{:S(2)}, u32[]{:S(2)}) collective-permute-start(bf16[128,512]{1,0:T(8,128)(2,1)S(1)} %shard_map.94.some_ref), channel_id=1, source_target_pairs={{0,256},{64,320},{128,384},{192,448},{256,0},{320,64},{384,128},{4... | collective-permute-start | bytes 393224 | tf_op jit(solution)/shard_map/ppermute | solution.py:343
  61.1 13.5 %collective-permute-start.5 = (bf16[256,512]{1,0:T(8,128)(2,1)S(1)}, bf16[256,512]{1,0:T(8,128)(2,1)S(1)}, u32[]{:S(2)}, u32[]{:S(2)}) collective-permute-start(bf16[256,512]{1,0:T(8,128)(2,1)S(1)} %get-tuple-element.36), channel_id=1, source_target_pairs={{0,63},{1,2},{2,1},{3,4},{4,3},{5,6},{6,5},{7,8},{8,7},{9,10},{10,... | collective-permute-start | bytes 786440 | tf_op jit(solution)/shard_map/ppermute | solution.py:279
  64.3 10.3 %collective-permute-start.6 = (bf16[256,512]{1,0:T(8,128)(2,1)S(1)}, bf16[256,512]{1,0:T(8,128)(2,1)S(1)}, u32[]{:S(2)}, u32[]{:S(2)}) collective-permute-start(bf16[256,512]{1,0:T(8,128)(2,1)S(1)} %get-tuple-element.37), channel_id=1, source_target_pairs={{0,1},{1,0},{2,3},{3,2},{4,5},{5,4},{6,7},{7,6},{8,9},{9,8},{10,11... | collective-permute-start | bytes 786440 | tf_op jit(solution)/shard_map/ppermute | solution.py:278

commit v3 on v2

--- a/solution.py
+++ b/solution.py
@@ -12,6 +12,7 @@
 HALO = 4
 MEMBERS = 2
 XS = 4
+YS = 4
 PACK_PARTS = 4
 OWN = LEV * ROWS
 SIDE = LEV * HALO
@@ -274,9 +275,20 @@
     along_x = [list(range(i, i + XS)) for i in range(0, mems, XS)]
     across_y = [(i, (i + XS) % mems) for i in range(mems)]
 
+    run = 2 * YS
+    across = [
+        (m * lons + i, (m if i // run == j // run else (m + XS) % mems) * lons + j)
+        for m in range(mems)
+        for i, j in beyond
+    ]
+
     def halo(outer, inner):
         from_inner = lax.ppermute(inner, "lon", within)
         return lax.ppermute(outer, "lon", beyond), from_inner
+
+    def misfit_halo(outer, inner):
+        from_inner = lax.ppermute(inner, "lon", within)
+        return lax.ppermute(outer, ("mem", "lon"), across), from_inner
 
     control = control.reshape(MEMBERS, OWN, LAT)
     perturb = perturb.reshape(MEMBERS, OWN, LAT)
@@ -351,7 +363,9 @@
     misfit = lax.all_to_all(misfit, "mem", 0, 0, axis_index_groups=along_x).reshape(OWN, LAT)
 
     edge = jax.ShapeDtypeStruct((SIDE, LAT), BF)
-    m_outer, m_inner = halo(*call(edge_kernel, (edge, edge), (misfit,), [VMEM], 0, 4 * square))
+    m_outer, m_inner = misfit_halo(
+        *call(edge_kernel, (edge, edge), (misfit,), [VMEM], 0, 4 * square)
+    )
     base = call(
         back_own_kernel,
         jax.ShapeDtypeStruct((MEMBERS, OWN, LAT), F32),

time: 77.4 us -> 74.9 us (0.968)
  waiting for transfers between devices: 13.2 us -> 9.04 us
  starting transfers between devices: 31.1 us -> 32.9 us
    ppermute x0 -> x2, starting transfers between devices: none -> 7.19 us  [the longest x1 5.27 us: misfit_halo(): return (lax.ppermute(outer, ('mem', 'lon'), across), from_inner)]
    ppermute x3 -> x2, waiting for transfers between devices: 8.26 us -> 1.56 us  [halo(): return (lax.ppermute(outer, 'lon', beyond), from_inner)]
    ppermute x3 -> x2, starting transfers between devices: 19.2 us -> 16 us  [halo(): return (lax.ppermute(outer, 'lon', beyond), from_inner)]
    ppermute x0 -> x2, waiting for transfers between devices: none -> 2.53 us  [the longest x1 2.52 us: misfit_halo(): return (lax.ppermute(outer, ('mem', 'lon'), across), from_inner)]
    ppermute x3 -> x2, starting transfers between devices: 6.13 us -> 3.84 us  [halo(): from_inner = lax.ppermute(inner, 'lon', within)]
where the time goes in v3:
time: 74.9 us; the launch traced here: 74.5 us
  starting transfers between devices  32.9 us (44%)
  blocking collectives  22.3 us (30%)
  Pallas kernels  10.3 us (14%)
  waiting for transfers between devices  9.04 us (12%)
    ppermute x2, starting transfers between devices, halo(): return (lax.ppermute(outer, 'lon', beyond), from_inner)  16 us
    all_to_all x1, blocking collectives, shards(): lax.all_to_all(partial.reshape(XS, quarter, LAT), 'mem', 0, 0, axis_index...  11.8 us
    all_to_all x1, blocking collectives, shards(): lax.all_to_all(misfit, 'mem', 0, 0, axis_index_groups=along_x)  10.5 us
    pallas_call x7, Pallas kernels, call(): pl.pallas_call(kernel, out_shape=out, in_specs=specs, out_specs=jax.tree....  7.89 us
    ppermute x1, starting transfers between devices, shards(): other = lax.ppermute(some, 'mem', across_y)  5.81 us
    ppermute x1, starting transfers between devices, misfit_halo(): return (lax.ppermute(outer, ('mem', 'lon'), across), from_inner)  5.27 us
    ppermute x1, waiting for transfers between devices, shards(): other = lax.ppermute(some, 'mem', across_y)  4.95 us
    ppermute x2, starting transfers between devices, halo(): from_inner = lax.ppermute(inner, 'lon', within)  3.84 us
  transfers between devices with their start and end apart: 7, of which 3 were waited for; matrix products, arithmetic and copies ran while one was open for 0% of the time, Pallas kernels for 8%

profile of v3, /device:TPU:2, one launch (start us, length us, event | category | flops | bytes accessed | tf_op | source)
XLA Modules:
  0.0 74.5 jit_solution(8568385531807290049)
XLA Ops:
  0.0 1.4 %shard_map.92 = (bf16[2,256,512]{2,1,0:T(8,128)(2,1)S(1)}, bf16[2,256,512]{2,1,0:T(8,128)(2,1)S(1)}) custom-call(bf16[2,512,512]{2,1,0:T(8,128)(2,1)} %bitcast.11), custom_call_target="tpu_custom_call" | custom-call | bytes 2097152 | tf_op jit(solution)/shard_map/pallas_call | solution.py:40
  1.4 13.4 %collective-permute-start = (bf16[2,256,512]{2,1,0:T(8,128)(2,1)S(1)}, bf16[2,256,512]{2,1,0:T(8,128)(2,1)S(1)}, u32[]{:S(2)}, u32[]{:S(2)}) collective-permute-start(bf16[2,256,512]{2,1,0:T(8,128)(2,1)S(1)} %get-tuple-element.27), channel_id=1, source_target_pairs={{0,63},{1,2},{2,1},{3,4},{4,3},{5,6},{6,5},{7,8},{8,7},{9,10},{10,... | collective-permute-start | bytes 1572872 | tf_op jit(solution)/shard_map/ppermute | solution.py:287
  14.8 1.9 %collective-permute-start.1 = (bf16[2,256,512]{2,1,0:T(8,128)(2,1)S(1)}, bf16[2,256,512]{2,1,0:T(8,128)(2,1)S(1)}, u32[]{:S(2)}, u32[]{:S(2)}) collective-permute-start(bf16[2,256,512]{2,1,0:T(8,128)(2,1)S(1)} %get-tuple-element.28), channel_id=1, source_target_pairs={{0,1},{1,0},{2,3},{3,2},{4,5},{5,4},{6,7},{7,6},{8,9},{9,8},{10,11... | collective-permute-start | bytes 1572872 | tf_op jit(solution)/shard_map/ppermute | solution.py:286
  16.8 3.6 %shard_map.91 = (bf16[512,512]{1,0:T(8,128)(2,1)S(1)}, bf16[512,512]{1,0:T(8,128)(2,1)S(1)}, bf16[512,512]{1,0:T(8,128)(2,1)S(1)}, f32[512,512]{1,0:T(8,128)S(1)...) custom-call(s32[2]{0:T(128)} %group_hbm.1, ...), custom_call_target="tpu_custom_call" | custom-call | flops 1073741824 | bytes 5242880 | tf_op jit(solution)/shard_map/pallas_call | solution.py:40
  20.4 2.6 %collective-permute-start.2 = (bf16[2,256,512]{2,1,0:T(8,128)(2,1)S(1)}, bf16[2,256,512]{2,1,0:T(8,128)(2,1)S(1)}, u32[]{:S(2)}, u32[]{:S(2)}) collective-permute-start(bf16[2,256,512]{2,1,0:T(8,128)(2,1)S(1)} %get-tuple-element.31), channel_id=1, source_target_pairs={{0,63},{1,2},{2,1},{3,4},{4,3},{5,6},{6,5},{7,8},{8,7},{9,10},{10,... | collective-permute-start | bytes 1572872 | tf_op jit(solution)/shard_map/ppermute | solution.py:287
  23.0 1.9 %collective-permute-start.3 = (bf16[2,256,512]{2,1,0:T(8,128)(2,1)S(1)}, bf16[2,256,512]{2,1,0:T(8,128)(2,1)S(1)}, u32[]{:S(2)}, u32[]{:S(2)}) collective-permute-start(bf16[2,256,512]{2,1,0:T(8,128)(2,1)S(1)} %get-tuple-element.32), channel_id=1, source_target_pairs={{0,1},{1,0},{2,3},{3,2},{4,5},{5,4},{6,7},{7,6},{8,9},{9,8},{10,11... | collective-permute-start | bytes 1572872 | tf_op jit(solution)/shard_map/ppermute | solution.py:286
  24.9 1.6 %collective-permute-done.outer_ref = bf16[2,256,512]{2,1,0:T(8,128)(2,1)S(1)} collective-permute-done((bf16[2,256,512]{2,1,0:T(8,128)(2,1)S(1)}, bf16[2,256,512]{2,1,0:T(8,128)(2,1)S(1)}, u32[]{:S(2)}, u32[]{:S(2)}) %collective-permute-start) | collective-permute-done | bytes 524320 | tf_op jit(solution)/shard_map/ppermute | solution.py:287
  26.5 0.0 collective-permute-done.1.inner_ref
  26.5 1.3 %shard_map.93 = bf16[512,512]{1,0:T(8,128)(2,1)S(1)} custom-call(bf16[512,512]{1,0:T(8,128)(2,1)S(1)} %get-tuple-element.26.side_ref, bf16[512,512]{1,0:T(8,128)(2,1)S(1)} %get-tuple-element.25.lat_ref, bf16[2,256,512]{2,1,0:T(8,128)(2,1)S(1)} %collective-permute-done.outer_ref, bf16[2,256,512]{2,1,0:T(8,128)(2,1)S(1)} %collective-permute-done.1.inner_ref, ...), custom_call_target="tpu_custom_call" | custom-call | flops 1073741824 | bytes 4718592 | tf_op jit(solution)/shard_map/pallas_call | solution.py:40
  27.8 11.8 %all_to_all.10.parts_ref = bf16[4,128,512]{2,1,0:T(8,128)(2,1)S(1)} all-to-all(bf16[4,128,512]{2,1,0:T(8,128)(2,1)S(1)} %bitcast.10), channel_id=1, replica_groups={{0,64,128,192},{256,320,384,448},{1,65,129,193},{257,321,385,449},{2,66..., dimensions={0} | all-to-all | bytes 1048576 | tf_op jit(solution)/shard_map/all_to_all | solution.py:348
  39.5 0.1 shard_map.94.some_ref
  39.6 0.0 collective-permute-done.2.p_outer_ref
  39.6 0.0 collective-permute-done.3.p_inner_ref
  39.6 5.8 %collective-permute-start.4 = (bf16[128,512]{1,0:T(8,128)(2,1)S(1)}, bf16[128,512]{1,0:T(8,128)(2,1)S(1)}, u32[]{:S(2)}, u32[]{:S(2)}) collective-permute-start(bf16[128,512]{1,0:T(8,128)(2,1)S(1)} %shard_map.94.some_ref), channel_id=1, source_target_pairs={{0,256},{64,320},{128,384},{192,448},{256,0},{320,64},{384,128},{4... | collective-permute-start | bytes 393224 | tf_op jit(solution)/shard_map/ppermute | solution.py:355
  45.5 4.9 %collective-permute-done.4.other_ref = bf16[128,512]{1,0:T(8,128)(2,1)S(1)} collective-permute-done((bf16[128,512]{1,0:T(8,128)(2,1)S(1)}, bf16[128,512]{1,0:T(8,128)(2,1)S(1)}, u32[]{:S(2)}, u32[]{:S(2)}) %collective-permute-start.4) | collective-permute-done | bytes 131104 | tf_op jit(solution)/shard_map/ppermute | solution.py:355
  50.4 0.1 shard_map.95
  50.5 10.5 %all_to_all.11 = bf16[4,128,512]{2,1,0:T(8,128)(2,1)S(1)} all-to-all(bf16[4,128,512]{2,1,0:T(8,128)(2,1)S(1)} %shard_map.95), channel_id=1, replica_groups={{0,64,128,192},{256,320,384,448},{1,65,129,193},{257,321,385,449},{2,66..., dimensions={0} | all-to-all | bytes 1048576 | tf_op jit(solution)/shard_map/all_to_all | solution.py:363
  61.0 0.2 shard_map.96
  61.1 5.3 %collective-permute-start.5 = (bf16[256,512]{1,0:T(8,128)(2,1)S(1)}, bf16[256,512]{1,0:T(8,128)(2,1)S(1)}, u32[]{:S(2)}, u32[]{:S(2)}) collective-permute-start(bf16[256,512]{1,0:T(8,128)(2,1)S(1)} %get-tuple-element.36), channel_id=1, source_target_pairs={{0,319},{1,2},{2,1},{3,4},{4,3},{5,6},{6,5},{7,264},{8,263},{9,10}... | collective-permute-start | bytes 786440 | tf_op jit(solution)/shard_map/ppermute | solution.py:291
  66.4 1.9 %collective-permute-start.6 = (bf16[256,512]{1,0:T(8,128)(2,1)S(1)}, bf16[256,512]{1,0:T(8,128)(2,1)S(1)}, u32[]{:S(2)}, u32[]{:S(2)}) collective-permute-start(bf16[256,512]{1,0:T(8,128)(2,1)S(1)} %get-tuple-element.37), channel_id=1, source_target_pairs={{0,1},{1,0},{2,3},{3,2},{4,5},{5,4},{6,7},{7,6},{8,9},{9,8},{10,11... | collective-permute-start | bytes 786440 | tf_op jit(solution)/shard_map/ppermute | solution.py:290
  68.3 1.3 %shard_map.97.base_ref = f32[2,512,512]{2,1,0:T(8,128)S(1)} custom-call(bf16[512,512]{1,0:T(8,128)(2,1)S(1)} %get-tuple-element.41.back_own_ref, bf16[512,512]{1,0:T(8,128)(2,1)S(1)} %get-tuple-element.25.lat_ref, bf16[512,512]{1,0:T(8,128)(2,1)S(1)} %bitcast.9, f32[2,512,512]{2,1,0:T(8,128)S(1)} %get-tuple-element.29.weighted_ref, ...), custom_call_target="tpu_custom_call" | custom-call | flops 1073741824 | bytes 4718592 | tf_op jit(solution)/shard_map/pallas_call | solution.py:40
  69.6 2.5 %collective-permute-done.5.outer_ref = bf16[256,512]{1,0:T(8,128)(2,1)S(1)} collective-permute-done((bf16[256,512]{1,0:T(8,128)(2,1)S(1)}, bf16[256,512]{1,0:T(8,128)(2,1)S(1)}, u32[]{:S(2)}, u32[]{:S(2)}) %collective-permute-start.5) | collective-permute-done | bytes 262176 | tf_op jit(solution)/shard_map/ppermute | solution.py:291
  72.1 0.0 collective-permute-done.6.inner_ref
  72.1 2.4 %shard_map.98 = bf16[2,512,512]{2,1,0:T(8,128)(2,1)} custom-call(bf16[512,512]{1,0:T(8,128)(2,1)S(1)} %get-tuple-element.24.back_side_ref, bf16[512,512]{1,0:T(8,128)(2,1)S(1)} %get-tuple-element.25.lat_ref, bf16[256,512]{1,0:T(8,128)(2,1)S(1)} %collective-permute-done.5.outer_ref, bf16[256,512]{1,0:T(8,128)(2,1)S(1)} %collective-permute-done.6.inner_ref, ...), custom_call_target="tpu_custom_call" | custom-call | flops 1073741824 | bytes 5242880 | tf_op jit(solution)/shard_map/pallas_call | solution.py:376
Async XLA Ops:
  1.4 25.1 %collective-permute-start = (bf16[2,256,512]{2,1,0:T(8,128)(2,1)S(1)}, bf16[2,256,512]{2,1,0:T(8,128)(2,1)S(1)}, u32[]{:S(2)}, u32[]{:S(2)}) collective-permute-start(bf16[2,256,512]{2,1,0:T(8,128)(2,1)S(1)} %get-tuple-element.27), channel_id=1, source_target_pairs={{0,63},{1,2},{2,1},{3,4},{4,3},{5,6},{6,5},{7,8},{8,7},{9,10},{10,... | collective-permute-start | bytes 1572872 | tf_op jit(solution)/shard_map/ppermute | solution.py:287
  14.8 11.6 %collective-permute-start.1 = (bf16[2,256,512]{2,1,0:T(8,128)(2,1)S(1)}, bf16[2,256,512]{2,1,0:T(8,128)(2,1)S(1)}, u32[]{:S(2)}, u32[]{:S(2)}) collective-permute-start(bf16[2,256,512]{2,1,0:T(8,128)(2,1)S(1)} %get-tuple-element.28), channel_id=1, source_target_pairs={{0,1},{1,0},{2,3},{3,2},{4,5},{5,4},{6,7},{7,6},{8,9},{9,8},{10,11... | collective-permute-start | bytes 1572872 | tf_op jit(solution)/shard_map/ppermute | solution.py:286
  20.4 19.2 %collective-permute-start.2 = (bf16[2,256,512]{2,1,0:T(8,128)(2,1)S(1)}, bf16[2,256,512]{2,1,0:T(8,128)(2,1)S(1)}, u32[]{:S(2)}, u32[]{:S(2)}) collective-permute-start(bf16[2,256,512]{2,1,0:T(8,128)(2,1)S(1)} %get-tuple-element.31), channel_id=1, source_target_pairs={{0,63},{1,2},{2,1},{3,4},{4,3},{5,6},{6,5},{7,8},{8,7},{9,10},{10,... | collective-permute-start | bytes 1572872 | tf_op jit(solution)/shard_map/ppermute | solution.py:287
  23.0 16.6 %collective-permute-start.3 = (bf16[2,256,512]{2,1,0:T(8,128)(2,1)S(1)}, bf16[2,256,512]{2,1,0:T(8,128)(2,1)S(1)}, u32[]{:S(2)}, u32[]{:S(2)}) collective-permute-start(bf16[2,256,512]{2,1,0:T(8,128)(2,1)S(1)} %get-tuple-element.32), channel_id=1, source_target_pairs={{0,1},{1,0},{2,3},{3,2},{4,5},{5,4},{6,7},{7,6},{8,9},{9,8},{10,11... | collective-permute-start | bytes 1572872 | tf_op jit(solution)/shard_map/ppermute | solution.py:286
  39.6 10.8 %collective-permute-start.4 = (bf16[128,512]{1,0:T(8,128)(2,1)S(1)}, bf16[128,512]{1,0:T(8,128)(2,1)S(1)}, u32[]{:S(2)}, u32[]{:S(2)}) collective-permute-start(bf16[128,512]{1,0:T(8,128)(2,1)S(1)} %shard_map.94.some_ref), channel_id=1, source_target_pairs={{0,256},{64,320},{128,384},{192,448},{256,0},{320,64},{384,128},{4... | collective-permute-start | bytes 393224 | tf_op jit(solution)/shard_map/ppermute | solution.py:355
  61.1 11.0 %collective-permute-start.5 = (bf16[256,512]{1,0:T(8,128)(2,1)S(1)}, bf16[256,512]{1,0:T(8,128)(2,1)S(1)}, u32[]{:S(2)}, u32[]{:S(2)}) collective-permute-start(bf16[256,512]{1,0:T(8,128)(2,1)S(1)} %get-tuple-element.36), channel_id=1, source_target_pairs={{0,319},{1,2},{2,1},{3,4},{4,3},{5,6},{6,5},{7,264},{8,263},{9,10}... | collective-permute-start | bytes 786440 | tf_op jit(solution)/shard_map/ppermute | solution.py:291
  66.4 5.7 %collective-permute-start.6 = (bf16[256,512]{1,0:T(8,128)(2,1)S(1)}, bf16[256,512]{1,0:T(8,128)(2,1)S(1)}, u32[]{:S(2)}, u32[]{:S(2)}) collective-permute-start(bf16[256,512]{1,0:T(8,128)(2,1)S(1)} %get-tuple-element.37), channel_id=1, source_target_pairs={{0,1},{1,0},{2,3},{3,2},{4,5},{5,4},{6,7},{7,6},{8,9},{9,8},{10,11... | collective-permute-start | bytes 786440 | tf_op jit(solution)/shard_map/ppermute | solution.py:290

commit v4 on v3

--- a/solution.py
+++ b/solution.py
@@ -1,3 +1,5 @@
+import functools
+
 import jax
 import jax.numpy as jnp
 from jax import lax
@@ -13,7 +15,7 @@
 MEMBERS = 2
 XS = 4
 YS = 4
-PACK_PARTS = 4
+PACK_PARTS = 2
 OWN = LEV * ROWS
 SIDE = LEV * HALO
 
@@ -58,6 +60,11 @@
     return top.reshape(rows // 2, columns), bottom.reshape(rows // 2, columns)
 
 
+def waits(lons):
+    lon = lax.axis_index("lon")
+    return (lon > lons - 2 * YS) & (lon < lons - 1)
+
+
 def odd_place():
     return lax.rem(lax.axis_index("lon"), 2) == 1
 
@@ -68,7 +75,7 @@
     inner_ref[at] = jnp.where(odd, top, bottom).astype(BF)
 
 
-def pack_kernel(x_ref, outer_ref, inner_ref, x, sems):
+def pack_kernel(x_ref, outer_ref, inner_ref, again_ref, x, sems):
     odd = odd_place()
     part = OWN // PACK_PARTS
     copies = []
@@ -79,7 +86,9 @@
     for i, copy in enumerate(copies):
         copy.wait()
         m, p = i // PACK_PARTS, i % PACK_PARTS
-        pack_into(odd, x[m, pl.ds(p * part, part)], outer_ref, inner_ref, (m, pl.ds(p * part // 2, part // 2)))
+        at = (m, pl.ds(p * part // 2, part // 2))
+        pack_into(odd, x[m, pl.ds(p * part, part)], outer_ref, inner_ref, at)
+        again_ref[at] = outer_ref[at]
 
 
 def half_like(members):
@@ -188,10 +197,14 @@
     partial_ref[...] = total
 
 
-def forward_kernel(side_ref, lat_ref, outer_ref, inner_ref, weighted_ref, partial_ref, out_ref):
+def forward_kernel(
+    lons, side_ref, lat_ref, outer_ref, inner_ref, later_ref, weighted_ref, partial_ref, out_ref
+):
+    late = waits(lons)
     total = partial_ref[...]
     for m in range(MEMBERS):
-        mixed = jnp.dot(side_ref[:, :SIDE], outer_ref[m], preferred_element_type=F32)
+        outer = jnp.where(late, later_ref[m], outer_ref[m])
+        mixed = jnp.dot(side_ref[:, :SIDE], outer, preferred_element_type=F32)
         mixed += jnp.dot(side_ref[:, SIDE:], inner_ref[m], preferred_element_type=F32)
         local = jnp.dot(mixed.astype(BF), lat_ref[...], preferred_element_type=F32)
         total += weighted_ref[m] * local
@@ -282,9 +295,13 @@
         for i, j in beyond
     ]
 
-    def halo(outer, inner):
+    later = [(i, j) for i, j in beyond if lons - run < i < lons - 1]
+    sooner = [(i, i) if (i, j) in later else (i, j) for i, j in beyond]
+
+    def halo(outer, inner, again):
         from_inner = lax.ppermute(inner, "lon", within)
-        return lax.ppermute(outer, "lon", beyond), from_inner
+        from_later = lax.ppermute(again, "lon", later)
+        return lax.ppermute(outer, "lon", sooner), from_inner, from_later
 
     def misfit_halo(outer, inner):
         from_inner = lax.ppermute(inner, "lon", within)
@@ -296,9 +313,9 @@
     matmul = 2 * OWN * LAT * LAT
     quarter = OWN // XS
 
-    c_outer, c_inner = halo(
+    c_outer, c_inner, c_later = halo(
         *call(
-            pack_kernel, (half_like(MEMBERS),) * 2, (control,), [HBM], 0, 8 * square,
+            pack_kernel, (half_like(MEMBERS),) * 3, (control,), [HBM], 0, 8 * square,
             (pltpu.VMEM((MEMBERS, OWN, LAT), BF), pltpu.SemaphoreType.DMA((MEMBERS * PACK_PARTS,))),
         )
     )
@@ -336,12 +353,12 @@
             pltpu.SemaphoreType.DMA((10,)),
         ),
     )
-    p_outer, p_inner = halo(p_outer, p_inner)
+    p_inner = lax.ppermute(p_inner, "lon", within)
     partial = call(
-        forward_kernel,
+        functools.partial(forward_kernel, lons),
         jax.ShapeDtypeStruct((OWN, LAT), BF),
-        (side, lat, c_outer, c_inner, weighted, partial),
-        [VMEM] * 6,
+        (side, lat, c_outer, c_inner, c_later, weighted, partial),
+        [VMEM] * 7,
         4 * matmul, 18 * square,
     )
 
@@ -351,8 +368,9 @@
     some = call(
         sum_kernel, jax.ShapeDtypeStruct((quarter, LAT), BF), (parts,), [VMEM], 0, 2 * square
     )
-    some, p_outer, p_inner = lax.optimization_barrier((some, p_outer, p_inner))
+    some, p_inner, p_outer = lax.optimization_barrier((some, p_inner, p_outer))
     other = lax.ppermute(some, "mem", across_y)
+    p_outer = lax.ppermute(p_outer, "lon", beyond)
     misfit = call(
         misfit_kernel,
         jax.ShapeDtypeStruct((XS, quarter, LAT), BF),
@@ -363,9 +381,9 @@
     misfit = lax.all_to_all(misfit, "mem", 0, 0, axis_index_groups=along_x).reshape(OWN, LAT)
 
     edge = jax.ShapeDtypeStruct((SIDE, LAT), BF)
-    m_outer, m_inner = misfit_halo(
-        *call(edge_kernel, (edge, edge), (misfit,), [VMEM], 0, 4 * square)
-    )
+    m_outer, m_inner = call(edge_kernel, (edge, edge), (misfit,), [VMEM], 0, 4 * square)
+    m_inner, p_outer = lax.optimization_barrier((m_inner, p_outer))
+    m_outer, m_inner = misfit_halo(m_outer, m_inner)
     base = call(
         back_own_kernel,
         jax.ShapeDtypeStruct((MEMBERS, OWN, LAT), F32),

time: 74.9 us -> 74.5 us (level)
  starting transfers between devices: 32.9 us -> 29.7 us
  waiting for transfers between devices: 9.04 us -> 10.5 us
  blocking collectives: 22.3 us -> 23.3 us
    ppermute x1, starting transfers between devices: 5.27 us -> 1.92 us  [misfit_halo(): return (lax.ppermute(outer, ('mem', 'lon'), across), from_inner)]
    ppermute x2 -> x4, starting transfers between devices: 16 us -> 18.9 us  [the longest x1 13.4 us: halo(): return (lax.ppermute(outer, 'lon', sooner), from_inner, from_later)]
    ppermute x2 -> x1, starting transfers between devices: 3.84 us -> 1.92 us  [halo(): from_inner = lax.ppermute(inner, 'lon', within)]
    ppermute x1, waiting for transfers between devices: 2.52 us -> 4.18 us  [misfit_halo(): return (lax.ppermute(outer, ('mem', 'lon'), across), from_inner)]
    all_to_all x1, blocking collectives: 11.8 us -> 12.8 us  [shards(): lax.all_to_all(partial.reshape(XS, quarter, LAT), 'mem', 0, 0, axis_index...]
    ppermute x1, starting transfers between devices: 5.81 us -> 5.02 us  [shards(): other = lax.ppermute(some, 'mem', across_y)]
    ppermute x2 -> x4, waiting for transfers between devices: 1.56 us -> 1.71 us  [the longest x1 1.7 us: shards(): p_outer = lax.ppermute(p_outer, 'lon', beyond)]
  transfers between devices with their start and end apart: 7 -> 8, of which waited for: 3 -> 3; matrix products, arithmetic and copies ran while one was open for 0% -> 0% of each run, Pallas kernels for 8% -> 9%
where the time goes in v4:
time: 74.5 us; the launch traced here: 74.1 us
  starting transfers between devices  29.7 us (40%)
  blocking collectives  23.3 us (31%)
  waiting for transfers between devices  10.5 us (14%)
  Pallas kernels  10.4 us (14%)
    ppermute x1, starting transfers between devices, halo(): return (lax.ppermute(outer, 'lon', sooner), from_inner, from_later)  13.4 us
    all_to_all x1, blocking collectives, shards(): lax.all_to_all(partial.reshape(XS, quarter, LAT), 'mem', 0, 0, axis_index...  12.8 us
    all_to_all x1, blocking collectives, shards(): lax.all_to_all(misfit, 'mem', 0, 0, axis_index_groups=along_x)  10.5 us
    pallas_call x7, Pallas kernels, call(): pl.pallas_call(kernel, out_shape=out, in_specs=specs, out_specs=jax.tree....  8.01 us
    ppermute x1, starting transfers between devices, shards(): other = lax.ppermute(some, 'mem', across_y)  5.02 us
    ppermute x1, waiting for transfers between devices, shards(): other = lax.ppermute(some, 'mem', across_y)  4.64 us
    ppermute x1, waiting for transfers between devices, misfit_halo(): return (lax.ppermute(outer, ('mem', 'lon'), across), from_inner)  4.18 us
    ppermute x1, starting transfers between devices, shards(): p_outer = lax.ppermute(p_outer, 'lon', beyond)  2.42 us
  transfers between devices with their start and end apart: 8, of which 3 were waited for; matrix products, arithmetic and copies ran while one was open for 0% of the time, Pallas kernels for 9%

profile of v4, /device:TPU:2, one launch (start us, length us, event | category | flops | bytes accessed | tf_op | source)
XLA Modules:
  0.0 74.1 jit_solution(10048077010762653155)
XLA Ops:
  0.0 1.5 %shard_map.92 = (bf16[2,256,512]{2,1,0:T(8,128)(2,1)S(1)}, bf16[2,256,512]{2,1,0:T(8,128)(2,1)S(1)}, bf16[2,256,512]{2,1,0:T(8,128)(2,1)S(1)}) custom-call(bf16[2,512,512]{2,1,0:T(8,128)(2,1)} %bitcast.11), custom_call_target="tpu_custom_call" | custom-call | bytes 2097152 | tf_op jit(solution)/shard_map/pallas_call | solution.py:42
  1.5 13.4 %collective-permute-start = (bf16[2,256,512]{2,1,0:T(8,128)(2,1)S(1)}, bf16[2,256,512]{2,1,0:T(8,128)(2,1)S(1)}, u32[]{:S(2)}, u32[]{:S(2)}) collective-permute-start(bf16[2,256,512]{2,1,0:T(8,128)(2,1)S(1)} %get-tuple-element.30), channel_id=1, source_target_pairs={{0,63},{1,2},{2,1},{3,4},{4,3},{5,6},{6,5},{7,8},{8,7},{9,10},{10,... | collective-permute-start | bytes 1572872 | tf_op jit(solution)/shard_map/ppermute | solution.py:304
  15.0 1.9 %collective-permute-start.1 = (bf16[2,256,512]{2,1,0:T(8,128)(2,1)S(1)}, bf16[2,256,512]{2,1,0:T(8,128)(2,1)S(1)}, u32[]{:S(2)}, u32[]{:S(2)}) collective-permute-start(bf16[2,256,512]{2,1,0:T(8,128)(2,1)S(1)} %get-tuple-element.31), channel_id=1, source_target_pairs={{0,1},{1,0},{2,3},{3,2},{4,5},{5,4},{6,7},{7,6},{8,9},{9,8},{10,11... | collective-permute-start | bytes 1572872 | tf_op jit(solution)/shard_map/ppermute | solution.py:302
  16.9 0.7 collective-permute-start.2
  17.6 3.6 %shard_map.91 = (bf16[512,512]{1,0:T(8,128)(2,1)S(1)}, bf16[512,512]{1,0:T(8,128)(2,1)S(1)}, bf16[512,512]{1,0:T(8,128)(2,1)S(1)}, f32[512,512]{1,0:T(8,128)S(1)...) custom-call(s32[2]{0:T(128)} %group_hbm.1, ...), custom_call_target="tpu_custom_call" | custom-call | flops 1073741824 | bytes 5242880 | tf_op jit(solution)/shard_map/pallas_call | solution.py:42
  21.2 2.4 %collective-permute-start.3 = (bf16[2,256,512]{2,1,0:T(8,128)(2,1)S(1)}, bf16[2,256,512]{2,1,0:T(8,128)(2,1)S(1)}, u32[]{:S(2)}, u32[]{:S(2)}) collective-permute-start(bf16[2,256,512]{2,1,0:T(8,128)(2,1)S(1)} %get-tuple-element.35), channel_id=1, source_target_pairs={{0,1},{1,0},{2,3},{3,2},{4,5},{5,4},{6,7},{7,6},{8,9},{9,8},{10,11... | collective-permute-start | bytes 1572872 | tf_op jit(solution)/shard_map/ppermute | solution.py:356
  23.6 0.0 collective-permute-done.outer_ref
  23.6 0.0 collective-permute-done.1.inner_ref
  23.7 1.3 %shard_map.93 = bf16[512,512]{1,0:T(8,128)(2,1)S(1)} custom-call(bf16[512,512]{1,0:T(8,128)(2,1)S(1)} %get-tuple-element.29.side_ref, bf16[512,512]{1,0:T(8,128)(2,1)S(1)} %get-tuple-element.28.lat_ref, bf16[2,256,512]{2,1,0:T(8,128)(2,1)S(1)} %collective-permute-done.outer_ref, bf16[2,256,512]{2,1,0:T(8,128)(2,1)S(1)} %collective-permute-done.1.inner_ref, ...), custom_call_target="tpu_custom_call" | custom-call | flops 1073741824 | bytes 4718592 | tf_op jit(solution)/shard_map/pallas_call | solution.py:42
  25.0 12.8 %all_to_all.10.parts_ref = bf16[4,128,512]{2,1,0:T(8,128)(2,1)S(1)} all-to-all(bf16[4,128,512]{2,1,0:T(8,128)(2,1)S(1)} %bitcast.10), channel_id=1, replica_groups={{0,64,128,192},{256,320,384,448},{1,65,129,193},{257,321,385,449},{2,66..., dimensions={0} | all-to-all | bytes 1048576 | tf_op jit(solution)/shard_map/all_to_all | solution.py:365
  37.8 0.1 shard_map.94.some_ref
  37.9 0.0 collective-permute-done.3.p_inner_ref
  37.9 5.0 %collective-permute-start.4 = (bf16[128,512]{1,0:T(8,128)(2,1)S(1)}, bf16[128,512]{1,0:T(8,128)(2,1)S(1)}, u32[]{:S(2)}, u32[]{:S(2)}) collective-permute-start(bf16[128,512]{1,0:T(8,128)(2,1)S(1)} %shard_map.94.some_ref), channel_id=1, source_target_pairs={{0,256},{64,320},{128,384},{192,448},{256,0},{320,64},{384,128},{4... | collective-permute-start | bytes 393224 | tf_op jit(solution)/shard_map/ppermute | solution.py:372
  42.9 2.4 %collective-permute-start.6 = (bf16[2,256,512]{2,1,0:T(8,128)(2,1)S(1)}, bf16[2,256,512]{2,1,0:T(8,128)(2,1)S(1)}, u32[]{:S(2)}, u32[]{:S(2)}) collective-permute-start(bf16[2,256,512]{2,1,0:T(8,128)(2,1)S(1)} %get-tuple-element.42), channel_id=1, source_target_pairs={{0,63},{1,2},{2,1},{3,4},{4,3},{5,6},{6,5},{7,8},{8,7},{9,10},{10,... | collective-permute-start | bytes 1572872 | tf_op jit(solution)/shard_map/ppermute | solution.py:373
  45.3 4.6 %collective-permute-done.4.other_ref = bf16[128,512]{1,0:T(8,128)(2,1)S(1)} collective-permute-done((bf16[128,512]{1,0:T(8,128)(2,1)S(1)}, bf16[128,512]{1,0:T(8,128)(2,1)S(1)}, u32[]{:S(2)}, u32[]{:S(2)}) %collective-permute-start.4) | collective-permute-done | bytes 131104 | tf_op jit(solution)/shard_map/ppermute | solution.py:372
  50.0 0.1 shard_map.95
  50.0 10.5 %all_to_all.11 = bf16[4,128,512]{2,1,0:T(8,128)(2,1)S(1)} all-to-all(bf16[4,128,512]{2,1,0:T(8,128)(2,1)S(1)} %shard_map.95), channel_id=1, replica_groups={{0,64,128,192},{256,320,384,448},{1,65,129,193},{257,321,385,449},{2,66..., dimensions={0} | all-to-all | bytes 1048576 | tf_op jit(solution)/shard_map/all_to_all | solution.py:381
  60.5 0.2 shard_map.96
  60.7 1.9 %collective-permute-start.5 = (bf16[256,512]{1,0:T(8,128)(2,1)S(1)}, bf16[256,512]{1,0:T(8,128)(2,1)S(1)}, u32[]{:S(2)}, u32[]{:S(2)}) collective-permute-start(bf16[256,512]{1,0:T(8,128)(2,1)S(1)} %get-tuple-element.40), channel_id=1, source_target_pairs={{0,319},{1,2},{2,1},{3,4},{4,3},{5,6},{6,5},{7,264},{8,263},{9,10}... | collective-permute-start | bytes 786440 | tf_op jit(solution)/shard_map/ppermute | solution.py:308
  62.6 1.7 %collective-permute-done.6.p_outer_ref = bf16[2,256,512]{2,1,0:T(8,128)(2,1)S(1)} collective-permute-done((bf16[2,256,512]{2,1,0:T(8,128)(2,1)S(1)}, bf16[2,256,512]{2,1,0:T(8,128)(2,1)S(1)}, u32[]{:S(2)}, u32[]{:S(2)}) %collective-permute-start.6) | collective-permute-done | bytes 524320 | tf_op jit(solution)/shard_map/ppermute | solution.py:373
  64.3 1.9 %collective-permute-start.7 = (bf16[256,512]{1,0:T(8,128)(2,1)S(1)}, bf16[256,512]{1,0:T(8,128)(2,1)S(1)}, u32[]{:S(2)}, u32[]{:S(2)}) collective-permute-start(bf16[256,512]{1,0:T(8,128)(2,1)S(1)} %get-tuple-element.43), channel_id=1, source_target_pairs={{0,1},{1,0},{2,3},{3,2},{4,5},{5,4},{6,7},{7,6},{8,9},{9,8},{10,11... | collective-permute-start | bytes 786440 | tf_op jit(solution)/shard_map/ppermute | solution.py:307
  66.2 1.3 %shard_map.97.base_ref = f32[2,512,512]{2,1,0:T(8,128)S(1)} custom-call(bf16[512,512]{1,0:T(8,128)(2,1)S(1)} %get-tuple-element.47.back_own_ref, bf16[512,512]{1,0:T(8,128)(2,1)S(1)} %get-tuple-element.28.lat_ref, bf16[512,512]{1,0:T(8,128)(2,1)S(1)} %bitcast.9, f32[2,512,512]{2,1,0:T(8,128)S(1)} %get-tuple-element.33.weighted_ref, ...), custom_call_target="tpu_custom_call" | custom-call | flops 1073741824 | bytes 4718592 | tf_op jit(solution)/shard_map/pallas_call | solution.py:42
  67.5 4.2 %collective-permute-done.5.outer_ref = bf16[256,512]{1,0:T(8,128)(2,1)S(1)} collective-permute-done((bf16[256,512]{1,0:T(8,128)(2,1)S(1)}, bf16[256,512]{1,0:T(8,128)(2,1)S(1)}, u32[]{:S(2)}, u32[]{:S(2)}) %collective-permute-start.5) | collective-permute-done | bytes 262176 | tf_op jit(solution)/shard_map/ppermute | solution.py:308
  71.7 2.4 %shard_map.98 = bf16[2,512,512]{2,1,0:T(8,128)(2,1)} custom-call(bf16[512,512]{1,0:T(8,128)(2,1)S(1)} %get-tuple-element.27.back_side_ref, bf16[512,512]{1,0:T(8,128)(2,1)S(1)} %get-tuple-element.28.lat_ref, bf16[256,512]{1,0:T(8,128)(2,1)S(1)} %collective-permute-done.5.outer_ref, bf16[256,512]{1,0:T(8,128)(2,1)S(1)} %collective-permute-done.7.inner_ref, ...), custom_call_target="tpu_custom_call" | custom-call | flops 1073741824 | bytes 5242880 | tf_op jit(solution)/shard_map/pallas_call | solution.py:394
  (2 shorter events, 0.0 us)
Async XLA Ops:
  1.5 22.1 %collective-permute-start = (bf16[2,256,512]{2,1,0:T(8,128)(2,1)S(1)}, bf16[2,256,512]{2,1,0:T(8,128)(2,1)S(1)}, u32[]{:S(2)}, u32[]{:S(2)}) collective-permute-start(bf16[2,256,512]{2,1,0:T(8,128)(2,1)S(1)} %get-tuple-element.30), channel_id=1, source_target_pairs={{0,63},{1,2},{2,1},{3,4},{4,3},{5,6},{6,5},{7,8},{8,7},{9,10},{10,... | collective-permute-start | bytes 1572872 | tf_op jit(solution)/shard_map/ppermute | solution.py:304
  15.0 8.7 %collective-permute-start.1 = (bf16[2,256,512]{2,1,0:T(8,128)(2,1)S(1)}, bf16[2,256,512]{2,1,0:T(8,128)(2,1)S(1)}, u32[]{:S(2)}, u32[]{:S(2)}) collective-permute-start(bf16[2,256,512]{2,1,0:T(8,128)(2,1)S(1)} %get-tuple-element.31), channel_id=1, source_target_pairs={{0,1},{1,0},{2,3},{3,2},{4,5},{5,4},{6,7},{7,6},{8,9},{9,8},{10,11... | collective-permute-start | bytes 1572872 | tf_op jit(solution)/shard_map/ppermute | solution.py:302
  16.9 6.8 %collective-permute-start.2 = (bf16[2,256,512]{2,1,0:T(8,128)(2,1)S(1)}, bf16[2,256,512]{2,1,0:T(8,128)(2,1)S(1)}, u32[]{:S(2)}, u32[]{:S(2)}) collective-permute-start(bf16[2,256,512]{2,1,0:T(8,128)(2,1)S(1)} %get-tuple-element.32), channel_id=1, source_target_pairs={{57,58},{58,57},{59,60},{60,59},{61,62},{62,61},{121,122},{122,121... | collective-permute-start | bytes 1572872 | tf_op jit(solution)/shard_map/ppermute | solution.py:303
  21.2 16.6 %collective-permute-start.3 = (bf16[2,256,512]{2,1,0:T(8,128)(2,1)S(1)}, bf16[2,256,512]{2,1,0:T(8,128)(2,1)S(1)}, u32[]{:S(2)}, u32[]{:S(2)}) collective-permute-start(bf16[2,256,512]{2,1,0:T(8,128)(2,1)S(1)} %get-tuple-element.35), channel_id=1, source_target_pairs={{0,1},{1,0},{2,3},{3,2},{4,5},{5,4},{6,7},{7,6},{8,9},{9,8},{10,11... | collective-permute-start | bytes 1572872 | tf_op jit(solution)/shard_map/ppermute | solution.py:356
  37.9 12.1 %collective-permute-start.4 = (bf16[128,512]{1,0:T(8,128)(2,1)S(1)}, bf16[128,512]{1,0:T(8,128)(2,1)S(1)}, u32[]{:S(2)}, u32[]{:S(2)}) collective-permute-start(bf16[128,512]{1,0:T(8,128)(2,1)S(1)} %shard_map.94.some_ref), channel_id=1, source_target_pairs={{0,256},{64,320},{128,384},{192,448},{256,0},{320,64},{384,128},{4... | collective-permute-start | bytes 393224 | tf_op jit(solution)/shard_map/ppermute | solution.py:372
  42.9 21.4 %collective-permute-start.6 = (bf16[2,256,512]{2,1,0:T(8,128)(2,1)S(1)}, bf16[2,256,512]{2,1,0:T(8,128)(2,1)S(1)}, u32[]{:S(2)}, u32[]{:S(2)}) collective-permute-start(bf16[2,256,512]{2,1,0:T(8,128)(2,1)S(1)} %get-tuple-element.42), channel_id=1, source_target_pairs={{0,63},{1,2},{2,1},{3,4},{4,3},{5,6},{6,5},{7,8},{8,7},{9,10},{10,... | collective-permute-start | bytes 1572872 | tf_op jit(solution)/shard_map/ppermute | solution.py:373
  60.7 11.0 %collective-permute-start.5 = (bf16[256,512]{1,0:T(8,128)(2,1)S(1)}, bf16[256,512]{1,0:T(8,128)(2,1)S(1)}, u32[]{:S(2)}, u32[]{:S(2)}) collective-permute-start(bf16[256,512]{1,0:T(8,128)(2,1)S(1)} %get-tuple-element.40), channel_id=1, source_target_pairs={{0,319},{1,2},{2,1},{3,4},{4,3},{5,6},{6,5},{7,264},{8,263},{9,10}... | collective-permute-start | bytes 786440 | tf_op jit(solution)/shard_map/ppermute | solution.py:308
  64.3 7.4 %collective-permute-start.7 = (bf16[256,512]{1,0:T(8,128)(2,1)S(1)}, bf16[256,512]{1,0:T(8,128)(2,1)S(1)}, u32[]{:S(2)}, u32[]{:S(2)}) collective-permute-start(bf16[256,512]{1,0:T(8,128)(2,1)S(1)} %get-tuple-element.43), channel_id=1, source_target_pairs={{0,1},{1,0},{2,3},{3,2},{4,5},{5,4},{6,7},{7,6},{8,9},{9,8},{10,11... | collective-permute-start | bytes 786440 | tf_op jit(solution)/shard_map/ppermute | solution.py:307

commit v5 on v4

--- a/solution.py
+++ b/solution.py
@@ -353,7 +353,6 @@
             pltpu.SemaphoreType.DMA((10,)),
         ),
     )
-    p_inner = lax.ppermute(p_inner, "lon", within)
     partial = call(
         functools.partial(forward_kernel, lons),
         jax.ShapeDtypeStruct((OWN, LAT), BF),
@@ -371,6 +370,7 @@
     some, p_inner, p_outer = lax.optimization_barrier((some, p_inner, p_outer))
     other = lax.ppermute(some, "mem", across_y)
     p_outer = lax.ppermute(p_outer, "lon", beyond)
+    p_inner = lax.ppermute(p_inner, "lon", within)
     misfit = call(
         misfit_kernel,
         jax.ShapeDtypeStruct((XS, quarter, LAT), BF),
@@ -382,7 +382,7 @@
 
     edge = jax.ShapeDtypeStruct((SIDE, LAT), BF)
     m_outer, m_inner = call(edge_kernel, (edge, edge), (misfit,), [VMEM], 0, 4 * square)
-    m_inner, p_outer = lax.optimization_barrier((m_inner, p_outer))
+    m_inner, p_outer, p_inner = lax.optimization_barrier((m_inner, p_outer, p_inner))
     m_outer, m_inner = misfit_halo(m_outer, m_inner)
     base = call(
         back_own_kernel,

time: 74.5 us -> 74.1 us (level)
  waiting for transfers between devices: 10.5 us -> 6.38 us
  starting transfers between devices: 29.7 us -> 33.2 us
    ppermute x1, waiting for transfers between devices: 4.64 us -> 0.92 us  [shards(): other = lax.ppermute(some, 'mem', across_y)]
    ppermute x1, starting transfers between devices: 1.92 us -> 3.95 us  [misfit_halo(): return (lax.ppermute(outer, ('mem', 'lon'), across), from_inner)]
    ppermute x1, starting transfers between devices: 2.42 us -> 4.35 us  [shards(): p_outer = lax.ppermute(p_outer, 'lon', beyond)]
    ppermute x1, waiting for transfers between devices: 1.7 us -> 0.01 us  [shards(): p_outer = lax.ppermute(p_outer, 'lon', beyond)]
    ppermute x1, waiting for transfers between devices: 0.01 us -> 1.62 us  [halo(): return (lax.ppermute(outer, 'lon', sooner), from_inner, from_later)]
    all_to_all x1, blocking collectives: 10.5 us -> 11.9 us  [shards(): lax.all_to_all(misfit, 'mem', 0, 0, axis_index_groups=along_x)]
    all_to_all x1, blocking collectives: 12.8 us -> 11.7 us  [shards(): lax.all_to_all(partial.reshape(XS, quarter, LAT), 'mem', 0, 0, axis_index...]
  transfers between devices with their start and end apart: 8 -> 8, of which waited for: 3 -> 3; matrix products, arithmetic and copies ran while one was open for 0% -> 0% of each run, Pallas kernels for 9% -> 7%
where the time goes in v5:
time: 74.1 us; the launch traced here: 73.7 us
  starting transfers between devices  33.2 us (45%)
  blocking collectives  23.6 us (32%)
  Pallas kernels  10.4 us (14%)
  waiting for transfers between devices  6.38 us (9%)
    ppermute x1, starting transfers between devices, halo(): return (lax.ppermute(outer, 'lon', sooner), from_inner, from_later)  13.4 us
    all_to_all x1, blocking collectives, shards(): lax.all_to_all(misfit, 'mem', 0, 0, axis_index_groups=along_x)  11.9 us
    all_to_all x1, blocking collectives, shards(): lax.all_to_all(partial.reshape(XS, quarter, LAT), 'mem', 0, 0, axis_index...  11.7 us
    pallas_call x7, Pallas kernels, call(): pl.pallas_call(kernel, out_shape=out, in_specs=specs, out_specs=jax.tree....  8.01 us
    ppermute x1, starting transfers between devices, shards(): other = lax.ppermute(some, 'mem', across_y)  5.02 us
    ppermute x1, starting transfers between devices, shards(): p_outer = lax.ppermute(p_outer, 'lon', beyond)  4.35 us
    ppermute x1, starting transfers between devices, misfit_halo(): return (lax.ppermute(outer, ('mem', 'lon'), across), from_inner)  3.95 us
    ppermute x1, waiting for transfers between devices, misfit_halo(): return (lax.ppermute(outer, ('mem', 'lon'), across), from_inner)  3.82 us
  transfers between devices with their start and end apart: 8, of which 3 were waited for; matrix products, arithmetic and copies ran while one was open for 0% of the time, Pallas kernels for 7%

profile of v5, /device:TPU:2, one launch (start us, length us, event | category | flops | bytes accessed | tf_op | source)
XLA Modules:
  0.0 73.7 jit_solution(13556245539976517814)
XLA Ops:
  0.0 1.5 %shard_map.92 = (bf16[2,256,512]{2,1,0:T(8,128)(2,1)S(1)}, bf16[2,256,512]{2,1,0:T(8,128)(2,1)S(1)}, bf16[2,256,512]{2,1,0:T(8,128)(2,1)S(1)}) custom-call(bf16[2,512,512]{2,1,0:T(8,128)(2,1)} %bitcast.11), custom_call_target="tpu_custom_call" | custom-call | bytes 2097152 | tf_op jit(solution)/shard_map/pallas_call | solution.py:42
  1.5 13.4 %collective-permute-start = (bf16[2,256,512]{2,1,0:T(8,128)(2,1)S(1)}, bf16[2,256,512]{2,1,0:T(8,128)(2,1)S(1)}, u32[]{:S(2)}, u32[]{:S(2)}) collective-permute-start(bf16[2,256,512]{2,1,0:T(8,128)(2,1)S(1)} %get-tuple-element.31), channel_id=1, source_target_pairs={{0,63},{1,2},{2,1},{3,4},{4,3},{5,6},{6,5},{7,8},{8,7},{9,10},{10,... | collective-permute-start | bytes 1572872 | tf_op jit(solution)/shard_map/ppermute | solution.py:304
  15.0 1.9 %collective-permute-start.1 = (bf16[2,256,512]{2,1,0:T(8,128)(2,1)S(1)}, bf16[2,256,512]{2,1,0:T(8,128)(2,1)S(1)}, u32[]{:S(2)}, u32[]{:S(2)}) collective-permute-start(bf16[2,256,512]{2,1,0:T(8,128)(2,1)S(1)} %get-tuple-element.32), channel_id=1, source_target_pairs={{0,1},{1,0},{2,3},{3,2},{4,5},{5,4},{6,7},{7,6},{8,9},{9,8},{10,11... | collective-permute-start | bytes 1572872 | tf_op jit(solution)/shard_map/ppermute | solution.py:302
  16.9 0.7 collective-permute-start.2
  17.6 3.6 %shard_map.91 = (bf16[512,512]{1,0:T(8,128)(2,1)S(1)}, bf16[512,512]{1,0:T(8,128)(2,1)S(1)}, bf16[512,512]{1,0:T(8,128)(2,1)S(1)}, f32[512,512]{1,0:T(8,128)S(1)...) custom-call(s32[2]{0:T(128)} %group_hbm.1, ...), custom_call_target="tpu_custom_call" | custom-call | flops 1073741824 | bytes 5242880 | tf_op jit(solution)/shard_map/pallas_call | solution.py:42
  21.2 1.6 %collective-permute-done.outer_ref = bf16[2,256,512]{2,1,0:T(8,128)(2,1)S(1)} collective-permute-done((bf16[2,256,512]{2,1,0:T(8,128)(2,1)S(1)}, bf16[2,256,512]{2,1,0:T(8,128)(2,1)S(1)}, u32[]{:S(2)}, u32[]{:S(2)}) %collective-permute-start) | collective-permute-done | bytes 524320 | tf_op jit(solution)/shard_map/ppermute | solution.py:304
  22.8 0.0 collective-permute-done.1.inner_ref
  22.8 0.0 collective-permute-done.2.later_ref
  22.8 1.3 %shard_map.93 = bf16[512,512]{1,0:T(8,128)(2,1)S(1)} custom-call(bf16[512,512]{1,0:T(8,128)(2,1)S(1)} %get-tuple-element.30.side_ref, bf16[512,512]{1,0:T(8,128)(2,1)S(1)} %get-tuple-element.29.lat_ref, bf16[2,256,512]{2,1,0:T(8,128)(2,1)S(1)} %collective-permute-done.outer_ref, bf16[2,256,512]{2,1,0:T(8,128)(2,1)S(1)} %collective-permute-done.1.inner_ref, ...), custom_call_target="tpu_custom_call" | custom-call | flops 1073741824 | bytes 4718592 | tf_op jit(solution)/shard_map/pallas_call | solution.py:42
  24.1 11.7 %all_to_all.10.parts_ref = bf16[4,128,512]{2,1,0:T(8,128)(2,1)S(1)} all-to-all(bf16[4,128,512]{2,1,0:T(8,128)(2,1)S(1)} %bitcast.10), channel_id=1, replica_groups={{0,64,128,192},{256,320,384,448},{1,65,129,193},{257,321,385,449},{2,66..., dimensions={0} | all-to-all | bytes 1048576 | tf_op jit(solution)/shard_map/all_to_all | solution.py:364
  35.9 0.1 shard_map.94.some_ref
  35.9 5.0 %collective-permute-start.3 = (bf16[128,512]{1,0:T(8,128)(2,1)S(1)}, bf16[128,512]{1,0:T(8,128)(2,1)S(1)}, u32[]{:S(2)}, u32[]{:S(2)}) collective-permute-start(bf16[128,512]{1,0:T(8,128)(2,1)S(1)} %shard_map.94.some_ref), channel_id=1, source_target_pairs={{0,256},{64,320},{128,384},{192,448},{256,0},{320,64},{384,128},{4... | collective-permute-start | bytes 393224 | tf_op jit(solution)/shard_map/ppermute | solution.py:371
  41.0 4.3 %collective-permute-start.5 = (bf16[2,256,512]{2,1,0:T(8,128)(2,1)S(1)}, bf16[2,256,512]{2,1,0:T(8,128)(2,1)S(1)}, u32[]{:S(2)}, u32[]{:S(2)}) collective-permute-start(bf16[2,256,512]{2,1,0:T(8,128)(2,1)S(1)} %get-tuple-element.43), channel_id=1, source_target_pairs={{0,63},{1,2},{2,1},{3,4},{4,3},{5,6},{6,5},{7,8},{8,7},{9,10},{10,... | collective-permute-start | bytes 1572872 | tf_op jit(solution)/shard_map/ppermute | solution.py:372
  45.3 1.9 %collective-permute-start.6 = (bf16[2,256,512]{2,1,0:T(8,128)(2,1)S(1)}, bf16[2,256,512]{2,1,0:T(8,128)(2,1)S(1)}, u32[]{:S(2)}, u32[]{:S(2)}) collective-permute-start(bf16[2,256,512]{2,1,0:T(8,128)(2,1)S(1)} %get-tuple-element.44), channel_id=1, source_target_pairs={{0,1},{1,0},{2,3},{3,2},{4,5},{5,4},{6,7},{7,6},{8,9},{9,8},{10,11... | collective-permute-start | bytes 1572872 | tf_op jit(solution)/shard_map/ppermute | solution.py:373
  47.2 0.9 %collective-permute-done.3.other_ref = bf16[128,512]{1,0:T(8,128)(2,1)S(1)} collective-permute-done((bf16[128,512]{1,0:T(8,128)(2,1)S(1)}, bf16[128,512]{1,0:T(8,128)(2,1)S(1)}, u32[]{:S(2)}, u32[]{:S(2)}) %collective-permute-start.3) | collective-permute-done | bytes 131104 | tf_op jit(solution)/shard_map/ppermute | solution.py:371
  48.2 0.1 shard_map.95
  48.2 11.9 %all_to_all.11 = bf16[4,128,512]{2,1,0:T(8,128)(2,1)S(1)} all-to-all(bf16[4,128,512]{2,1,0:T(8,128)(2,1)S(1)} %shard_map.95), channel_id=1, replica_groups={{0,64,128,192},{256,320,384,448},{1,65,129,193},{257,321,385,449},{2,66..., dimensions={0} | all-to-all | bytes 1048576 | tf_op jit(solution)/shard_map/all_to_all | solution.py:381
  60.2 0.2 shard_map.96
  60.3 4.0 %collective-permute-start.4 = (bf16[256,512]{1,0:T(8,128)(2,1)S(1)}, bf16[256,512]{1,0:T(8,128)(2,1)S(1)}, u32[]{:S(2)}, u32[]{:S(2)}) collective-permute-start(bf16[256,512]{1,0:T(8,128)(2,1)S(1)} %get-tuple-element.41), channel_id=1, source_target_pairs={{0,319},{1,2},{2,1},{3,4},{4,3},{5,6},{6,5},{7,264},{8,263},{9,10}... | collective-permute-start | bytes 786440 | tf_op jit(solution)/shard_map/ppermute | solution.py:308
  64.3 0.0 collective-permute-done.5.p_outer_ref
  64.3 1.9 %collective-permute-start.7 = (bf16[256,512]{1,0:T(8,128)(2,1)S(1)}, bf16[256,512]{1,0:T(8,128)(2,1)S(1)}, u32[]{:S(2)}, u32[]{:S(2)}) collective-permute-start(bf16[256,512]{1,0:T(8,128)(2,1)S(1)} %get-tuple-element.45), channel_id=1, source_target_pairs={{0,1},{1,0},{2,3},{3,2},{4,5},{5,4},{6,7},{7,6},{8,9},{9,8},{10,11... | collective-permute-start | bytes 786440 | tf_op jit(solution)/shard_map/ppermute | solution.py:307
  66.2 1.3 %shard_map.97.base_ref = f32[2,512,512]{2,1,0:T(8,128)S(1)} custom-call(bf16[512,512]{1,0:T(8,128)(2,1)S(1)} %get-tuple-element.49.back_own_ref, bf16[512,512]{1,0:T(8,128)(2,1)S(1)} %get-tuple-element.29.lat_ref, bf16[512,512]{1,0:T(8,128)(2,1)S(1)} %bitcast.9, f32[2,512,512]{2,1,0:T(8,128)S(1)} %get-tuple-element.34.weighted_ref, ...), custom_call_target="tpu_custom_call" | custom-call | flops 1073741824 | bytes 4718592 | tf_op jit(solution)/shard_map/pallas_call | solution.py:42
  67.5 3.8 %collective-permute-done.4.outer_ref = bf16[256,512]{1,0:T(8,128)(2,1)S(1)} collective-permute-done((bf16[256,512]{1,0:T(8,128)(2,1)S(1)}, bf16[256,512]{1,0:T(8,128)(2,1)S(1)}, u32[]{:S(2)}, u32[]{:S(2)}) %collective-permute-start.4) | collective-permute-done | bytes 262176 | tf_op jit(solution)/shard_map/ppermute | solution.py:308
  71.3 2.4 %shard_map.98 = bf16[2,512,512]{2,1,0:T(8,128)(2,1)} custom-call(bf16[512,512]{1,0:T(8,128)(2,1)S(1)} %get-tuple-element.28.back_side_ref, bf16[512,512]{1,0:T(8,128)(2,1)S(1)} %get-tuple-element.29.lat_ref, bf16[256,512]{1,0:T(8,128)(2,1)S(1)} %collective-permute-done.4.outer_ref, bf16[256,512]{1,0:T(8,128)(2,1)S(1)} %collective-permute-done.7.inner_ref, ...), custom_call_target="tpu_custom_call" | custom-call | flops 1073741824 | bytes 5242880 | tf_op jit(solution)/shard_map/pallas_call | solution.py:394
  (2 shorter events, 0.0 us)
Async XLA Ops:
  1.5 21.3 %collective-permute-start = (bf16[2,256,512]{2,1,0:T(8,128)(2,1)S(1)}, bf16[2,256,512]{2,1,0:T(8,128)(2,1)S(1)}, u32[]{:S(2)}, u32[]{:S(2)}) collective-permute-start(bf16[2,256,512]{2,1,0:T(8,128)(2,1)S(1)} %get-tuple-element.31), channel_id=1, source_target_pairs={{0,63},{1,2},{2,1},{3,4},{4,3},{5,6},{6,5},{7,8},{8,7},{9,10},{10,... | collective-permute-start | bytes 1572872 | tf_op jit(solution)/shard_map/ppermute | solution.py:304
  15.0 7.9 %collective-permute-start.1 = (bf16[2,256,512]{2,1,0:T(8,128)(2,1)S(1)}, bf16[2,256,512]{2,1,0:T(8,128)(2,1)S(1)}, u32[]{:S(2)}, u32[]{:S(2)}) collective-permute-start(bf16[2,256,512]{2,1,0:T(8,128)(2,1)S(1)} %get-tuple-element.32), channel_id=1, source_target_pairs={{0,1},{1,0},{2,3},{3,2},{4,5},{5,4},{6,7},{7,6},{8,9},{9,8},{10,11... | collective-permute-start | bytes 1572872 | tf_op jit(solution)/shard_map/ppermute | solution.py:302
  16.9 6.0 %collective-permute-start.2 = (bf16[2,256,512]{2,1,0:T(8,128)(2,1)S(1)}, bf16[2,256,512]{2,1,0:T(8,128)(2,1)S(1)}, u32[]{:S(2)}, u32[]{:S(2)}) collective-permute-start(bf16[2,256,512]{2,1,0:T(8,128)(2,1)S(1)} %get-tuple-element.33), channel_id=1, source_target_pairs={{57,58},{58,57},{59,60},{60,59},{61,62},{62,61},{121,122},{122,121... | collective-permute-start | bytes 1572872 | tf_op jit(solution)/shard_map/ppermute | solution.py:303
  35.9 12.2 %collective-permute-start.3 = (bf16[128,512]{1,0:T(8,128)(2,1)S(1)}, bf16[128,512]{1,0:T(8,128)(2,1)S(1)}, u32[]{:S(2)}, u32[]{:S(2)}) collective-permute-start(bf16[128,512]{1,0:T(8,128)(2,1)S(1)} %shard_map.94.some_ref), channel_id=1, source_target_pairs={{0,256},{64,320},{128,384},{192,448},{256,0},{320,64},{384,128},{4... | collective-permute-start | bytes 393224 | tf_op jit(solution)/shard_map/ppermute | solution.py:371
  41.0 23.3 %collective-permute-start.5 = (bf16[2,256,512]{2,1,0:T(8,128)(2,1)S(1)}, bf16[2,256,512]{2,1,0:T(8,128)(2,1)S(1)}, u32[]{:S(2)}, u32[]{:S(2)}) collective-permute-start(bf16[2,256,512]{2,1,0:T(8,128)(2,1)S(1)} %get-tuple-element.43), channel_id=1, source_target_pairs={{0,63},{1,2},{2,1},{3,4},{4,3},{5,6},{6,5},{7,8},{8,7},{9,10},{10,... | collective-permute-start | bytes 1572872 | tf_op jit(solution)/shard_map/ppermute | solution.py:372
  45.3 19.0 %collective-permute-start.6 = (bf16[2,256,512]{2,1,0:T(8,128)(2,1)S(1)}, bf16[2,256,512]{2,1,0:T(8,128)(2,1)S(1)}, u32[]{:S(2)}, u32[]{:S(2)}) collective-permute-start(bf16[2,256,512]{2,1,0:T(8,128)(2,1)S(1)} %get-tuple-element.44), channel_id=1, source_target_pairs={{0,1},{1,0},{2,3},{3,2},{4,5},{5,4},{6,7},{7,6},{8,9},{9,8},{10,11... | collective-permute-start | bytes 1572872 | tf_op jit(solution)/shard_map/ppermute | solution.py:373
  60.3 11.0 %collective-permute-start.4 = (bf16[256,512]{1,0:T(8,128)(2,1)S(1)}, bf16[256,512]{1,0:T(8,128)(2,1)S(1)}, u32[]{:S(2)}, u32[]{:S(2)}) collective-permute-start(bf16[256,512]{1,0:T(8,128)(2,1)S(1)} %get-tuple-element.41), channel_id=1, source_target_pairs={{0,319},{1,2},{2,1},{3,4},{4,3},{5,6},{6,5},{7,264},{8,263},{9,10}... | collective-permute-start | bytes 786440 | tf_op jit(solution)/shard_map/ppermute | solution.py:308
  64.3 7.0 %collective-permute-start.7 = (bf16[256,512]{1,0:T(8,128)(2,1)S(1)}, bf16[256,512]{1,0:T(8,128)(2,1)S(1)}, u32[]{:S(2)}, u32[]{:S(2)}) collective-permute-start(bf16[256,512]{1,0:T(8,128)(2,1)S(1)} %get-tuple-element.45), channel_id=1, source_target_pairs={{0,1},{1,0},{2,3},{3,2},{4,5},{5,4},{6,7},{7,6},{8,9},{9,8},{10,11... | collective-permute-start | bytes 786440 | tf_op jit(solution)/shard_map/ppermute | solution.py:307

commit v6 on v5

--- a/solution.py
+++ b/solution.py
@@ -248,24 +248,16 @@
         weighted = (scale_ref[m][None] * p).reshape(SIDE, LAT)
         return (weighted * misfit_ref[...].astype(F32)).astype(BF)
 
-    half = OWN // 2
     copies = []
     for m in range(MEMBERS):
         from_outer = back(m, p_outer_ref, outer_ref)
         from_inner = back(m, p_inner_ref, inner_ref)
-        for h in range(2):
-            rows = pl.ds(h * half, half)
-            mixed = jnp.dot(back_side_ref[rows, :SIDE], from_outer, preferred_element_type=F32)
-            mixed += jnp.dot(back_side_ref[rows, SIDE:], from_inner, preferred_element_type=F32)
-            latback = lax.dot_general(
-                mixed.astype(BF), lat_ref[...], LAST, preferred_element_type=F32
-            )
-            out[m, rows, :] = (base_ref[m, rows, :] + latback).astype(BF)
-            copy = pltpu.make_async_copy(
-                out.at[m, rows], out_hbm.at[m, rows], sems.at[2 * m + h]
-            )
-            copy.start()
-            copies.append(copy)
+        sides = jnp.concatenate([from_outer, from_inner], axis=0)
+        mixed = jnp.dot(back_side_ref[...], sides, preferred_element_type=F32).astype(BF)
+        latback = lax.dot_general(mixed, lat_ref[...], LAST, preferred_element_type=F32)
+        out[m] = (base_ref[m] + latback).astype(BF)
+        copies.append(pltpu.make_async_copy(out.at[m], out_hbm.at[m], sems.at[m]))
+        copies[m].start()
     for copy in copies:
         copy.wait()
 
@@ -398,7 +390,7 @@
         out_specs=HBM,
         scratch_shapes=(
             pltpu.VMEM((MEMBERS, OWN, LAT), BF),
-            pltpu.SemaphoreType.DMA((2 * MEMBERS,)),
+            pltpu.SemaphoreType.DMA((MEMBERS,)),
         ),
         compiler_params=pltpu.CompilerParams(vmem_limit_bytes=VMEM_LIMIT),
         cost_estimate=pl.CostEstimate(

time: 74.1 us -> 73.9 us (level)
  no operation moved by 1% of the time
where the time goes in v6:
time: 73.9 us; the launch traced here: 73.5 us
  starting transfers between devices  33.2 us (45%)
  blocking collectives  23.6 us (32%)
  Pallas kernels  10.1 us (14%)
  waiting for transfers between devices  6.38 us (9%)
    ppermute x1, starting transfers between devices, halo(): return (lax.ppermute(outer, 'lon', sooner), from_inner, from_later)  13.4 us
    all_to_all x1, blocking collectives, shards(): lax.all_to_all(misfit, 'mem', 0, 0, axis_index_groups=along_x)  11.9 us
    all_to_all x1, blocking collectives, shards(): lax.all_to_all(partial.reshape(XS, quarter, LAT), 'mem', 0, 0, axis_index...  11.7 us
    pallas_call x7, Pallas kernels, call(): pl.pallas_call(kernel, out_shape=out, in_specs=specs, out_specs=jax.tree....  8.01 us
    ppermute x1, starting transfers between devices, shards(): other = lax.ppermute(some, 'mem', across_y)  5.02 us
    ppermute x1, starting transfers between devices, shards(): p_outer = lax.ppermute(p_outer, 'lon', beyond)  4.35 us
    ppermute x1, starting transfers between devices, misfit_halo(): return (lax.ppermute(outer, ('mem', 'lon'), across), from_inner)  3.95 us
    ppermute x1, waiting for transfers between devices, misfit_halo(): return (lax.ppermute(outer, ('mem', 'lon'), across), from_inner)  3.82 us
  transfers between devices with their start and end apart: 8, of which 3 were waited for; matrix products, arithmetic and copies ran while one was open for 0% of the time, Pallas kernels for 7%

profile of v6, /device:TPU:2, one launch (start us, length us, event | category | flops | bytes accessed | tf_op | source)
XLA Modules:
  0.0 73.5 jit_solution(13826369986750089856)
XLA Ops:
  0.0 1.5 %shard_map.92 = (bf16[2,256,512]{2,1,0:T(8,128)(2,1)S(1)}, bf16[2,256,512]{2,1,0:T(8,128)(2,1)S(1)}, bf16[2,256,512]{2,1,0:T(8,128)(2,1)S(1)}) custom-call(bf16[2,512,512]{2,1,0:T(8,128)(2,1)} %bitcast.11), custom_call_target="tpu_custom_call" | custom-call | bytes 2097152 | tf_op jit(solution)/shard_map/pallas_call | solution.py:42
  1.5 13.4 %collective-permute-start = (bf16[2,256,512]{2,1,0:T(8,128)(2,1)S(1)}, bf16[2,256,512]{2,1,0:T(8,128)(2,1)S(1)}, u32[]{:S(2)}, u32[]{:S(2)}) collective-permute-start(bf16[2,256,512]{2,1,0:T(8,128)(2,1)S(1)} %get-tuple-element.31), channel_id=1, source_target_pairs={{0,63},{1,2},{2,1},{3,4},{4,3},{5,6},{6,5},{7,8},{8,7},{9,10},{10,... | collective-permute-start | bytes 1572872 | tf_op jit(solution)/shard_map/ppermute | solution.py:296
  15.0 1.9 %collective-permute-start.1 = (bf16[2,256,512]{2,1,0:T(8,128)(2,1)S(1)}, bf16[2,256,512]{2,1,0:T(8,128)(2,1)S(1)}, u32[]{:S(2)}, u32[]{:S(2)}) collective-permute-start(bf16[2,256,512]{2,1,0:T(8,128)(2,1)S(1)} %get-tuple-element.32), channel_id=1, source_target_pairs={{0,1},{1,0},{2,3},{3,2},{4,5},{5,4},{6,7},{7,6},{8,9},{9,8},{10,11... | collective-permute-start | bytes 1572872 | tf_op jit(solution)/shard_map/ppermute | solution.py:294
  16.9 0.7 collective-permute-start.2
  17.6 3.6 %shard_map.91 = (bf16[512,512]{1,0:T(8,128)(2,1)S(1)}, bf16[512,512]{1,0:T(8,128)(2,1)S(1)}, bf16[512,512]{1,0:T(8,128)(2,1)S(1)}, f32[512,512]{1,0:T(8,128)S(1)...) custom-call(s32[2]{0:T(128)} %group_hbm.1, ...), custom_call_target="tpu_custom_call" | custom-call | flops 1073741824 | bytes 5242880 | tf_op jit(solution)/shard_map/pallas_call | solution.py:42
  21.2 1.6 %collective-permute-done.outer_ref = bf16[2,256,512]{2,1,0:T(8,128)(2,1)S(1)} collective-permute-done((bf16[2,256,512]{2,1,0:T(8,128)(2,1)S(1)}, bf16[2,256,512]{2,1,0:T(8,128)(2,1)S(1)}, u32[]{:S(2)}, u32[]{:S(2)}) %collective-permute-start) | collective-permute-done | bytes 524320 | tf_op jit(solution)/shard_map/ppermute | solution.py:296
  22.8 0.0 collective-permute-done.1.inner_ref
  22.8 0.0 collective-permute-done.2.later_ref
  22.8 1.3 %shard_map.93 = bf16[512,512]{1,0:T(8,128)(2,1)S(1)} custom-call(bf16[512,512]{1,0:T(8,128)(2,1)S(1)} %get-tuple-element.30.side_ref, bf16[512,512]{1,0:T(8,128)(2,1)S(1)} %get-tuple-element.29.lat_ref, bf16[2,256,512]{2,1,0:T(8,128)(2,1)S(1)} %collective-permute-done.outer_ref, bf16[2,256,512]{2,1,0:T(8,128)(2,1)S(1)} %collective-permute-done.1.inner_ref, ...), custom_call_target="tpu_custom_call" | custom-call | flops 1073741824 | bytes 4718592 | tf_op jit(solution)/shard_map/pallas_call | solution.py:42
  24.1 11.7 %all_to_all.10.parts_ref = bf16[4,128,512]{2,1,0:T(8,128)(2,1)S(1)} all-to-all(bf16[4,128,512]{2,1,0:T(8,128)(2,1)S(1)} %bitcast.10), channel_id=1, replica_groups={{0,64,128,192},{256,320,384,448},{1,65,129,193},{257,321,385,449},{2,66..., dimensions={0} | all-to-all | bytes 1048576 | tf_op jit(solution)/shard_map/all_to_all | solution.py:356
  35.9 0.1 shard_map.94.some_ref
  35.9 5.0 %collective-permute-start.3 = (bf16[128,512]{1,0:T(8,128)(2,1)S(1)}, bf16[128,512]{1,0:T(8,128)(2,1)S(1)}, u32[]{:S(2)}, u32[]{:S(2)}) collective-permute-start(bf16[128,512]{1,0:T(8,128)(2,1)S(1)} %shard_map.94.some_ref), channel_id=1, source_target_pairs={{0,256},{64,320},{128,384},{192,448},{256,0},{320,64},{384,128},{4... | collective-permute-start | bytes 393224 | tf_op jit(solution)/shard_map/ppermute | solution.py:363
  41.0 4.3 %collective-permute-start.5 = (bf16[2,256,512]{2,1,0:T(8,128)(2,1)S(1)}, bf16[2,256,512]{2,1,0:T(8,128)(2,1)S(1)}, u32[]{:S(2)}, u32[]{:S(2)}) collective-permute-start(bf16[2,256,512]{2,1,0:T(8,128)(2,1)S(1)} %get-tuple-element.43), channel_id=1, source_target_pairs={{0,63},{1,2},{2,1},{3,4},{4,3},{5,6},{6,5},{7,8},{8,7},{9,10},{10,... | collective-permute-start | bytes 1572872 | tf_op jit(solution)/shard_map/ppermute | solution.py:364
  45.3 1.9 %collective-permute-start.6 = (bf16[2,256,512]{2,1,0:T(8,128)(2,1)S(1)}, bf16[2,256,512]{2,1,0:T(8,128)(2,1)S(1)}, u32[]{:S(2)}, u32[]{:S(2)}) collective-permute-start(bf16[2,256,512]{2,1,0:T(8,128)(2,1)S(1)} %get-tuple-element.44), channel_id=1, source_target_pairs={{0,1},{1,0},{2,3},{3,2},{4,5},{5,4},{6,7},{7,6},{8,9},{9,8},{10,11... | collective-permute-start | bytes 1572872 | tf_op jit(solution)/shard_map/ppermute | solution.py:365
  47.2 0.9 %collective-permute-done.3.other_ref = bf16[128,512]{1,0:T(8,128)(2,1)S(1)} collective-permute-done((bf16[128,512]{1,0:T(8,128)(2,1)S(1)}, bf16[128,512]{1,0:T(8,128)(2,1)S(1)}, u32[]{:S(2)}, u32[]{:S(2)}) %collective-permute-start.3) | collective-permute-done | bytes 131104 | tf_op jit(solution)/shard_map/ppermute | solution.py:363
  48.2 0.1 shard_map.95
  48.2 11.9 %all_to_all.11 = bf16[4,128,512]{2,1,0:T(8,128)(2,1)S(1)} all-to-all(bf16[4,128,512]{2,1,0:T(8,128)(2,1)S(1)} %shard_map.95), channel_id=1, replica_groups={{0,64,128,192},{256,320,384,448},{1,65,129,193},{257,321,385,449},{2,66..., dimensions={0} | all-to-all | bytes 1048576 | tf_op jit(solution)/shard_map/all_to_all | solution.py:373
  60.2 0.2 shard_map.96
  60.3 4.0 %collective-permute-start.4 = (bf16[256,512]{1,0:T(8,128)(2,1)S(1)}, bf16[256,512]{1,0:T(8,128)(2,1)S(1)}, u32[]{:S(2)}, u32[]{:S(2)}) collective-permute-start(bf16[256,512]{1,0:T(8,128)(2,1)S(1)} %get-tuple-element.41), channel_id=1, source_target_pairs={{0,319},{1,2},{2,1},{3,4},{4,3},{5,6},{6,5},{7,264},{8,263},{9,10}... | collective-permute-start | bytes 786440 | tf_op jit(solution)/shard_map/ppermute | solution.py:300
  64.3 0.0 collective-permute-done.6.p_inner_ref
  64.3 1.9 %collective-permute-start.7 = (bf16[256,512]{1,0:T(8,128)(2,1)S(1)}, bf16[256,512]{1,0:T(8,128)(2,1)S(1)}, u32[]{:S(2)}, u32[]{:S(2)}) collective-permute-start(bf16[256,512]{1,0:T(8,128)(2,1)S(1)} %get-tuple-element.45), channel_id=1, source_target_pairs={{0,1},{1,0},{2,3},{3,2},{4,5},{5,4},{6,7},{7,6},{8,9},{9,8},{10,11... | collective-permute-start | bytes 786440 | tf_op jit(solution)/shard_map/ppermute | solution.py:299
  66.2 1.3 %shard_map.97.base_ref = f32[2,512,512]{2,1,0:T(8,128)S(1)} custom-call(bf16[512,512]{1,0:T(8,128)(2,1)S(1)} %get-tuple-element.49.back_own_ref, bf16[512,512]{1,0:T(8,128)(2,1)S(1)} %get-tuple-element.29.lat_ref, bf16[512,512]{1,0:T(8,128)(2,1)S(1)} %bitcast.9, f32[2,512,512]{2,1,0:T(8,128)S(1)} %get-tuple-element.34.weighted_ref, ...), custom_call_target="tpu_custom_call" | custom-call | flops 1073741824 | bytes 4718592 | tf_op jit(solution)/shard_map/pallas_call | solution.py:42
  67.5 3.8 %collective-permute-done.4.outer_ref = bf16[256,512]{1,0:T(8,128)(2,1)S(1)} collective-permute-done((bf16[256,512]{1,0:T(8,128)(2,1)S(1)}, bf16[256,512]{1,0:T(8,128)(2,1)S(1)}, u32[]{:S(2)}, u32[]{:S(2)}) %collective-permute-start.4) | collective-permute-done | bytes 262176 | tf_op jit(solution)/shard_map/ppermute | solution.py:300
  71.3 2.1 %shard_map.98 = bf16[2,512,512]{2,1,0:T(8,128)(2,1)} custom-call(bf16[512,512]{1,0:T(8,128)(2,1)S(1)} %get-tuple-element.28.back_side_ref, bf16[512,512]{1,0:T(8,128)(2,1)S(1)} %get-tuple-element.29.lat_ref, bf16[256,512]{1,0:T(8,128)(2,1)S(1)} %collective-permute-done.4.outer_ref, bf16[256,512]{1,0:T(8,128)(2,1)S(1)} %collective-permute-done.7.inner_ref, ...), custom_call_target="tpu_custom_call" | custom-call | flops 1073741824 | bytes 5242880 | tf_op jit(solution)/shard_map/pallas_call | solution.py:386
  (2 shorter events, 0.0 us)
Async XLA Ops:
  1.5 21.3 %collective-permute-start = (bf16[2,256,512]{2,1,0:T(8,128)(2,1)S(1)}, bf16[2,256,512]{2,1,0:T(8,128)(2,1)S(1)}, u32[]{:S(2)}, u32[]{:S(2)}) collective-permute-start(bf16[2,256,512]{2,1,0:T(8,128)(2,1)S(1)} %get-tuple-element.31), channel_id=1, source_target_pairs={{0,63},{1,2},{2,1},{3,4},{4,3},{5,6},{6,5},{7,8},{8,7},{9,10},{10,... | collective-permute-start | bytes 1572872 | tf_op jit(solution)/shard_map/ppermute | solution.py:296
  15.0 7.9 %collective-permute-start.1 = (bf16[2,256,512]{2,1,0:T(8,128)(2,1)S(1)}, bf16[2,256,512]{2,1,0:T(8,128)(2,1)S(1)}, u32[]{:S(2)}, u32[]{:S(2)}) collective-permute-start(bf16[2,256,512]{2,1,0:T(8,128)(2,1)S(1)} %get-tuple-element.32), channel_id=1, source_target_pairs={{0,1},{1,0},{2,3},{3,2},{4,5},{5,4},{6,7},{7,6},{8,9},{9,8},{10,11... | collective-permute-start | bytes 1572872 | tf_op jit(solution)/shard_map/ppermute | solution.py:294
  16.9 6.0 %collective-permute-start.2 = (bf16[2,256,512]{2,1,0:T(8,128)(2,1)S(1)}, bf16[2,256,512]{2,1,0:T(8,128)(2,1)S(1)}, u32[]{:S(2)}, u32[]{:S(2)}) collective-permute-start(bf16[2,256,512]{2,1,0:T(8,128)(2,1)S(1)} %get-tuple-element.33), channel_id=1, source_target_pairs={{57,58},{58,57},{59,60},{60,59},{61,62},{62,61},{121,122},{122,121... | collective-permute-start | bytes 1572872 | tf_op jit(solution)/shard_map/ppermute | solution.py:295
  35.9 12.2 %collective-permute-start.3 = (bf16[128,512]{1,0:T(8,128)(2,1)S(1)}, bf16[128,512]{1,0:T(8,128)(2,1)S(1)}, u32[]{:S(2)}, u32[]{:S(2)}) collective-permute-start(bf16[128,512]{1,0:T(8,128)(2,1)S(1)} %shard_map.94.some_ref), channel_id=1, source_target_pairs={{0,256},{64,320},{128,384},{192,448},{256,0},{320,64},{384,128},{4... | collective-permute-start | bytes 393224 | tf_op jit(solution)/shard_map/ppermute | solution.py:363
  41.0 23.3 %collective-permute-start.5 = (bf16[2,256,512]{2,1,0:T(8,128)(2,1)S(1)}, bf16[2,256,512]{2,1,0:T(8,128)(2,1)S(1)}, u32[]{:S(2)}, u32[]{:S(2)}) collective-permute-start(bf16[2,256,512]{2,1,0:T(8,128)(2,1)S(1)} %get-tuple-element.43), channel_id=1, source_target_pairs={{0,63},{1,2},{2,1},{3,4},{4,3},{5,6},{6,5},{7,8},{8,7},{9,10},{10,... | collective-permute-start | bytes 1572872 | tf_op jit(solution)/shard_map/ppermute | solution.py:364
  45.3 19.0 %collective-permute-start.6 = (bf16[2,256,512]{2,1,0:T(8,128)(2,1)S(1)}, bf16[2,256,512]{2,1,0:T(8,128)(2,1)S(1)}, u32[]{:S(2)}, u32[]{:S(2)}) collective-permute-start(bf16[2,256,512]{2,1,0:T(8,128)(2,1)S(1)} %get-tuple-element.44), channel_id=1, source_target_pairs={{0,1},{1,0},{2,3},{3,2},{4,5},{5,4},{6,7},{7,6},{8,9},{9,8},{10,11... | collective-permute-start | bytes 1572872 | tf_op jit(solution)/shard_map/ppermute | solution.py:365
  60.3 11.0 %collective-permute-start.4 = (bf16[256,512]{1,0:T(8,128)(2,1)S(1)}, bf16[256,512]{1,0:T(8,128)(2,1)S(1)}, u32[]{:S(2)}, u32[]{:S(2)}) collective-permute-start(bf16[256,512]{1,0:T(8,128)(2,1)S(1)} %get-tuple-element.41), channel_id=1, source_target_pairs={{0,319},{1,2},{2,1},{3,4},{4,3},{5,6},{6,5},{7,264},{8,263},{9,10}... | collective-permute-start | bytes 786440 | tf_op jit(solution)/shard_map/ppermute | solution.py:300
  64.3 7.0 %collective-permute-start.7 = (bf16[256,512]{1,0:T(8,128)(2,1)S(1)}, bf16[256,512]{1,0:T(8,128)(2,1)S(1)}, u32[]{:S(2)}, u32[]{:S(2)}) collective-permute-start(bf16[256,512]{1,0:T(8,128)(2,1)S(1)} %get-tuple-element.45), channel_id=1, source_target_pairs={{0,1},{1,0},{2,3},{3,2},{4,5},{5,4},{6,7},{7,6},{8,9},{9,8},{10,11... | collective-permute-start | bytes 786440 | tf_op jit(solution)/shard_map/ppermute | solution.py:299

commit v7 on v6

--- a/solution.py
+++ b/solution.py
@@ -75,7 +75,7 @@
     inner_ref[at] = jnp.where(odd, top, bottom).astype(BF)
 
 
-def pack_kernel(x_ref, outer_ref, inner_ref, again_ref, x, sems):
+def pack_kernel(lons, x_ref, outer_ref, inner_ref, again_ref, x, sems):
     odd = odd_place()
     part = OWN // PACK_PARTS
     copies = []
@@ -88,7 +88,10 @@
         m, p = i // PACK_PARTS, i % PACK_PARTS
         at = (m, pl.ds(p * part // 2, part // 2))
         pack_into(odd, x[m, pl.ds(p * part, part)], outer_ref, inner_ref, at)
-        again_ref[at] = outer_ref[at]
+
+    @pl.when(waits(lons))
+    def _():
+        again_ref[...] = outer_ref[...]
 
 
 def half_like(members):
@@ -254,10 +257,17 @@
         from_inner = back(m, p_inner_ref, inner_ref)
         sides = jnp.concatenate([from_outer, from_inner], axis=0)
         mixed = jnp.dot(back_side_ref[...], sides, preferred_element_type=F32).astype(BF)
-        latback = lax.dot_general(mixed, lat_ref[...], LAST, preferred_element_type=F32)
-        out[m] = (base_ref[m] + latback).astype(BF)
-        copies.append(pltpu.make_async_copy(out.at[m], out_hbm.at[m], sems.at[m]))
-        copies[m].start()
+        pieces = 1 if m < MEMBERS - 1 else 2
+        width = LAT // pieces
+        for h in range(pieces):
+            columns = pl.ds(h * width, width)
+            latback = lax.dot_general(mixed, lat_ref[columns, :], LAST, preferred_element_type=F32)
+            out[m, :, columns] = (base_ref[m, :, columns] + latback).astype(BF)
+            copy = pltpu.make_async_copy(
+                out.at[m, :, columns], out_hbm.at[m, :, columns], sems.at[m + h]
+            )
+            copy.start()
+            copies.append(copy)
     for copy in copies:
         copy.wait()
 
@@ -307,7 +317,7 @@
 
     c_outer, c_inner, c_later = halo(
         *call(
-            pack_kernel, (half_like(MEMBERS),) * 3, (control,), [HBM], 0, 8 * square,
+            functools.partial(pack_kernel, lons), (half_like(MEMBERS),) * 3, (control,), [HBM], 0, 8 * square,
             (pltpu.VMEM((MEMBERS, OWN, LAT), BF), pltpu.SemaphoreType.DMA((MEMBERS * PACK_PARTS,))),
         )
     )
@@ -390,7 +400,7 @@
         out_specs=HBM,
         scratch_shapes=(
             pltpu.VMEM((MEMBERS, OWN, LAT), BF),
-            pltpu.SemaphoreType.DMA((MEMBERS,)),
+            pltpu.SemaphoreType.DMA((MEMBERS + 1,)),
         ),
         compiler_params=pltpu.CompilerParams(vmem_limit_bytes=VMEM_LIMIT),
         cost_estimate=pl.CostEstimate(

time: 73.9 us -> 73.7 us (level)
  no operation moved by 1% of the time
where the time goes in v7:
time: 73.7 us; the launch traced here: 73.3 us
  starting transfers between devices  33.2 us (45%)
  blocking collectives  23.6 us (32%)
  Pallas kernels  9.92 us (13%)
  waiting for transfers between devices  6.34 us (9%)
    ppermute x1, starting transfers between devices, halo(): return (lax.ppermute(outer, 'lon', sooner), from_inner, from_later)  13.4 us
    all_to_all x1, blocking collectives, shards(): lax.all_to_all(misfit, 'mem', 0, 0, axis_index_groups=along_x)  11.9 us
    all_to_all x1, blocking collectives, shards(): lax.all_to_all(partial.reshape(XS, quarter, LAT), 'mem', 0, 0, axis_index...  11.7 us
    pallas_call x7, Pallas kernels, call(): pl.pallas_call(kernel, out_shape=out, in_specs=specs, out_specs=jax.tree....  7.8 us
    ppermute x1, starting transfers between devices, shards(): other = lax.ppermute(some, 'mem', across_y)  5.03 us
    ppermute x1, starting transfers between devices, shards(): p_outer = lax.ppermute(p_outer, 'lon', beyond)  4.35 us
    ppermute x1, starting transfers between devices, misfit_halo(): return (lax.ppermute(outer, ('mem', 'lon'), across), from_inner)  3.97 us
    ppermute x1, waiting for transfers between devices, misfit_halo(): return (lax.ppermute(outer, ('mem', 'lon'), across), from_inner)  3.8 us
  transfers between devices with their start and end apart: 8, of which 3 were waited for; matrix products, arithmetic and copies ran while one was open for 0% of the time, Pallas kernels for 7%

profile of v7, /device:TPU:2, one launch (start us, length us, event | category | flops | bytes accessed | tf_op | source)
XLA Modules:
  0.0 73.3 jit_solution(4043651710696420134)
XLA Ops:
  0.0 1.3 %shard_map.92 = (bf16[2,256,512]{2,1,0:T(8,128)(2,1)S(1)}, bf16[2,256,512]{2,1,0:T(8,128)(2,1)S(1)}, bf16[2,256,512]{2,1,0:T(8,128)(2,1)S(1)}) custom-call(bf16[2,512,512]{2,1,0:T(8,128)(2,1)} %bitcast.11), custom_call_target="tpu_custom_call" | custom-call | bytes 2097152 | tf_op jit(solution)/shard_map/pallas_call | solution.py:42
  1.3 13.4 %collective-permute-start = (bf16[2,256,512]{2,1,0:T(8,128)(2,1)S(1)}, bf16[2,256,512]{2,1,0:T(8,128)(2,1)S(1)}, u32[]{:S(2)}, u32[]{:S(2)}) collective-permute-start(bf16[2,256,512]{2,1,0:T(8,128)(2,1)S(1)} %get-tuple-element.31), channel_id=1, source_target_pairs={{0,63},{1,2},{2,1},{3,4},{4,3},{5,6},{6,5},{7,8},{8,7},{9,10},{10,... | collective-permute-start | bytes 1572872 | tf_op jit(solution)/shard_map/ppermute | solution.py:306
  14.8 1.9 %collective-permute-start.1 = (bf16[2,256,512]{2,1,0:T(8,128)(2,1)S(1)}, bf16[2,256,512]{2,1,0:T(8,128)(2,1)S(1)}, u32[]{:S(2)}, u32[]{:S(2)}) collective-permute-start(bf16[2,256,512]{2,1,0:T(8,128)(2,1)S(1)} %get-tuple-element.32), channel_id=1, source_target_pairs={{0,1},{1,0},{2,3},{3,2},{4,5},{5,4},{6,7},{7,6},{8,9},{9,8},{10,11... | collective-permute-start | bytes 1572872 | tf_op jit(solution)/shard_map/ppermute | solution.py:304
  16.7 0.7 collective-permute-start.2
  17.4 3.6 %shard_map.91 = (bf16[512,512]{1,0:T(8,128)(2,1)S(1)}, bf16[512,512]{1,0:T(8,128)(2,1)S(1)}, bf16[512,512]{1,0:T(8,128)(2,1)S(1)}, f32[512,512]{1,0:T(8,128)S(1)...) custom-call(s32[2]{0:T(128)} %group_hbm.1, ...), custom_call_target="tpu_custom_call" | custom-call | flops 1073741824 | bytes 5242880 | tf_op jit(solution)/shard_map/pallas_call | solution.py:42
  21.0 1.6 %collective-permute-done.outer_ref = bf16[2,256,512]{2,1,0:T(8,128)(2,1)S(1)} collective-permute-done((bf16[2,256,512]{2,1,0:T(8,128)(2,1)S(1)}, bf16[2,256,512]{2,1,0:T(8,128)(2,1)S(1)}, u32[]{:S(2)}, u32[]{:S(2)}) %collective-permute-start) | collective-permute-done | bytes 524320 | tf_op jit(solution)/shard_map/ppermute | solution.py:306
  22.6 0.0 collective-permute-done.1.inner_ref
  22.6 1.3 %shard_map.93 = bf16[512,512]{1,0:T(8,128)(2,1)S(1)} custom-call(bf16[512,512]{1,0:T(8,128)(2,1)S(1)} %get-tuple-element.30.side_ref, bf16[512,512]{1,0:T(8,128)(2,1)S(1)} %get-tuple-element.29.lat_ref, bf16[2,256,512]{2,1,0:T(8,128)(2,1)S(1)} %collective-permute-done.outer_ref, bf16[2,256,512]{2,1,0:T(8,128)(2,1)S(1)} %collective-permute-done.1.inner_ref, ...), custom_call_target="tpu_custom_call" | custom-call | flops 1073741824 | bytes 4718592 | tf_op jit(solution)/shard_map/pallas_call | solution.py:42
  23.9 11.7 %all_to_all.10.parts_ref = bf16[4,128,512]{2,1,0:T(8,128)(2,1)S(1)} all-to-all(bf16[4,128,512]{2,1,0:T(8,128)(2,1)S(1)} %bitcast.10), channel_id=1, replica_groups={{0,64,128,192},{256,320,384,448},{1,65,129,193},{257,321,385,449},{2,66..., dimensions={0} | all-to-all | bytes 1048576 | tf_op jit(solution)/shard_map/all_to_all | solution.py:366
  35.6 0.1 shard_map.94.some_ref
  35.7 5.0 %collective-permute-start.3 = (bf16[128,512]{1,0:T(8,128)(2,1)S(1)}, bf16[128,512]{1,0:T(8,128)(2,1)S(1)}, u32[]{:S(2)}, u32[]{:S(2)}) collective-permute-start(bf16[128,512]{1,0:T(8,128)(2,1)S(1)} %shard_map.94.some_ref), channel_id=1, source_target_pairs={{0,256},{64,320},{128,384},{192,448},{256,0},{320,64},{384,128},{4... | collective-permute-start | bytes 393224 | tf_op jit(solution)/shard_map/ppermute | solution.py:373
  40.8 4.3 %collective-permute-start.5 = (bf16[2,256,512]{2,1,0:T(8,128)(2,1)S(1)}, bf16[2,256,512]{2,1,0:T(8,128)(2,1)S(1)}, u32[]{:S(2)}, u32[]{:S(2)}) collective-permute-start(bf16[2,256,512]{2,1,0:T(8,128)(2,1)S(1)} %get-tuple-element.43), channel_id=1, source_target_pairs={{0,63},{1,2},{2,1},{3,4},{4,3},{5,6},{6,5},{7,8},{8,7},{9,10},{10,... | collective-permute-start | bytes 1572872 | tf_op jit(solution)/shard_map/ppermute | solution.py:374
  45.1 1.9 %collective-permute-start.6 = (bf16[2,256,512]{2,1,0:T(8,128)(2,1)S(1)}, bf16[2,256,512]{2,1,0:T(8,128)(2,1)S(1)}, u32[]{:S(2)}, u32[]{:S(2)}) collective-permute-start(bf16[2,256,512]{2,1,0:T(8,128)(2,1)S(1)} %get-tuple-element.44), channel_id=1, source_target_pairs={{0,1},{1,0},{2,3},{3,2},{4,5},{5,4},{6,7},{7,6},{8,9},{9,8},{10,11... | collective-permute-start | bytes 1572872 | tf_op jit(solution)/shard_map/ppermute | solution.py:375
  47.0 0.9 %collective-permute-done.3.other_ref = bf16[128,512]{1,0:T(8,128)(2,1)S(1)} collective-permute-done((bf16[128,512]{1,0:T(8,128)(2,1)S(1)}, bf16[128,512]{1,0:T(8,128)(2,1)S(1)}, u32[]{:S(2)}, u32[]{:S(2)}) %collective-permute-start.3) | collective-permute-done | bytes 131104 | tf_op jit(solution)/shard_map/ppermute | solution.py:373
  48.0 0.1 shard_map.95
  48.0 11.9 %all_to_all.11 = bf16[4,128,512]{2,1,0:T(8,128)(2,1)S(1)} all-to-all(bf16[4,128,512]{2,1,0:T(8,128)(2,1)S(1)} %shard_map.95), channel_id=1, replica_groups={{0,64,128,192},{256,320,384,448},{1,65,129,193},{257,321,385,449},{2,66..., dimensions={0} | all-to-all | bytes 1048576 | tf_op jit(solution)/shard_map/all_to_all | solution.py:383
  59.9 0.2 shard_map.96
  60.1 4.0 %collective-permute-start.4 = (bf16[256,512]{1,0:T(8,128)(2,1)S(1)}, bf16[256,512]{1,0:T(8,128)(2,1)S(1)}, u32[]{:S(2)}, u32[]{:S(2)}) collective-permute-start(bf16[256,512]{1,0:T(8,128)(2,1)S(1)} %get-tuple-element.41), channel_id=1, source_target_pairs={{0,319},{1,2},{2,1},{3,4},{4,3},{5,6},{6,5},{7,264},{8,263},{9,10}... | collective-permute-start | bytes 786440 | tf_op jit(solution)/shard_map/ppermute | solution.py:310
  64.1 0.0 collective-permute-done.6.p_inner_ref
  64.1 1.9 %collective-permute-start.7 = (bf16[256,512]{1,0:T(8,128)(2,1)S(1)}, bf16[256,512]{1,0:T(8,128)(2,1)S(1)}, u32[]{:S(2)}, u32[]{:S(2)}) collective-permute-start(bf16[256,512]{1,0:T(8,128)(2,1)S(1)} %get-tuple-element.45), channel_id=1, source_target_pairs={{0,1},{1,0},{2,3},{3,2},{4,5},{5,4},{6,7},{7,6},{8,9},{9,8},{10,11... | collective-permute-start | bytes 786440 | tf_op jit(solution)/shard_map/ppermute | solution.py:309
  66.0 1.3 %shard_map.97.base_ref = f32[2,512,512]{2,1,0:T(8,128)S(1)} custom-call(bf16[512,512]{1,0:T(8,128)(2,1)S(1)} %get-tuple-element.49.back_own_ref, bf16[512,512]{1,0:T(8,128)(2,1)S(1)} %get-tuple-element.29.lat_ref, bf16[512,512]{1,0:T(8,128)(2,1)S(1)} %bitcast.9, f32[2,512,512]{2,1,0:T(8,128)S(1)} %get-tuple-element.34.weighted_ref, ...), custom_call_target="tpu_custom_call" | custom-call | flops 1073741824 | bytes 4718592 | tf_op jit(solution)/shard_map/pallas_call | solution.py:42
  67.3 3.8 %collective-permute-done.4.outer_ref = bf16[256,512]{1,0:T(8,128)(2,1)S(1)} collective-permute-done((bf16[256,512]{1,0:T(8,128)(2,1)S(1)}, bf16[256,512]{1,0:T(8,128)(2,1)S(1)}, u32[]{:S(2)}, u32[]{:S(2)}) %collective-permute-start.4) | collective-permute-done | bytes 262176 | tf_op jit(solution)/shard_map/ppermute | solution.py:310
  71.1 0.0 collective-permute-done.7.inner_ref
  71.1 2.1 %shard_map.98 = bf16[2,512,512]{2,1,0:T(8,128)(2,1)} custom-call(bf16[512,512]{1,0:T(8,128)(2,1)S(1)} %get-tuple-element.28.back_side_ref, bf16[512,512]{1,0:T(8,128)(2,1)S(1)} %get-tuple-element.29.lat_ref, bf16[256,512]{1,0:T(8,128)(2,1)S(1)} %collective-permute-done.4.outer_ref, bf16[256,512]{1,0:T(8,128)(2,1)S(1)} %collective-permute-done.7.inner_ref, ...), custom_call_target="tpu_custom_call" | custom-call | flops 1073741824 | bytes 5242880 | tf_op jit(solution)/shard_map/pallas_call | solution.py:396
  (2 shorter events, 0.0 us)
Async XLA Ops:
  1.3 21.3 %collective-permute-start = (bf16[2,256,512]{2,1,0:T(8,128)(2,1)S(1)}, bf16[2,256,512]{2,1,0:T(8,128)(2,1)S(1)}, u32[]{:S(2)}, u32[]{:S(2)}) collective-permute-start(bf16[2,256,512]{2,1,0:T(8,128)(2,1)S(1)} %get-tuple-element.31), channel_id=1, source_target_pairs={{0,63},{1,2},{2,1},{3,4},{4,3},{5,6},{6,5},{7,8},{8,7},{9,10},{10,... | collective-permute-start | bytes 1572872 | tf_op jit(solution)/shard_map/ppermute | solution.py:306
  14.8 7.9 %collective-permute-start.1 = (bf16[2,256,512]{2,1,0:T(8,128)(2,1)S(1)}, bf16[2,256,512]{2,1,0:T(8,128)(2,1)S(1)}, u32[]{:S(2)}, u32[]{:S(2)}) collective-permute-start(bf16[2,256,512]{2,1,0:T(8,128)(2,1)S(1)} %get-tuple-element.32), channel_id=1, source_target_pairs={{0,1},{1,0},{2,3},{3,2},{4,5},{5,4},{6,7},{7,6},{8,9},{9,8},{10,11... | collective-permute-start | bytes 1572872 | tf_op jit(solution)/shard_map/ppermute | solution.py:304
  16.7 6.0 %collective-permute-start.2 = (bf16[2,256,512]{2,1,0:T(8,128)(2,1)S(1)}, bf16[2,256,512]{2,1,0:T(8,128)(2,1)S(1)}, u32[]{:S(2)}, u32[]{:S(2)}) collective-permute-start(bf16[2,256,512]{2,1,0:T(8,128)(2,1)S(1)} %get-tuple-element.33), channel_id=1, source_target_pairs={{57,58},{58,57},{59,60},{60,59},{61,62},{62,61},{121,122},{122,121... | collective-permute-start | bytes 1572872 | tf_op jit(solution)/shard_map/ppermute | solution.py:305
  35.7 12.2 %collective-permute-start.3 = (bf16[128,512]{1,0:T(8,128)(2,1)S(1)}, bf16[128,512]{1,0:T(8,128)(2,1)S(1)}, u32[]{:S(2)}, u32[]{:S(2)}) collective-permute-start(bf16[128,512]{1,0:T(8,128)(2,1)S(1)} %shard_map.94.some_ref), channel_id=1, source_target_pairs={{0,256},{64,320},{128,384},{192,448},{256,0},{320,64},{384,128},{4... | collective-permute-start | bytes 393224 | tf_op jit(solution)/shard_map/ppermute | solution.py:373
  40.8 23.3 %collective-permute-start.5 = (bf16[2,256,512]{2,1,0:T(8,128)(2,1)S(1)}, bf16[2,256,512]{2,1,0:T(8,128)(2,1)S(1)}, u32[]{:S(2)}, u32[]{:S(2)}) collective-permute-start(bf16[2,256,512]{2,1,0:T(8,128)(2,1)S(1)} %get-tuple-element.43), channel_id=1, source_target_pairs={{0,63},{1,2},{2,1},{3,4},{4,3},{5,6},{6,5},{7,8},{8,7},{9,10},{10,... | collective-permute-start | bytes 1572872 | tf_op jit(solution)/shard_map/ppermute | solution.py:374
  45.1 19.0 %collective-permute-start.6 = (bf16[2,256,512]{2,1,0:T(8,128)(2,1)S(1)}, bf16[2,256,512]{2,1,0:T(8,128)(2,1)S(1)}, u32[]{:S(2)}, u32[]{:S(2)}) collective-permute-start(bf16[2,256,512]{2,1,0:T(8,128)(2,1)S(1)} %get-tuple-element.44), channel_id=1, source_target_pairs={{0,1},{1,0},{2,3},{3,2},{4,5},{5,4},{6,7},{7,6},{8,9},{9,8},{10,11... | collective-permute-start | bytes 1572872 | tf_op jit(solution)/shard_map/ppermute | solution.py:375
  60.1 11.0 %collective-permute-start.4 = (bf16[256,512]{1,0:T(8,128)(2,1)S(1)}, bf16[256,512]{1,0:T(8,128)(2,1)S(1)}, u32[]{:S(2)}, u32[]{:S(2)}) collective-permute-start(bf16[256,512]{1,0:T(8,128)(2,1)S(1)} %get-tuple-element.41), channel_id=1, source_target_pairs={{0,319},{1,2},{2,1},{3,4},{4,3},{5,6},{6,5},{7,264},{8,263},{9,10}... | collective-permute-start | bytes 786440 | tf_op jit(solution)/shard_map/ppermute | solution.py:310
  64.1 7.0 %collective-permute-start.7 = (bf16[256,512]{1,0:T(8,128)(2,1)S(1)}, bf16[256,512]{1,0:T(8,128)(2,1)S(1)}, u32[]{:S(2)}, u32[]{:S(2)}) collective-permute-start(bf16[256,512]{1,0:T(8,128)(2,1)S(1)} %get-tuple-element.45), channel_id=1, source_target_pairs={{0,1},{1,0},{2,3},{3,2},{4,5},{5,4},{6,7},{7,6},{8,9},{9,8},{10,11... | collective-permute-start | bytes 786440 | tf_op jit(solution)/shard_map/ppermute | solution.py:309
